TPU v7x, 128 devices: a whole 4x4x4 slice. The times are simulated.
128 devices in a mesh: ctx: 32 (over z, x, core), head: 4 (over y).
Axes of the slice: x: 4, y: 4, z: 4, core: 2. Of those that a mesh axis runs over, the one named last changes fastest.
Arguments:
- tokens: bfloat16 [8192, 3072], P('ctx', 'head'), may hold values from -6 to 6
- query_key_value_weight: bfloat16 [3, 3072, 4096], P(None, None, 'head'), may hold values from -0.109375 to 0.109375
- output_weight: bfloat16 [4096, 3072], P('head'), may hold values from -0.09375 to 0.09375
- input_down_weights: bfloat16 [3, 3072, 16], P(None, 'head'), may hold values from -0.109375 to 0.109375
- input_up_weights: bfloat16 [3, 16, 4096], P(None, None, 'head'), may hold values from -1.5 to 1.5
- output_down_weight: bfloat16 [4096, 16], P('head'), may hold values from -0.09375 to 0.09375
- output_up_weight: bfloat16 [16, 3072], P(None, 'head'), may hold values from -1.5 to 1.5
- cotangent: bfloat16 [8192, 3072], P('ctx', 'head'), may hold values from -6 to 6
Outputs:
- output: bfloat16 [8192, 3072], P('ctx', 'head')
- input_grad: bfloat16 [8192, 3072], P('ctx', 'head')
- grad_down_qkv: float32 [3, 3072, 16], P(None, 'head')
- grad_up_qkv: float32 [3, 16, 4096], P(None, None, 'head')
- grad_down_out: float32 [4096, 16], P('head')
- grad_up_out: float32 [16, 3072], P(None, 'head')
All inputs are finite; a program needn't handle non-finite values.
Results may differ from a plain program's by a relative error of at most 0.029.
Values may be sent and summed in bfloat16 or wider, within the bound.
No kernel may reach another device: no remote copies, remote signals or barrier semaphores. Data moves between devices by JAX's collectives and lax.ppermute only.
A program may use at most 128 MiB of HBM per device.

v0:
```python
import functools

import jax
import jax.numpy as jnp
from jax import lax
from jax.experimental import pallas as pl
from jax.experimental.pallas import tpu as pltpu
from jax.sharding import PartitionSpec as P

HEAD_DIM = 128
RANK = 16
TILE = 256
LANES = 128
adapter_scale = 0.5
epsilon = 1e-06
bf16 = jnp.bfloat16
f32 = jnp.float32
HINT = 2 * 10**10
VMEM_BYTES = 12 * 2**20

NN = (((1,), (0,)), ((), ()))
NT = (((1,), (1,)), ((), ()))
TN = (((0,), (0,)), ((), ()))

IN_HBM = pl.BlockSpec(memory_space=pltpu.HBM)
IN_VMEM = pl.BlockSpec(memory_space=pltpu.VMEM)
UNREAD = pl.BlockSpec(memory_space=pl.ANY)


def mm(a, b, dims=NN):
    return lax.dot_general(a, b, dims, preferred_element_type=f32)


def struct(shape, dtype):
    return jax.ShapeDtypeStruct(shape, dtype)


def call(kernel, specs, out_shape, flops, moved, scratch=(), aliases=None):
    many = isinstance(out_shape, (list, tuple))
    return pl.pallas_call(
        kernel,
        in_specs=specs,
        out_specs=[IN_VMEM] * len(out_shape) if many else IN_VMEM,
        out_shape=out_shape,
        scratch_shapes=list(scratch),
        input_output_aliases=aliases or {},
        compiler_params=pltpu.CompilerParams(vmem_limit_bytes=VMEM_BYTES),
        cost_estimate=pl.CostEstimate(flops=flops, bytes_accessed=moved, transcendentals=0),
    )


def member(shift):
    return lax.rem(lax.axis_index("head") + shift + 4, 4)


def first_core():
    return lax.rem(lax.axis_index("ctx"), 2) == 0


def chunk_rows(weight_ref, m, shift, width):
    return weight_ref[m, pl.ds(pl.multiple_of(member(shift) * width, width), width)]


def start_kernel(tok_ref, down_ref, top_ref, bottom_ref):
    half = top_ref.shape[0]
    width = tok_ref.shape[1]
    top_ref[:, :width] = tok_ref[:half]
    bottom_ref[:, :width] = tok_ref[half:]
    small = mm(tok_ref[...], down_ref[...], NT)
    value = small.astype(bf16)
    rest = (small - value.astype(f32)).astype(bf16)
    pad = jnp.zeros((half, LANES - 6 * RANK), bf16)
    small = jnp.concatenate(
        [value[:half], rest[:half], pad, value[half:], rest[half:], pad], axis=1
    )
    top_ref[:, width:] = small
    bottom_ref[:, width:] = small


def start(tok, down_t):
    rows, width = tok.shape
    return call(
        start_kernel,
        [IN_VMEM] * 2,
        [struct((rows // 2, width + 2 * LANES), bf16)] * 2,
        HINT,
        6 * rows * width,
    )(tok, down_t)


def project_first_kernel(tok_ref, weight_ref, total_ref):
    for m in range(3):
        total_ref[m] = mm(tok_ref[...], chunk_rows(weight_ref, m, 0, tok_ref.shape[1]))


def project_first(tok, weight):
    rows, width = tok.shape
    cols = weight.shape[2]
    return call(
        project_first_kernel,
        [IN_VMEM] * 2,
        struct((3, rows, cols), f32),
        6 * rows * width * cols,
        6 * width * cols,
    )(tok, weight)


def joined(buffer, top_ref, bottom_ref):
    half = top_ref.shape[0]
    buffer[:half] = top_ref[:, : buffer.shape[1]]
    buffer[half:] = bottom_ref[:, : buffer.shape[1]]
    return buffer[...]


def project_next_kernel(by, top_ref, bottom_ref, sum_ref, weight_ref, total_ref, buffer):
    tok = joined(buffer, top_ref, bottom_ref)
    for m in range(3):
        total_ref[m] = sum_ref[m] + mm(tok, chunk_rows(weight_ref, m, -by, tok.shape[1]))


def project_next(by, halves, total, weight, width):
    _, rows, cols = total.shape
    return call(
        functools.partial(project_next_kernel, by),
        [IN_VMEM] * 4,
        struct((3, rows, cols), f32),
        6 * rows * width * cols,
        6 * width * cols,
        [pltpu.VMEM((rows, width), bf16)],
        {2: 0},
    )(*halves, total, weight)


def cotangent_kernel(cot_ref, out_up_ref, unread, out_ref):
    rows, width = cot_ref.shape
    out_ref[:, :width] = cot_ref[...]
    back = mm(cot_ref[...], out_up_ref[...], NT).astype(bf16)
    out_ref[:, width:] = jnp.concatenate(
        [back, jnp.zeros((rows, LANES - RANK), bf16)], axis=1
    )


def cotangent_parts(cot, out_up, unread):
    rows, width = cot.shape
    return call(
        cotangent_kernel,
        [IN_VMEM] * 2 + [UNREAD],
        struct((rows, width + LANES), bf16),
        2 * rows * width * RANK,
        4 * rows * width,
    )(cot, out_up, unread)


def split_states(state, mine_ref, given_ref):
    half = mine_ref.shape[0]
    first = first_core()
    for h in range(half):
        low, high = state[h], state[half + h]
        mine_ref[h] = jnp.where(first, low, high)
        given_ref[h] = jnp.where(first, high, low).astype(bf16)


def project_last_kernel(
    top_ref, bottom_ref, sum_ref, own_ref, one_ref, three_ref, up_ref, weight_ref,
    qkv_ref, mine_ref, given_ref, low_ref, state, buffer,
):
    tok = joined(buffer, top_ref, bottom_ref)
    half = top_ref.shape[0]
    width = tok.shape[1]
    low = sum(
        ref[:, width:].astype(f32) for ref in (own_ref, one_ref, three_ref, top_ref)
    )
    for at, part in ((slice(0, half), low[:, :LANES]), (slice(half, 2 * half), low[:, LANES:])):
        low_ref[at] = (part[:, : 3 * RANK] + part[:, 3 * RANK : 6 * RANK]).astype(bf16)
    for m in (1, 2, 0):
        total = sum_ref[m] + mm(tok, chunk_rows(weight_ref, m, -2, width))
        total = total + adapter_scale * mm(low_ref[:, m * RANK : (m + 1) * RANK], up_ref[m])
        qkv_ref[m] = total.astype(bf16)
    for h in range(state.shape[0]):
        at = slice(h * HEAD_DIM, (h + 1) * HEAD_DIM)
        state[h] = mm(qkv_ref[1, :, at], qkv_ref[2, :, at], TN)
    split_states(state, mine_ref, given_ref)


def project_last(halves, total, smalls, up, weight, width):
    _, rows, cols = total.shape
    heads = cols // HEAD_DIM
    square = (HEAD_DIM, HEAD_DIM)
    return call(
        project_last_kernel,
        [IN_VMEM] * 8,
        [
            struct((3, rows, cols), bf16),
            struct((heads // 2,) + square, f32),
            struct((heads // 2,) + square, bf16),
            struct((rows, 3 * RANK), bf16),
        ],
        6 * rows * width * cols,
        6 * width * cols,
        [pltpu.VMEM((heads,) + square, f32), pltpu.VMEM((rows, width), bf16)],
    )(*halves, total, *smalls, up, weight)


def attended_gradient_kernel(
    cot0, cot1, cot3, top_ref, bottom_ref, down_ref, weight_ref, out_ref, back_ref, buffer
):
    width = cot0.shape[1] - LANES
    joined(buffer, top_ref, bottom_ref)
    refs = ((0, cot0), (1, cot1), (3, cot3), (2, buffer))
    back = sum(ref[:, width:].astype(f32) for _, ref in refs).astype(bf16)[:, :RANK]
    back_ref[...] = back
    total = adapter_scale * mm(back, down_ref[...])
    for by, ref in refs:
        chunk = pl.ds(pl.multiple_of(member(-by) * width, width), width)
        total = total + mm(ref[:, :width], weight_ref[:, chunk], NT)
    out_ref[...] = total


def attended_gradient(cots, down_out, weight):
    rows, wide = cots[0].shape
    cols, full = weight.shape
    return call(
        attended_gradient_kernel,
        [IN_VMEM] * 7,
        [struct((rows, cols), f32), struct((rows, RANK), bf16)],
        2 * rows * full * cols,
        2 * full * cols,
        [pltpu.VMEM((rows, wide), bf16)],
    )(*cots, down_out, weight)


def lower_mask(rows):
    s = lax.broadcasted_iota(jnp.int32, (rows, rows), 0)
    t = lax.broadcasted_iota(jnp.int32, (rows, rows), 1)
    return s >= t


def lanes_of(h):
    return slice(h * HEAD_DIM, (h + 1) * HEAD_DIM)


def held_of(own_ref, back_ref, h):
    half = own_ref.shape[0]
    i = h % half
    if h < half:
        return jnp.where(first_core(), own_ref[i], back_ref[i])
    return jnp.where(first_core(), back_ref[i], own_ref[i])


def inside_kernel(qkv_ref, unread, scores_ref, raw_ref):
    mask = lower_mask(raw_ref.shape[0])
    for h in range(scores_ref.shape[0]):
        q, k, v = (qkv_ref[m, :, lanes_of(h)] for m in range(3))
        scores = jnp.where(mask, mm(q, k, NT), 0.0).astype(bf16)
        scores_ref[h] = scores
        raw_ref[:, lanes_of(h)] = mm(scores, v)


def inside_forward(qkv, unread):
    _, rows, cols = qkv.shape
    heads = cols // HEAD_DIM
    return call(
        inside_kernel,
        [IN_VMEM, UNREAD],
        [struct((heads, rows, rows), bf16), struct((rows, cols), f32)],
        4 * rows * cols * rows,
        6 * rows * cols,
    )(qkv, unread)


def halves_kernel(one_ref, three_ref, unread, top_ref, bottom_ref):
    half = top_ref.shape[0]
    top_ref[...] = one_ref[:half]
    bottom_ref[...] = three_ref[half:]


def halves(one, three, unread):
    rows, width = one.shape
    return call(
        halves_kernel,
        [IN_VMEM] * 2 + [UNREAD],
        [struct((rows // 2, width), bf16)] * 2,
        rows * width,
        4 * rows * width,
    )(one, three, unread)


def forward_kernel(
    qkv_ref, raw_ref, own_ref, back_ref, grad_ref, att_ref, draw_ref, mine_ref, given_ref, state
):
    for h in range(state.shape[0]):
        at = lanes_of(h)
        q = qkv_ref[0, :, at]
        raw = raw_ref[:, at] + mm(q, held_of(own_ref, back_ref, h))
        inverse = lax.rsqrt(jnp.mean(raw * raw, axis=-1, keepdims=True) + epsilon)
        normed = raw * inverse
        att_ref[:, at] = normed.astype(bf16)
        grad = grad_ref[:, at]
        along = jnp.mean(grad * normed, axis=-1, keepdims=True)
        draw = ((grad - normed * along) * inverse).astype(bf16)
        draw_ref[:, at] = draw
        state[h] = mm(q, draw, TN)
    split_states(state, mine_ref, given_ref)


def forward_heads(qkv, raw, held, grad):
    _, rows, cols = qkv.shape
    heads = cols // HEAD_DIM
    square = (HEAD_DIM, HEAD_DIM)
    return call(
        forward_kernel,
        [IN_VMEM] * 5,
        [
            struct((rows, cols), bf16),
            struct((rows, cols), bf16),
            struct((heads // 2,) + square, f32),
            struct((heads // 2,) + square, bf16),
        ],
        8 * rows * cols * HEAD_DIM,
        14 * rows * cols,
        [pltpu.VMEM((heads,) + square, f32)],
    )(qkv, raw, *held, grad)


def to_blocks(out_ref, base, rows):
    for b in range(rows.shape[1] // LANES):
        out_ref[base + b] = rows[:, b * LANES : (b + 1) * LANES]


def within_kernel(
    qkv_ref, scores_ref, own_ref, back_ref, draw_ref, att_ref, back_mid_ref, low_ref, up_ref,
    down_ref, unread, dq_ref, dk_ref, dv_ref, back_q_ref, mid_ref, early_ref,
):
    rows = draw_ref.shape[0]
    heads = scores_ref.shape[0]
    mask = lower_mask(rows)
    for h in range(heads):
        at = lanes_of(h)
        q, k, v = (qkv_ref[m, :, at] for m in range(3))
        draw = draw_ref[:, at]
        dscores = jnp.where(mask, mm(draw, v, NT), 0.0).astype(bf16)
        dq = mm(dscores, k) + mm(draw, held_of(own_ref, back_ref, h), NT)
        dq_ref[:, at] = dq.astype(bf16)
        dk_ref[:, at] = mm(dscores, q, TN)
        dv_ref[:, at] = mm(scores_ref[h], draw, TN)
    back_q_ref[...] = mm(dq_ref[...], up_ref[0], NT)
    mid_ref[...] = mm(att_ref[...], down_ref[...], NT)
    to_blocks(early_ref, 0, mm(back_mid_ref[...], att_ref[...], TN))
    to_blocks(early_ref, heads, mm(low_ref[:, :RANK], dq_ref[...], TN))


def within_block(qkv, scores, held, draw, att, back_mid, low, up, down_out, unread):
    _, rows, cols = qkv.shape
    heads = cols // HEAD_DIM
    return call(
        within_kernel,
        [IN_VMEM] * 10 + [UNREAD],
        [
            struct((rows, cols), bf16),
            struct((rows, cols), f32),
            struct((rows, cols), f32),
            struct((rows, RANK), f32),
            struct((rows, RANK), f32),
            struct((2 * heads, RANK, LANES), f32),
        ],
        4 * rows * cols * (4 * rows),
        18 * rows * cols,
    )(qkv, scores, *held, draw, att, back_mid, low, up, down_out, unread)


def across_kernel(
    qkv_ref, own_ref, back_ref, dk_ref, dv_ref, back_q_ref, mid_ref, up_ref, out_ref, low_ref
):
    for h in range(out_ref.shape[2] // HEAD_DIM):
        at = lanes_of(h)
        held = held_of(own_ref, back_ref, h)
        out_ref[0, :, at] = (dk_ref[:, at] + mm(qkv_ref[2, :, at], held, NT)).astype(bf16)
        out_ref[1, :, at] = (dv_ref[:, at] + mm(qkv_ref[1, :, at], held)).astype(bf16)
    low_ref[:, :RANK] = back_q_ref[...].astype(bf16)
    low_ref[:, 3 * RANK :] = mid_ref[...].astype(bf16)
    for m in (1, 2):
        low_ref[:, m * RANK : (m + 1) * RANK] = mm(out_ref[m - 1], up_ref[m], NT).astype(bf16)


def across_blocks(qkv, held, dk, dv, back_q, mid, up):
    _, rows, cols = qkv.shape
    return call(
        across_kernel,
        [IN_VMEM] * 8,
        [struct((2, rows, cols), bf16), struct((rows, 4 * RANK), bf16)],
        8 * rows * cols * HEAD_DIM,
        18 * rows * cols,
    )(qkv, *held, dk, dv, back_q, mid, up)


def output_product(by, att_ref, weight_ref, width):
    chunk = pl.ds(pl.multiple_of(member(by) * width, width), width)
    return mm(att_ref[...], weight_ref[:, chunk])


def output_far_kernel(att_ref, weight_ref, unread0, unread1, top_ref, bottom_ref):
    half, width = top_ref.shape
    part = output_product(2, att_ref, weight_ref, width).astype(bf16)
    top_ref[...] = part[:half]
    bottom_ref[...] = part[half:]


def output_far(att, weight, width, unread):
    rows, cols = att.shape
    return call(
        output_far_kernel,
        [IN_VMEM] * 2 + [UNREAD] * 2,
        [struct((rows // 2, width), bf16)] * 2,
        2 * rows * cols * width,
        2 * cols * width,
    )(att, weight, *unread)


def output_near_kernel(
    att_ref, relay_top, relay_bottom, weight_ref, unread, own_ref, one_ref, three_ref
):
    half, width = relay_top.shape
    own_ref[...] = output_product(0, att_ref, weight_ref, width)
    one = output_product(1, att_ref, weight_ref, width)
    one_ref[:half] = (one[:half] + relay_top[...].astype(f32)).astype(bf16)
    one_ref[half:] = one[half:].astype(bf16)
    three = output_product(3, att_ref, weight_ref, width)
    three_ref[:half] = three[:half].astype(bf16)
    three_ref[half:] = (three[half:] + relay_bottom[...].astype(f32)).astype(bf16)


def output_near(att, relays, weight, unread):
    rows, cols = att.shape
    width = relays[0].shape[1]
    return call(
        output_near_kernel,
        [IN_VMEM] * 4 + [UNREAD],
        [struct((rows, width), f32)] + [struct((rows, width), bf16)] * 2,
        6 * rows * cols * width,
        6 * cols * width,
    )(att, *relays, weight, unread)


def output_sum_kernel(own_ref, one_ref, three_ref, low_ref, up_ref, unread, out_ref):
    total = own_ref[...] + one_ref[...].astype(f32) + three_ref[...].astype(f32)
    total = total + adapter_scale * mm(low_ref[:, 3 * RANK :], up_ref[...])
    out_ref[...] = total.astype(bf16)


def output_sum(own, parts, low, up, unread):
    rows, width = own.shape
    return call(
        output_sum_kernel,
        [IN_VMEM] * 5 + [UNREAD],
        struct((rows, width), bf16),
        2 * rows * width * RANK,
        10 * rows * width,
    )(own, *parts, low, up, unread)


def query_kernel(dq_ref, weight_ref, unread, out_ref):
    parts, _, width = out_ref.shape
    for p in range(parts):
        out_ref[p] = mm(dq_ref[...], weight_ref[0, p * width : (p + 1) * width], NT)


def query_part(dq, weight, width, unread):
    rows, cols = dq.shape
    parts = weight.shape[1] // width
    return call(
        query_kernel,
        [IN_VMEM] * 2 + [UNREAD],
        struct((parts, rows, width), f32),
        2 * rows * cols * width * parts,
        2 * cols * width * parts,
    )(dq, weight, unread)


def input_product(by, dkv_ref, dq_ref, weight_ref):
    total = dq_ref[member(by)]
    for m in range(2):
        total = total + mm(
            dkv_ref[m], chunk_rows(weight_ref, m + 1, by, total.shape[1]), NT
        )
    return total


def input_piece_kernel(by, dkv_ref, dq_ref, weight_ref, unread, out_ref):
    out_ref[...] = input_product(by, dkv_ref, dq_ref, weight_ref).astype(bf16)


def input_own_kernel(dkv_ref, dq_ref, weight_ref, unread, out_ref):
    out_ref[...] = input_product(0, dkv_ref, dq_ref, weight_ref)


def input_call(kernel, dkv, dq_parts, weight, out, *more):
    _, rows, cols = dkv.shape
    width = dq_parts.shape[2]
    return call(
        kernel,
        [IN_VMEM] * 3 + [UNREAD] * len(more),
        out,
        4 * rows * cols * width,
        4 * cols * width,
    )(dkv, dq_parts, weight, *more)


def input_sum_kernel(own_ref, two_ref, one_ref, three_ref, low_ref, down_ref, out_ref):
    total = own_ref[...] + adapter_scale * mm(low_ref[:, : 3 * RANK], down_ref[...])
    for ref in (two_ref, one_ref, three_ref):
        total = total + ref[...].astype(f32)
    out_ref[...] = total.astype(bf16)


def input_sum(own, parts, low, down_t):
    rows, width = own.shape
    return call(
        input_sum_kernel,
        [IN_VMEM] * 6,
        struct((rows, width), bf16),
        6 * rows * width * RANK,
        12 * rows * width,
    )(own, *parts, low, down_t)


def grads_kernel(
    back0, back2, back1, back3, tok_ref, cot_ref, low_ref, dkv_ref, early_ref,
    *refs,
):
    back_ref, mine_ref, given_ref, packed = refs[-4:]
    back = back0[...].astype(f32) + back2[...].astype(f32)
    back = (back + back1[...].astype(f32) + back3[...].astype(f32)).astype(bf16)
    back_ref[...] = back
    down = mm(back[:, : 3 * RANK], tok_ref[...], TN)
    up_out = mm(back[:, 3 * RANK :], cot_ref[...], TN)
    at = 0
    for m in range(3):
        to_blocks(packed, at, down[m * RANK : (m + 1) * RANK])
        at += tok_ref.shape[1] // LANES
    to_blocks(packed, at, up_out)
    at += cot_ref.shape[1] // LANES
    packed[at : at + early_ref.shape[0]] = early_ref[...]
    at += early_ref.shape[0]
    for m in (1, 2):
        to_blocks(packed, at, mm(low_ref[:, m * RANK : (m + 1) * RANK], dkv_ref[m - 1], TN))
        at += dkv_ref.shape[2] // LANES
    half = mine_ref.shape[0]
    first = first_core()
    mine_ref[...] = jnp.where(first, packed[:half], packed[half:])
    given_ref[...] = jnp.where(first, packed[half:], packed[:half]).astype(bf16)


def grads(backs, tokens, cot, low, dkv, early, unread):
    rows, width = tokens.shape
    cols = dkv.shape[2]
    half = 2 * (width + cols) // LANES
    return call(
        grads_kernel,
        [IN_VMEM] * 9 + [UNREAD] * len(unread),
        [
            struct(backs[0].shape, bf16),
            struct((half, RANK, LANES), f32),
            struct((half, RANK, LANES), bf16),
        ],
        2 * rows * RANK * (3 * width + 2 * cols),
        2 * dkv.size + 2 * tokens.size,
        [pltpu.VMEM((2 * half, RANK, LANES), f32)],
    )(*backs, tokens, cot, low, dkv, early, *unread)


def unpack_kernel(scale, own_ref, back_ref, down_ref, up_ref, down_out_ref, up_out_ref):
    half = own_ref.shape[0]
    at = 0

    def take(count):
        nonlocal at
        at += count
        first = first_core()
        blocks = []
        for b in range(at - count, at):
            own, back = own_ref[b % half], back_ref[b % half]
            block = jnp.where(first, own, back) if b < half else jnp.where(first, back, own)
            blocks.append(block.astype(f32))
        return scale * jnp.concatenate(blocks, axis=1)

    wide, heads = up_out_ref.shape[1] // LANES, down_out_ref.shape[1] // LANES
    for m in range(3):
        down_ref[m] = take(wide)
    up_out_ref[...] = take(wide)
    down_out_ref[...] = take(heads)
    for m in range(3):
        up_ref[m] = take(heads)


def unpack(own, back, scale, width, cols):
    return call(
        functools.partial(unpack_kernel, scale),
        [IN_VMEM] * 2,
        [
            struct((3, RANK, width), f32),
            struct((3, RANK, cols), f32),
            struct((RANK, cols), f32),
            struct((RANK, width), f32),
        ],
        own.size,
        12 * own.size,
    )(own, back)


def shift(array, by):
    n = lax.axis_size("head")
    return lax.ppermute(array, "head", [(i, (i + by) % n) for i in range(n)])


def from_head(array):
    return [shift(array, by) for by in (2, 1, 3)]


def swap_cores(array):
    n = lax.axis_size("ctx")
    return lax.ppermute(array, "ctx", [(i, i ^ 1) for i in range(n)])


def chip_place():
    n = lax.axis_size("ctx")
    chip = lax.axis_index("ctx") // 2
    side = {32: 4}[n]
    return lax.rem(chip, side), chip // side


def along(array, axis, by):
    n = lax.axis_size("ctx")
    side = {32: 4}[n]
    pairs = []
    for i in range(n):
        core, x, z = i % 2, (i // 2) % side, i // (2 * side)
        if axis == "x":
            x = (x + by) % side
        else:
            z = (z + by) % side
        pairs.append((i, (z * side + x) * 2 + core))
    return lax.ppermute(array, "ctx", pairs)


def from_axis(array, axis):
    return [along(array, axis, by) for by in (1, 3, 2)]


def pair_kernel(mine_ref, got_ref, out_ref):
    out_ref[...] = (mine_ref[...] + got_ref[...].astype(f32)).astype(bf16)


def before_sum(reverse, place, refs):
    total = jnp.zeros(refs[0].shape, f32)
    for by, ref in zip((1, 3, 2), refs):
        wanted = (place < by) if reverse else (place >= by)
        total = total + jnp.where(wanted, ref[...].astype(f32), 0.0)
    return total


def row_kernel(reverse, mine_ref, got_ref, one_ref, three_ref, two_ref, *refs):
    row_ref, before_ref = refs[-2:]
    others = (one_ref, three_ref, two_ref)
    total = mine_ref[...] + got_ref[...].astype(f32)
    for ref in others:
        total = total + ref[...].astype(f32)
    row_ref[...] = total.astype(bf16)
    before_ref[...] = before_sum(reverse, chip_place()[0], others)


def combine_kernel(
    reverse, mine_ref, got_ref, before_ref, one_ref, three_ref, two_ref, *refs
):
    own_ref, other_ref = refs[-2:]
    chip = before_ref[...] + before_sum(reverse, chip_place()[1], (one_ref, three_ref, two_ref))
    first = first_core() != reverse
    own_ref[...] = jnp.where(first, chip, chip + got_ref[...].astype(f32)).astype(bf16)
    other_ref[...] = jnp.where(first, chip + mine_ref[...], chip).astype(bf16)


def glue(kernel, operands, out_dtypes, unread=()):
    shape = operands[0].shape
    return call(
        kernel,
        [IN_VMEM] * len(operands) + [UNREAD] * len(unread),
        [struct(shape, dtype) for dtype in out_dtypes],
        operands[0].size,
        8 * operands[0].size,
    )(*operands, *unread)


def scan_pair(mine, given):
    got = swap_cores(given)
    return glue(pair_kernel, [mine, got], [bf16])[0], got


def scan_row(mine, got, arrived, reverse, during):
    row, before = glue(
        functools.partial(row_kernel, reverse), [mine, got] + arrived, [bf16, f32], during
    )
    return mine, got, row, before


def scan_rest(middle, arrived, reverse, during):
    mine, got, _, before = middle
    own, other = glue(
        functools.partial(combine_kernel, reverse),
        [mine, got, before] + arrived,
        [bf16, bf16],
        during,
    )
    return own, swap_cores(other)


def row_sum_kernel(count, mine_ref, *refs):
    total = mine_ref[...].astype(f32)
    for ref in refs[:count]:
        total = total + ref[...].astype(f32)
    refs[-1][...] = total.astype(bf16)


def sum_pair(mine, given):
    got = swap_cores(given)
    return glue(functools.partial(row_sum_kernel, 1), [mine, got], [bf16])[0], got


def sum_row(mine, got, arrived, during):
    return glue(
        functools.partial(row_sum_kernel, 4), [mine, got] + arrived, [bf16], during
    )[0]


def sum_rest(row):
    (total,) = glue(functools.partial(row_sum_kernel, 3), [row] + from_axis(row, "z"), [bf16])
    return total, swap_cores(total)


def on_device(
    tokens,
    query_key_value_weight,
    output_weight,
    input_down_weights,
    input_up_weights,
    output_down_weight,
    output_up_weight,
    cotangent,
):
    rows, width = tokens.shape
    cols = query_key_value_weight.shape[2]
    n = lax.axis_size("ctx")
    scale_factor = adapter_scale * (rows * n) ** (-0.5)
    down_t = input_down_weights.transpose(0, 2, 1).reshape(3 * RANK, width)
    down_out_t = output_down_weight.T

    weight = query_key_value_weight

    top, bottom = start(tokens, down_t)
    one_top, three_bottom = shift(top, 1), shift(bottom, 3)
    one_bottom, three_top = shift(bottom, 1), shift(top, 3)
    two = shift(one_top, 1), shift(three_bottom, 3)
    total = project_first(tokens, weight)
    total = project_next(1, (one_top, one_bottom), total, weight, width)
    total = project_next(3, (three_top, three_bottom), total, weight, width)
    cot_own = cotangent_parts(cotangent, output_up_weight, total)
    cot_one, cot_three = shift(cot_own, 1), shift(cot_own, 3)
    qkv, mine, given, low = project_last(
        two, total, (top, one_top, three_top), input_up_weights, weight, width
    )

    pair, got = scan_pair(mine, given)
    scores, raw = inside_forward(qkv, pair)
    arrived = from_axis(pair, "x")
    cot_top, cot_bottom = halves(cot_one, cot_three, arrived[0])
    cot_two = shift(cot_top, 1), shift(cot_bottom, 3)
    middle = scan_row(mine, got, arrived, False, [raw, cot_top])
    grad, back_mid = attended_gradient(
        [cot_own, cot_one, cot_three, *cot_two], down_out_t, output_weight
    )
    held = scan_rest(middle, from_axis(middle[2], "z"), False, [])

    attended, d_raw, mine, given = forward_heads(qkv, raw, held, grad)
    pair, got = scan_pair(mine, given)
    dq, dk_within, dv_within, back_q, mid, early = within_block(
        qkv, scores, held, d_raw, attended, back_mid, low, input_up_weights, down_out_t, pair
    )
    arrived = from_axis(pair, "x")
    far_top, far_bottom = output_far(attended, output_weight, width, [arrived[0], early])
    relays = shift(far_top, 1), shift(far_bottom, 3)
    middle = scan_row(mine, got, arrived, True, [early, far_top])
    dq_parts = query_part(dq, weight, width, middle[2])
    out_own, out_one, out_three = output_near(attended, relays, output_weight, middle[2])
    out_got = shift(out_one, 1), shift(out_three, 3)
    suffix = scan_rest(middle, from_axis(middle[2], "z"), True, [dq_parts, out_own])

    dkv, back_part = across_blocks(
        qkv, suffix, dk_within, dv_within, back_q, mid, input_up_weights
    )
    back_got = from_head(back_part)
    piece, near = struct((rows, width), bf16), struct((rows, width), f32)

    def sent(by, unread):
        kernel = functools.partial(input_piece_kernel, by)
        part = input_call(kernel, dkv, dq_parts, weight, piece, unread)
        return part, shift(part, by)

    part_two, got_two = sent(2, back_got[0])
    part_one, got_one = sent(1, part_two)
    part_three, got_three = sent(3, part_one)
    back_low, mine, given = grads(
        [back_part] + back_got, tokens, cotangent, low, dkv, early, [part_three]
    )
    pair, got = sum_pair(mine, given)
    row = sum_row(mine, got, from_axis(pair, "x"), [got_two])
    grad_own = input_call(input_own_kernel, dkv, dq_parts, weight, near, row)
    output = output_sum(out_own, out_got, back_low, output_up_weight, row)
    grad_got = [got_two, got_one, got_three]
    sums = sum_rest(row)
    input_grad = input_sum(grad_own, grad_got, back_low, down_t)
    grad_down_qkv, grad_up_qkv, grad_down_out, grad_up_out = unpack(
        *sums, scale_factor, width, cols
    )
    return (
        output,
        input_grad,
        grad_down_qkv.transpose(0, 2, 1),
        grad_up_qkv,
        grad_down_out.T,
        grad_up_out,
    )


def solution(mesh):
    return jax.shard_map(
        on_device,
        mesh=mesh,
        in_specs=(
            P("ctx", "head"),
            P(None, None, "head"),
            P("head", None),
            P(None, "head", None),
            P(None, None, "head"),
            P("head", None),
            P(None, "head"),
            P("ctx", "head"),
        ),
        out_specs=(
            P("ctx", "head"),
            P("ctx", "head"),
            P(None, "head", None),
            P(None, None, "head"),
            P("head", None),
            P(None, "head"),
        ),
        check_vma=False,
    )
```

profile of v0, /device:TPU:1, one launch (start us, length us, event | category | flops | bytes accessed | tf_op | source)
XLA Modules:
  0.0 126.6 jit_solution(5686040174323719044)
XLA Ops:
  0.7 1.1 copy-done
  1.8 1.1 copy-done.6
  3.2 3.6 %collective-permute-start.2 = (bf16[128,1024]{1,0:T(8,128)(2,1)S(1)}, bf16[128,1024]{1,0:T(8,128)(2,1)S(1)}, u32[]{:S(2)}, u32[]{:S(2)}) collective-permute-start(bf16[128,1024]{1,0:T(8,128)(2,1)S(1)} %get-tuple-element.51), channel_id=1, source_target_pairs={{0,3},{1,0},{2,1},{3,2},{4,7},{5,4},{6,5},{7,6},{8,11},{9,8},{10,9... | collective-permute-start | bytes 786440 | tf_op jit(solution)/shard_map/ppermute | solution.py:612
  6.9 2.7 %collective-permute-start.4 = (bf16[128,1024]{1,0:T(8,128)(2,1)S(1)}, bf16[128,1024]{1,0:T(8,128)(2,1)S(1)}, u32[]{:S(2)}, u32[]{:S(2)}) collective-permute-start(bf16[128,1024]{1,0:T(8,128)(2,1)S(1)} %get-tuple-element.50.own_ref), channel_id=1, source_target_pairs={{0,3},{1,0},{2,1},{3,2},{4,7},{5,4},{6,5},{7,6},{8,11},{9,8},{10,9... | collective-permute-start | bytes 786440 | tf_op jit(solution)/shard_map/ppermute | solution.py:612
  9.6 1.4 %shard_map.128.sum_ref = f32[3,256,1024]{2,1,0:T(8,128)S(1)} custom-call(bf16[256,768]{1,0:T(8,128)(2,1)S(1)} %copy-done, bf16[3,3072,1024]{2,1,0:T(8,128)(2,1)S(1)} %bitcast.7), custom_call_target="tpu_custom_call" | custom-call | flops 1207959552 | bytes 4718592 | tf_op jit(solution)/shard_map/pallas_call | solution.py:99
  11.8 3.4 %collective-permute-start.3 = (bf16[128,1024]{1,0:T(8,128)(2,1)S(1)}, bf16[128,1024]{1,0:T(8,128)(2,1)S(1)}, u32[]{:S(2)}, u32[]{:S(2)}) collective-permute-start(bf16[128,1024]{1,0:T(8,128)(2,1)S(1)} %collective-permute-done.2.bottom_ref), channel_id=1, source_target_pairs={{0,3},{1,0},{2,1},{3,2},{4,7},{5,4},{6,5},{7,6},{8,11},{9,8},{10,9... | collective-permute-start | bytes 786440 | tf_op jit(solution)/shard_map/ppermute | solution.py:612
  15.3 5.3 %collective-permute-done.5.bottom_ref = bf16[128,1024]{1,0:T(8,128)(2,1)S(1)} collective-permute-done((bf16[128,1024]{1,0:T(8,128)(2,1)S(1)}, bf16[128,1024]{1,0:T(8,128)(2,1)S(1)}, u32[]{:S(2)}, u32[]{:S(2)}) %collective-permute-start.5) | collective-permute-done | bytes 262176 | tf_op jit(solution)/shard_map/ppermute | solution.py:612
  20.5 1.6 %shard_map.129.sum_ref = f32[3,256,1024]{2,1,0:T(8,128)S(1)} custom-call(bf16[128,1024]{1,0:T(8,128)(2,1)S(1)} %collective-permute-done.top_ref.one_ref, bf16[128,1024]{1,0:T(8,128)(2,1)S(1)} %collective-permute-done.5.bottom_ref, f32[3,256,1024]{2,1,0:T(8,128)S(1)} %shard_map.128.sum_ref, ...), custom_call_target="tpu_custom_call", output_to_operand_aliasing={{}: (2, {})} | custom-call | flops 1207959552 | bytes 4718592 | tf_op jit(solution)/shard_map/pallas_call | solution.py:123
  22.2 1.6 %shard_map.130.sum_ref.unread = f32[3,256,1024]{2,1,0:T(8,128)S(1)} custom-call(bf16[128,1024]{1,0:T(8,128)(2,1)S(1)} %collective-permute-done.4.top_ref.three_ref, bf16[128,1024]{1,0:T(8,128)(2,1)S(1)} %collective-permute-done.2.bottom_ref, f32[3,256,1024]{2,1,0:T(8,128)S(1)} %shard_map.129.sum_ref, ...), custom_call_target="tpu_custom_call", output_to_operand_aliasing={{}: (2, {})} | custom-call | flops 1207959552 | bytes 4718592 | tf_op jit(solution)/shard_map/pallas_call | solution.py:123
  24.2 1.5 %collective-permute-start.10 = (bf16[256,896]{1,0:T(8,128)(2,1)S(1)}, bf16[256,896]{1,0:T(8,128)(2,1)S(1)}, u32[]{:S(2)}, u32[]{:S(2)}) collective-permute-start(bf16[256,896]{1,0:T(8,128)(2,1)S(1)} %shard_map.134.cot0), channel_id=1, source_target_pairs={{0,1},{1,2},{2,3},{3,0},{4,5},{5,6},{6,7},{7,4},{8,9},{9,10},{10,1... | collective-permute-start | bytes 1376264 | tf_op jit(solution)/shard_map/ppermute | solution.py:612
  26.2 2.2 %shard_map.131 = (bf16[3,256,1024]{2,1,0:T(8,128)(2,1)S(1)}, f32[4,128,128]{2,1,0:T(8,128)S(1)}, bf16[4,128,128]{2,1,0:T(8,128)(2,1)S(1)}, bf16[256,48]{1,0:T(8,128)(2,1)S(1)}) custom-call(bf16[128,1024]{1,0:T(8,128)(2,1)S(1)} %collective-permute-done.1.top_ref, bf16[128,1024]{1,0:T(8,128)(2,1)S(1)} %collective-permute-done.3.bottom_ref, ...), custom_call_target="tpu_custom_call" | custom-call | flops 1207959552 | bytes 4718592 | tf_op jit(solution)/shard_map/pallas_call | solution.py:189
  28.4 3.5 %collective-permute-start.6 = (bf16[4,128,128]{2,1,0:T(8,128)(2,1)S(1)}, bf16[4,128,128]{2,1,0:T(8,128)(2,1)S(1)}, u32[]{:S(2)}, u32[]{:S(2)}) collective-permute-start(bf16[4,128,128]{2,1,0:T(8,128)(2,1)S(1)} %get-tuple-element.54), channel_id=1, source_target_pairs={{0,4},{4,0},{8,12},{12,8},{16,20},{20,16},{24,28},{28,24},{32,36},... | collective-permute-start | bytes 393224 | tf_op jit(solution)/shard_map/ppermute | solution.py:621
  32.9 1.3 %collective-permute-start.7 = (bf16[4,128,128]{2,1,0:T(8,128)(2,1)S(1)}, bf16[4,128,128]{2,1,0:T(8,128)(2,1)S(1)}, u32[]{:S(2)}, u32[]{:S(2)}) collective-permute-start(bf16[4,128,128]{2,1,0:T(8,128)(2,1)S(1)} %shard_map.132.unread), channel_id=1, source_target_pairs={{0,8},{4,12},{8,16},{12,20},{16,24},{20,28},{24,0},{28,4},{32,40},... | collective-permute-start | bytes 393224 | tf_op jit(solution)/shard_map/ppermute | solution.py:642
  34.2 2.5 %collective-permute-start.9 = (bf16[4,128,128]{2,1,0:T(8,128)(2,1)S(1)}, bf16[4,128,128]{2,1,0:T(8,128)(2,1)S(1)}, u32[]{:S(2)}, u32[]{:S(2)}) collective-permute-start(bf16[4,128,128]{2,1,0:T(8,128)(2,1)S(1)} %shard_map.132.unread), channel_id=1, source_target_pairs={{0,16},{4,20},{8,24},{12,28},{16,0},{20,4},{24,8},{28,12},{32,48},... | collective-permute-start | bytes 393224 | tf_op jit(solution)/shard_map/ppermute | solution.py:642
  36.6 1.1 collective-permute-start.8
  37.8 1.1 collective-permute-done.7.unread.one_ref
  38.9 1.1 collective-permute-start.17
  41.4 1.3 %collective-permute-done.9.two_ref = bf16[4,128,128]{2,1,0:T(8,128)(2,1)S(1)} collective-permute-done((bf16[4,128,128]{2,1,0:T(8,128)(2,1)S(1)}, bf16[4,128,128]{2,1,0:T(8,128)(2,1)S(1)}, u32[]{:S(2)}, u32[]{:S(2)}) %collective-permute-start.9) | collective-permute-done | bytes 131104 | tf_op jit(solution)/shard_map/ppermute | solution.py:642
  42.9 3.9 %collective-permute-start.14 = (bf16[4,128,128]{2,1,0:T(8,128)(2,1)S(1)}, bf16[4,128,128]{2,1,0:T(8,128)(2,1)S(1)}, u32[]{:S(2)}, u32[]{:S(2)}) collective-permute-start(bf16[4,128,128]{2,1,0:T(8,128)(2,1)S(1)} %get-tuple-element.58), channel_id=1, source_target_pairs={{0,64},{4,68},{8,72},{12,76},{16,80},{20,84},{24,88},{28,92},{32,9... | collective-permute-start | bytes 393224 | tf_op jit(solution)/shard_map/ppermute | solution.py:642
  49.1 3.6 %collective-permute-done.13.three_ref = bf16[4,128,128]{2,1,0:T(8,128)(2,1)S(1)} collective-permute-done((bf16[4,128,128]{2,1,0:T(8,128)(2,1)S(1)}, bf16[4,128,128]{2,1,0:T(8,128)(2,1)S(1)}, u32[]{:S(2)}, u32[]{:S(2)}) %collective-permute-start.13) | collective-permute-done | bytes 131104 | tf_op jit(solution)/shard_map/ppermute | solution.py:642
  52.8 2.5 %collective-permute-start.15 = (bf16[4,128,128]{2,1,0:T(8,128)(2,1)S(1)}, bf16[4,128,128]{2,1,0:T(8,128)(2,1)S(1)}, u32[]{:S(2)}, u32[]{:S(2)}) collective-permute-start(bf16[4,128,128]{2,1,0:T(8,128)(2,1)S(1)} %get-tuple-element.60), channel_id=1, source_target_pairs={{0,4},{4,0},{8,12},{12,8},{16,20},{20,16},{24,28},{28,24},{32,36},... | collective-permute-start | bytes 393224 | tf_op jit(solution)/shard_map/ppermute | solution.py:621
  55.4 1.9 %shard_map.138 = (f32[256,1024]{1,0:T(8,128)S(1)}, bf16[256,16]{1,0:T(8,128)(2,1)S(1)}) custom-call(bf16[256,896]{1,0:T(8,128)(2,1)S(1)} %shard_map.134.cot0, bf16[256,896]{1,0:T(8,128)(2,1)S(1)} %collective-permute-done.10.one_ref.cot1, bf16[256,896]{1,0:T(8,128)(2,1)S(1)} %collective-permute-done.11.three_ref.cot3, ...), custom_call_target="tpu_custom_call" | custom-call | flops 1610612736 | bytes 6291456 | tf_op jit(solution)/shard_map/pallas_call | solution.py:222
  57.3 1.4 %shard_map.139 = (bf16[256,1024]{1,0:T(8,128)(2,1)S(1)}, bf16[256,1024]{1,0:T(8,128)(2,1)S(1)}, f32[4,128,128]{2,1,0:T(8,128)S(1)}, bf16[4,128,128]{2,1,0:T(8,128)(2,1)S(1)}) custom-call(bf16[3,256,1024]{2,1,0:T(8,128)(2,1)S(1)} %get-tuple-element.52.qkv_ref, f32[256,1024]{1,0:T(8,128)S(1)} %get-tuple-element.55.refs_0_.raw_ref, ...), custom_call_target="tpu_custom_call" | custom-call | flops 268435456 | bytes 3670016 | tf_op jit(solution)/shard_map/pallas_call | solution.py:310
  58.8 1.3 %collective-permute-done.18.got_ref = bf16[4,128,128]{2,1,0:T(8,128)(2,1)S(1)} collective-permute-done((bf16[4,128,128]{2,1,0:T(8,128)(2,1)S(1)}, bf16[4,128,128]{2,1,0:T(8,128)(2,1)S(1)}, u32[]{:S(2)}, u32[]{:S(2)}) %collective-permute-start.18) | collective-permute-done | bytes 131104 | tf_op jit(solution)/shard_map/ppermute | solution.py:621
  60.1 1.1 collective-permute-start.19
  61.2 2.1 %collective-permute-start.23 = (bf16[4,128,128]{2,1,0:T(8,128)(2,1)S(1)}, bf16[4,128,128]{2,1,0:T(8,128)(2,1)S(1)}, u32[]{:S(2)}, u32[]{:S(2)}) collective-permute-start(bf16[4,128,128]{2,1,0:T(8,128)(2,1)S(1)} %shard_map.140.unread), channel_id=1, source_target_pairs={{0,16},{4,20},{8,24},{12,28},{16,0},{20,4},{24,8},{28,12},{32,48},... | collective-permute-start | bytes 393224 | tf_op jit(solution)/shard_map/ppermute | solution.py:642
  63.4 1.3 %collective-permute-start.22 = (bf16[4,128,128]{2,1,0:T(8,128)(2,1)S(1)}, bf16[4,128,128]{2,1,0:T(8,128)(2,1)S(1)}, u32[]{:S(2)}, u32[]{:S(2)}) collective-permute-start(bf16[4,128,128]{2,1,0:T(8,128)(2,1)S(1)} %shard_map.140.unread), channel_id=1, source_target_pairs={{0,24},{4,28},{8,0},{12,4},{16,8},{20,12},{24,16},{28,20},{32,56},... | collective-permute-start | bytes 393224 | tf_op jit(solution)/shard_map/ppermute | solution.py:642
  64.7 3.0 %shard_map.141 = (bf16[256,1024]{1,0:T(8,128)(2,1)S(1)}, f32[256,1024]{1,0:T(8,128)S(1)}, f32[256,1024]{1,0:T(8,128)S(1)}, f32[256,16]{1,0:T(8,128)S(1)}, f32[25...) custom-call(bf16[3,256,1024]{2,1,0:T(8,128)(2,1)S(1)} %get-tuple-element.52.qkv_ref, ...), custom_call_target="tpu_custom_call" | custom-call | flops 1073741824 | bytes 4718592 | tf_op jit(solution)/shard_map/pallas_call | solution.py:355
  68.2 1.1 collective-permute-start.21
  69.9 1.9 %collective-permute-start.28 = (bf16[4,128,128]{2,1,0:T(8,128)(2,1)S(1)}, bf16[4,128,128]{2,1,0:T(8,128)(2,1)S(1)}, u32[]{:S(2)}, u32[]{:S(2)}) collective-permute-start(bf16[4,128,128]{2,1,0:T(8,128)(2,1)S(1)} %get-tuple-element.73.unread), channel_id=1, source_target_pairs={{0,64},{4,68},{8,72},{12,76},{16,80},{20,84},{24,88},{28,92},{32,9... | collective-permute-start | bytes 393224 | tf_op jit(solution)/shard_map/ppermute | solution.py:642
  73.3 1.8 %shard_map.145.refs_0_.dq_ref = f32[4,256,768]{2,1,0:T(8,128)S(1)} custom-call(bf16[256,1024]{1,0:T(8,128)(2,1)S(1)} %get-tuple-element.78.dq_ref, bf16[3,3072,1024]{2,1,0:T(8,128)(2,1)S(1)} %bitcast.7, bf16[4,128,128]{2,1,0:T(8,128)(2,1)S(1)} %get-tuple-element.73.unread), custom_call_target="tpu_custom_call" | custom-call | flops 1610612736 | bytes 6291456 | tf_op jit(solution)/shard_map/pallas_call | solution.py:470
  75.6 1.4 %shard_map.144 = (f32[256,768]{1,0:T(8,128)S(1)}, bf16[256,768]{1,0:T(8,128)(2,1)S(1)}, bf16[256,768]{1,0:T(8,128)(2,1)S(1)}) custom-call(bf16[256,1024]{1,0:T(8,128)(2,1)S(1)} %get-tuple-element.63.att_ref, bf16[128,768]{1,0:T(8,128)(2,1)S(1)} %collective-permute-done.20.relay_top, bf16[128,768]{1,0:T(8,128)(2,1)S(1)} %collective-permute-done.21.relay_bottom, ...), custom_call_target="tpu_custom_call" | custom-call | flops 1207959552 | bytes 4718592 | tf_op jit(solution)/shard_map/pallas_call | solution.py:435
  77.5 1.8 %collective-permute-done.26.one_ref = bf16[4,128,128]{2,1,0:T(8,128)(2,1)S(1)} collective-permute-done((bf16[4,128,128]{2,1,0:T(8,128)(2,1)S(1)}, bf16[4,128,128]{2,1,0:T(8,128)(2,1)S(1)}, u32[]{:S(2)}, u32[]{:S(2)}) %collective-permute-start.26) | collective-permute-done | bytes 131104 | tf_op jit(solution)/shard_map/ppermute | solution.py:642
  79.5 1.8 %collective-permute-start.29 = (bf16[4,128,128]{2,1,0:T(8,128)(2,1)S(1)}, bf16[4,128,128]{2,1,0:T(8,128)(2,1)S(1)}, u32[]{:S(2)}, u32[]{:S(2)}) collective-permute-start(bf16[4,128,128]{2,1,0:T(8,128)(2,1)S(1)} %get-tuple-element.80), channel_id=1, source_target_pairs={{0,4},{4,0},{8,12},{12,8},{16,20},{20,16},{24,28},{28,24},{32,36},... | collective-permute-start | bytes 393224 | tf_op jit(solution)/shard_map/ppermute | solution.py:621
  83.8 1.6 %collective-permute-start.32 = (bf16[256,64]{1,0:T(8,128)(2,1)S(1)}, bf16[256,64]{1,0:T(8,128)(2,1)S(1)}, u32[]{:S(2)}, u32[]{:S(2)}) collective-permute-start(bf16[256,64]{1,0:T(8,128)(2,1)S(1)} %get-tuple-element.85.back0), channel_id=1, source_target_pairs={{0,3},{1,0},{2,1},{3,2},{4,7},{5,4},{6,5},{7,6},{8,11},{9,8},{10,9... | collective-permute-start | bytes 98312 | tf_op jit(solution)/shard_map/ppermute | solution.py:612
  85.9 1.9 %collective-permute-done.30.unread.back2 = bf16[256,64]{1,0:T(8,128)(2,1)S(1)} collective-permute-done((bf16[256,64]{1,0:T(8,128)(2,1)S(1)}, bf16[256,64]{1,0:T(8,128)(2,1)S(1)}, u32[]{:S(2)}, u32[]{:S(2)}) %collective-permute-start.30) | collective-permute-done | bytes 32800 | tf_op jit(solution)/shard_map/ppermute | solution.py:612
  92.1 1.9 %collective-permute-start.33 = (bf16[28,16,128]{2,1,0:T(8,128)(2,1)S(1)}, bf16[28,16,128]{2,1,0:T(8,128)(2,1)S(1)}, u32[]{:S(2)}, u32[]{:S(2)}) collective-permute-start(bf16[28,16,128]{2,1,0:T(8,128)(2,1)S(1)} %get-tuple-element.89), channel_id=1, source_target_pairs={{0,4},{4,0},{8,12},{12,8},{16,20},{20,16},{24,28},{28,24},{32,36},... | collective-permute-start | bytes 344072 | tf_op jit(solution)/shard_map/ppermute | solution.py:621
  94.9 1.2 collective-permute-start.36
  96.1 1.9 %collective-permute-start.35 = (bf16[28,16,128]{2,1,0:T(8,128)(2,1)S(1)}, bf16[28,16,128]{2,1,0:T(8,128)(2,1)S(1)}, u32[]{:S(2)}, u32[]{:S(2)}) collective-permute-start(bf16[28,16,128]{2,1,0:T(8,128)(2,1)S(1)} %shard_map.152), channel_id=1, source_target_pairs={{0,24},{4,28},{8,0},{12,4},{16,8},{20,12},{24,16},{28,20},{32,56},... | collective-permute-start | bytes 344072 | tf_op jit(solution)/shard_map/ppermute | solution.py:642
  98.0 2.9 %collective-permute-start.24 = (bf16[256,768]{1,0:T(8,128)(2,1)S(1)}, bf16[256,768]{1,0:T(8,128)(2,1)S(1)}, u32[]{:S(2)}, u32[]{:S(2)}) collective-permute-start(bf16[256,768]{1,0:T(8,128)(2,1)S(1)} %get-tuple-element.75), channel_id=1, source_target_pairs={{0,1},{1,2},{2,3},{3,0},{4,5},{5,6},{6,7},{7,4},{8,9},{9,10},{10,1... | collective-permute-start | bytes 1179656 | tf_op jit(solution)/shard_map/ppermute | solution.py:612
  101.0 2.0 %collective-permute-start.25 = (bf16[256,768]{1,0:T(8,128)(2,1)S(1)}, bf16[256,768]{1,0:T(8,128)(2,1)S(1)}, u32[]{:S(2)}, u32[]{:S(2)}) collective-permute-start(bf16[256,768]{1,0:T(8,128)(2,1)S(1)} %get-tuple-element.76), channel_id=1, source_target_pairs={{0,3},{1,0},{2,1},{3,2},{4,7},{5,4},{6,5},{7,6},{8,11},{9,8},{10,9... | collective-permute-start | bytes 1179656 | tf_op jit(solution)/shard_map/ppermute | solution.py:612
  104.6 2.6 %collective-permute-start.39 = (bf16[256,768]{1,0:T(8,128)(2,1)S(1)}, bf16[256,768]{1,0:T(8,128)(2,1)S(1)}, u32[]{:S(2)}, u32[]{:S(2)}) collective-permute-start(bf16[256,768]{1,0:T(8,128)(2,1)S(1)} %shard_map.150.refs_0_), channel_id=1, source_target_pairs={{0,3},{1,0},{2,1},{3,2},{4,7},{5,4},{6,5},{7,6},{8,11},{9,8},{10,9... | collective-permute-start | bytes 1179656 | tf_op jit(solution)/shard_map/ppermute | solution.py:612
  107.2 1.5 %collective-permute-done.42.refs_2_ = bf16[28,16,128]{2,1,0:T(8,128)(2,1)S(1)} collective-permute-done((bf16[28,16,128]{2,1,0:T(8,128)(2,1)S(1)}, bf16[28,16,128]{2,1,0:T(8,128)(2,1)S(1)}, u32[]{:S(2)}, u32[]{:S(2)}) %collective-permute-start.42) | collective-permute-done | bytes 114720 | tf_op jit(solution)/shard_map/ppermute | solution.py:642
  108.8 1.1 collective-permute-start.41
  109.9 2.8 %collective-permute-done.41.refs_1_ = bf16[28,16,128]{2,1,0:T(8,128)(2,1)S(1)} collective-permute-done((bf16[28,16,128]{2,1,0:T(8,128)(2,1)S(1)}, bf16[28,16,128]{2,1,0:T(8,128)(2,1)S(1)}, u32[]{:S(2)}, u32[]{:S(2)}) %collective-permute-start.41) | collective-permute-done | bytes 114720 | tf_op jit(solution)/shard_map/ppermute | solution.py:642
  112.7 5.1 %collective-permute-done.40.refs_0_ = bf16[28,16,128]{2,1,0:T(8,128)(2,1)S(1)} collective-permute-done((bf16[28,16,128]{2,1,0:T(8,128)(2,1)S(1)}, bf16[28,16,128]{2,1,0:T(8,128)(2,1)S(1)}, u32[]{:S(2)}, u32[]{:S(2)}) %collective-permute-start.40) | collective-permute-done | bytes 114720 | tf_op jit(solution)/shard_map/ppermute | solution.py:642
  117.9 4.6 %collective-permute-start.43 = (bf16[28,16,128]{2,1,0:T(8,128)(2,1)S(1)}, bf16[28,16,128]{2,1,0:T(8,128)(2,1)S(1)}, u32[]{:S(2)}, u32[]{:S(2)}) collective-permute-start(bf16[28,16,128]{2,1,0:T(8,128)(2,1)S(1)} %shard_map.157.own_ref), channel_id=1, source_target_pairs={{0,4},{4,0},{8,12},{12,8},{16,20},{20,16},{24,28},{28,24},{32,36},... | collective-permute-start | bytes 344072 | tf_op jit(solution)/shard_map/ppermute | solution.py:621
  124.6 1.1 shard_map.156
  (104 shorter events, 23.9 us)
Async XLA Ops:
  0.6 8.9 %slice-start = ((s8[18874368]{0:T(1024)(128)(4,1)}), s8[4194304]{0:T(1024)(128)(4,1)S(1)}, s32[]{:S(2)}) async-start(s8[18874368]{0:T(1024)(128)(4,1)} %bitcast.6), calls=%async_computation | async-start | bytes 8388608
  3.2 8.6 %collective-permute-start.2 = (bf16[128,1024]{1,0:T(8,128)(2,1)S(1)}, bf16[128,1024]{1,0:T(8,128)(2,1)S(1)}, u32[]{:S(2)}, u32[]{:S(2)}) collective-permute-start(bf16[128,1024]{1,0:T(8,128)(2,1)S(1)} %get-tuple-element.51), channel_id=1, source_target_pairs={{0,3},{1,0},{2,1},{3,2},{4,7},{5,4},{6,5},{7,6},{8,11},{9,8},{10,9... | collective-permute-start | bytes 786440 | tf_op jit(solution)/shard_map/ppermute | solution.py:612
  6.9 8.4 %collective-permute-start = (bf16[128,1024]{1,0:T(8,128)(2,1)S(1)}, bf16[128,1024]{1,0:T(8,128)(2,1)S(1)}, u32[]{:S(2)}, u32[]{:S(2)}) collective-permute-start(bf16[128,1024]{1,0:T(8,128)(2,1)S(1)} %get-tuple-element.50.own_ref), channel_id=1, source_target_pairs={{0,1},{1,2},{2,3},{3,0},{4,5},{5,6},{6,7},{7,4},{8,9},{9,10},{10,1... | collective-permute-start | bytes 786440 | tf_op jit(solution)/shard_map/ppermute | solution.py:612
  6.9 13.7 %collective-permute-start.5 = (bf16[128,1024]{1,0:T(8,128)(2,1)S(1)}, bf16[128,1024]{1,0:T(8,128)(2,1)S(1)}, u32[]{:S(2)}, u32[]{:S(2)}) collective-permute-start(bf16[128,1024]{1,0:T(8,128)(2,1)S(1)} %get-tuple-element.51), channel_id=1, source_target_pairs={{0,1},{1,2},{2,3},{3,0},{4,5},{5,6},{6,7},{7,4},{8,9},{9,10},{10,1... | collective-permute-start | bytes 786440 | tf_op jit(solution)/shard_map/ppermute | solution.py:612
  6.9 15.3 %collective-permute-start.4 = (bf16[128,1024]{1,0:T(8,128)(2,1)S(1)}, bf16[128,1024]{1,0:T(8,128)(2,1)S(1)}, u32[]{:S(2)}, u32[]{:S(2)}) collective-permute-start(bf16[128,1024]{1,0:T(8,128)(2,1)S(1)} %get-tuple-element.50.own_ref), channel_id=1, source_target_pairs={{0,3},{1,0},{2,1},{3,2},{4,7},{5,4},{6,5},{7,6},{8,11},{9,8},{10,9... | collective-permute-start | bytes 786440 | tf_op jit(solution)/shard_map/ppermute | solution.py:612
  11.8 13.8 %collective-permute-start.3 = (bf16[128,1024]{1,0:T(8,128)(2,1)S(1)}, bf16[128,1024]{1,0:T(8,128)(2,1)S(1)}, u32[]{:S(2)}, u32[]{:S(2)}) collective-permute-start(bf16[128,1024]{1,0:T(8,128)(2,1)S(1)} %collective-permute-done.2.bottom_ref), channel_id=1, source_target_pairs={{0,3},{1,0},{2,1},{3,2},{4,7},{5,4},{6,5},{7,6},{8,11},{9,8},{10,9... | collective-permute-start | bytes 786440 | tf_op jit(solution)/shard_map/ppermute | solution.py:612
  15.3 10.9 %collective-permute-start.1 = (bf16[128,1024]{1,0:T(8,128)(2,1)S(1)}, bf16[128,1024]{1,0:T(8,128)(2,1)S(1)}, u32[]{:S(2)}, u32[]{:S(2)}) collective-permute-start(bf16[128,1024]{1,0:T(8,128)(2,1)S(1)} %collective-permute-done.top_ref.one_ref), channel_id=1, source_target_pairs={{0,1},{1,2},{2,3},{3,0},{4,5},{5,6},{6,7},{7,4},{8,9},{9,10},{10,1... | collective-permute-start | bytes 786440 | tf_op jit(solution)/shard_map/ppermute | solution.py:612
  23.8 31.5 %slice-start.5 = ((s8[6291456]{0:T(1024)(128)(4,1)}), s8[4194304]{0:T(1024)(128)(4,1)S(1)}, s32[]{:S(2)}) async-start(s8[6291456]{0:T(1024)(128)(4,1)} %bitcast.8), calls=%async_computation.5 | async-start | bytes 8388608
  24.1 31.2 %slice-start.6 = ((s8[6291456]{0:T(1024)(128)(4,1)}), s8[2097152]{0:T(1024)(128)(4,1)S(1)}, s32[]{:S(2)}) async-start(s8[6291456]{0:T(1024)(128)(4,1)} %bitcast.8), calls=%async_computation.6 | async-start | bytes 4194304
  24.1 13.7 %collective-permute-start.11 = (bf16[256,896]{1,0:T(8,128)(2,1)S(1)}, bf16[256,896]{1,0:T(8,128)(2,1)S(1)}, u32[]{:S(2)}, u32[]{:S(2)}) collective-permute-start(bf16[256,896]{1,0:T(8,128)(2,1)S(1)} %shard_map.134.cot0), channel_id=1, source_target_pairs={{0,3},{1,0},{2,1},{3,2},{4,7},{5,4},{6,5},{7,6},{8,11},{9,8},{10,9... | collective-permute-start | bytes 1376264 | tf_op jit(solution)/shard_map/ppermute | solution.py:612
  24.2 13.6 %collective-permute-start.10 = (bf16[256,896]{1,0:T(8,128)(2,1)S(1)}, bf16[256,896]{1,0:T(8,128)(2,1)S(1)}, u32[]{:S(2)}, u32[]{:S(2)}) collective-permute-start(bf16[256,896]{1,0:T(8,128)(2,1)S(1)} %shard_map.134.cot0), channel_id=1, source_target_pairs={{0,1},{1,2},{2,3},{3,0},{4,5},{5,6},{6,7},{7,4},{8,9},{9,10},{10,1... | collective-permute-start | bytes 1376264 | tf_op jit(solution)/shard_map/ppermute | solution.py:612
  28.4 4.5 %collective-permute-start.6 = (bf16[4,128,128]{2,1,0:T(8,128)(2,1)S(1)}, bf16[4,128,128]{2,1,0:T(8,128)(2,1)S(1)}, u32[]{:S(2)}, u32[]{:S(2)}) collective-permute-start(bf16[4,128,128]{2,1,0:T(8,128)(2,1)S(1)} %get-tuple-element.54), channel_id=1, source_target_pairs={{0,4},{4,0},{8,12},{12,8},{16,20},{20,16},{24,28},{28,24},{32,36},... | collective-permute-start | bytes 393224 | tf_op jit(solution)/shard_map/ppermute | solution.py:621
  32.9 22.5 %copy-start.4 = (bf16[1024,16]{0,1:T(8,128)(2,1)S(1)}, bf16[1024,16]{0,1:T(8,128)(2,1)}, u32[]{:S(2)}) copy-start(bf16[1024,16]{0,1:T(8,128)(2,1)} %param.13) | copy-start | bytes 98308
  32.9 6.0 %collective-permute-start.7 = (bf16[4,128,128]{2,1,0:T(8,128)(2,1)S(1)}, bf16[4,128,128]{2,1,0:T(8,128)(2,1)S(1)}, u32[]{:S(2)}, u32[]{:S(2)}) collective-permute-start(bf16[4,128,128]{2,1,0:T(8,128)(2,1)S(1)} %shard_map.132.unread), channel_id=1, source_target_pairs={{0,8},{4,12},{8,16},{12,20},{16,24},{20,28},{24,0},{28,4},{32,40},... | collective-permute-start | bytes 393224 | tf_op jit(solution)/shard_map/ppermute | solution.py:642
  34.2 8.5 %collective-permute-start.9 = (bf16[4,128,128]{2,1,0:T(8,128)(2,1)S(1)}, bf16[4,128,128]{2,1,0:T(8,128)(2,1)S(1)}, u32[]{:S(2)}, u32[]{:S(2)}) collective-permute-start(bf16[4,128,128]{2,1,0:T(8,128)(2,1)S(1)} %shard_map.132.unread), channel_id=1, source_target_pairs={{0,16},{4,20},{8,24},{12,28},{16,0},{20,4},{24,8},{28,12},{32,48},... | collective-permute-start | bytes 393224 | tf_op jit(solution)/shard_map/ppermute | solution.py:642
  36.6 6.1 %collective-permute-start.8 = (bf16[4,128,128]{2,1,0:T(8,128)(2,1)S(1)}, bf16[4,128,128]{2,1,0:T(8,128)(2,1)S(1)}, u32[]{:S(2)}, u32[]{:S(2)}) collective-permute-start(bf16[4,128,128]{2,1,0:T(8,128)(2,1)S(1)} %shard_map.132.unread), channel_id=1, source_target_pairs={{0,24},{4,28},{8,0},{12,4},{16,8},{20,12},{24,16},{28,20},{32,56},... | collective-permute-start | bytes 393224 | tf_op jit(solution)/shard_map/ppermute | solution.py:642
  38.9 16.4 %collective-permute-start.17 = (bf16[128,896]{1,0:T(8,128)(2,1)S(1)}, bf16[128,896]{1,0:T(8,128)(2,1)S(1)}, u32[]{:S(2)}, u32[]{:S(2)}) collective-permute-start(bf16[128,896]{1,0:T(8,128)(2,1)S(1)} %get-tuple-element.61), channel_id=1, source_target_pairs={{0,3},{1,0},{2,1},{3,2},{4,7},{5,4},{6,5},{7,6},{8,11},{9,8},{10,9... | collective-permute-start | bytes 688136 | tf_op jit(solution)/shard_map/ppermute | solution.py:612
  40.0 15.3 %collective-permute-start.16 = (bf16[128,896]{1,0:T(8,128)(2,1)S(1)}, bf16[128,896]{1,0:T(8,128)(2,1)S(1)}, u32[]{:S(2)}, u32[]{:S(2)}) collective-permute-start(bf16[128,896]{1,0:T(8,128)(2,1)S(1)} %get-tuple-element.56.refs_1_), channel_id=1, source_target_pairs={{0,1},{1,2},{2,3},{3,0},{4,5},{5,6},{6,7},{7,4},{8,9},{9,10},{10,1... | collective-permute-start | bytes 688136 | tf_op jit(solution)/shard_map/ppermute | solution.py:612
  42.9 6.2 %collective-permute-start.14 = (bf16[4,128,128]{2,1,0:T(8,128)(2,1)S(1)}, bf16[4,128,128]{2,1,0:T(8,128)(2,1)S(1)}, u32[]{:S(2)}, u32[]{:S(2)}) collective-permute-start(bf16[4,128,128]{2,1,0:T(8,128)(2,1)S(1)} %get-tuple-element.58), channel_id=1, source_target_pairs={{0,64},{4,68},{8,72},{12,76},{16,80},{20,84},{24,88},{28,92},{32,9... | collective-permute-start | bytes 393224 | tf_op jit(solution)/shard_map/ppermute | solution.py:642
  46.7 5.9 %collective-permute-start.13 = (bf16[4,128,128]{2,1,0:T(8,128)(2,1)S(1)}, bf16[4,128,128]{2,1,0:T(8,128)(2,1)S(1)}, u32[]{:S(2)}, u32[]{:S(2)}) collective-permute-start(bf16[4,128,128]{2,1,0:T(8,128)(2,1)S(1)} %get-tuple-element.58), channel_id=1, source_target_pairs={{0,96},{4,100},{8,104},{12,108},{16,112},{20,116},{24,120},{28,124... | collective-permute-start | bytes 393224 | tf_op jit(solution)/shard_map/ppermute | solution.py:642
  47.1 5.5 %collective-permute-start.12 = (bf16[4,128,128]{2,1,0:T(8,128)(2,1)S(1)}, bf16[4,128,128]{2,1,0:T(8,128)(2,1)S(1)}, u32[]{:S(2)}, u32[]{:S(2)}) collective-permute-start(bf16[4,128,128]{2,1,0:T(8,128)(2,1)S(1)} %get-tuple-element.58), channel_id=1, source_target_pairs={{0,32},{4,36},{8,40},{12,44},{16,48},{20,52},{24,56},{28,60},{32,6... | collective-permute-start | bytes 393224 | tf_op jit(solution)/shard_map/ppermute | solution.py:642
  52.8 4.5 %collective-permute-start.15 = (bf16[4,128,128]{2,1,0:T(8,128)(2,1)S(1)}, bf16[4,128,128]{2,1,0:T(8,128)(2,1)S(1)}, u32[]{:S(2)}, u32[]{:S(2)}) collective-permute-start(bf16[4,128,128]{2,1,0:T(8,128)(2,1)S(1)} %get-tuple-element.60), channel_id=1, source_target_pairs={{0,4},{4,0},{8,12},{12,8},{16,20},{20,16},{24,28},{28,24},{32,36},... | collective-permute-start | bytes 393224 | tf_op jit(solution)/shard_map/ppermute | solution.py:621
  58.7 1.4 %collective-permute-start.18 = (bf16[4,128,128]{2,1,0:T(8,128)(2,1)S(1)}, bf16[4,128,128]{2,1,0:T(8,128)(2,1)S(1)}, u32[]{:S(2)}, u32[]{:S(2)}) collective-permute-start(bf16[4,128,128]{2,1,0:T(8,128)(2,1)S(1)} %get-tuple-element.65), channel_id=1, source_target_pairs={{0,4},{4,0},{8,12},{12,8},{16,20},{20,16},{24,28},{28,24},{32,36},... | collective-permute-start | bytes 393224 | tf_op jit(solution)/shard_map/ppermute | solution.py:621
  60.1 7.5 %collective-permute-start.19 = (bf16[4,128,128]{2,1,0:T(8,128)(2,1)S(1)}, bf16[4,128,128]{2,1,0:T(8,128)(2,1)S(1)}, u32[]{:S(2)}, u32[]{:S(2)}) collective-permute-start(bf16[4,128,128]{2,1,0:T(8,128)(2,1)S(1)} %shard_map.140.unread), channel_id=1, source_target_pairs={{0,8},{4,12},{8,16},{12,20},{16,24},{20,28},{24,0},{28,4},{32,40},... | collective-permute-start | bytes 393224 | tf_op jit(solution)/shard_map/ppermute | solution.py:642
  61.2 8.5 %collective-permute-start.23 = (bf16[4,128,128]{2,1,0:T(8,128)(2,1)S(1)}, bf16[4,128,128]{2,1,0:T(8,128)(2,1)S(1)}, u32[]{:S(2)}, u32[]{:S(2)}) collective-permute-start(bf16[4,128,128]{2,1,0:T(8,128)(2,1)S(1)} %shard_map.140.unread), channel_id=1, source_target_pairs={{0,16},{4,20},{8,24},{12,28},{16,0},{20,4},{24,8},{28,12},{32,48},... | collective-permute-start | bytes 393224 | tf_op jit(solution)/shard_map/ppermute | solution.py:642
  63.4 6.4 %collective-permute-start.22 = (bf16[4,128,128]{2,1,0:T(8,128)(2,1)S(1)}, bf16[4,128,128]{2,1,0:T(8,128)(2,1)S(1)}, u32[]{:S(2)}, u32[]{:S(2)}) collective-permute-start(bf16[4,128,128]{2,1,0:T(8,128)(2,1)S(1)} %shard_map.140.unread), channel_id=1, source_target_pairs={{0,24},{4,28},{8,0},{12,4},{16,8},{20,12},{24,16},{28,20},{32,56},... | collective-permute-start | bytes 393224 | tf_op jit(solution)/shard_map/ppermute | solution.py:642
  68.2 6.9 %collective-permute-start.21 = (bf16[128,768]{1,0:T(8,128)(2,1)S(1)}, bf16[128,768]{1,0:T(8,128)(2,1)S(1)}, u32[]{:S(2)}, u32[]{:S(2)}) collective-permute-start(bf16[128,768]{1,0:T(8,128)(2,1)S(1)} %get-tuple-element.72), channel_id=1, source_target_pairs={{0,3},{1,0},{2,1},{3,2},{4,7},{5,4},{6,5},{7,6},{8,11},{9,8},{10,9... | collective-permute-start | bytes 589832 | tf_op jit(solution)/shard_map/ppermute | solution.py:612
  69.3 6.3 %collective-permute-start.20 = (bf16[128,768]{1,0:T(8,128)(2,1)S(1)}, bf16[128,768]{1,0:T(8,128)(2,1)S(1)}, u32[]{:S(2)}, u32[]{:S(2)}) collective-permute-start(bf16[128,768]{1,0:T(8,128)(2,1)S(1)} %get-tuple-element.71.refs_1_), channel_id=1, source_target_pairs={{0,1},{1,2},{2,3},{3,0},{4,5},{5,6},{6,7},{7,4},{8,9},{9,10},{10,1... | collective-permute-start | bytes 589832 | tf_op jit(solution)/shard_map/ppermute | solution.py:612
  69.9 7.2 %collective-permute-start.28 = (bf16[4,128,128]{2,1,0:T(8,128)(2,1)S(1)}, bf16[4,128,128]{2,1,0:T(8,128)(2,1)S(1)}, u32[]{:S(2)}, u32[]{:S(2)}) collective-permute-start(bf16[4,128,128]{2,1,0:T(8,128)(2,1)S(1)} %get-tuple-element.73.unread), channel_id=1, source_target_pairs={{0,64},{4,68},{8,72},{12,76},{16,80},{20,84},{24,88},{28,92},{32,9... | collective-permute-start | bytes 393224 | tf_op jit(solution)/shard_map/ppermute | solution.py:642
  71.8 5.7 %collective-permute-start.27 = (bf16[4,128,128]{2,1,0:T(8,128)(2,1)S(1)}, bf16[4,128,128]{2,1,0:T(8,128)(2,1)S(1)}, u32[]{:S(2)}, u32[]{:S(2)}) collective-permute-start(bf16[4,128,128]{2,1,0:T(8,128)(2,1)S(1)} %get-tuple-element.73.unread), channel_id=1, source_target_pairs={{0,96},{4,100},{8,104},{12,108},{16,112},{20,116},{24,120},{28,124... | collective-permute-start | bytes 393224 | tf_op jit(solution)/shard_map/ppermute | solution.py:642
  72.7 6.6 %collective-permute-start.26 = (bf16[4,128,128]{2,1,0:T(8,128)(2,1)S(1)}, bf16[4,128,128]{2,1,0:T(8,128)(2,1)S(1)}, u32[]{:S(2)}, u32[]{:S(2)}) collective-permute-start(bf16[4,128,128]{2,1,0:T(8,128)(2,1)S(1)} %get-tuple-element.73.unread), channel_id=1, source_target_pairs={{0,32},{4,36},{8,40},{12,44},{16,48},{20,52},{24,56},{28,60},{32,6... | collective-permute-start | bytes 393224 | tf_op jit(solution)/shard_map/ppermute | solution.py:642
  79.5 2.8 %collective-permute-start.29 = (bf16[4,128,128]{2,1,0:T(8,128)(2,1)S(1)}, bf16[4,128,128]{2,1,0:T(8,128)(2,1)S(1)}, u32[]{:S(2)}, u32[]{:S(2)}) collective-permute-start(bf16[4,128,128]{2,1,0:T(8,128)(2,1)S(1)} %get-tuple-element.80), channel_id=1, source_target_pairs={{0,4},{4,0},{8,12},{12,8},{16,20},{20,16},{24,28},{28,24},{32,36},... | collective-permute-start | bytes 393224 | tf_op jit(solution)/shard_map/ppermute | solution.py:621
  83.1 4.7 %collective-permute-start.30 = (bf16[256,64]{1,0:T(8,128)(2,1)S(1)}, bf16[256,64]{1,0:T(8,128)(2,1)S(1)}, u32[]{:S(2)}, u32[]{:S(2)}) collective-permute-start(bf16[256,64]{1,0:T(8,128)(2,1)S(1)} %get-tuple-element.85.back0), channel_id=1, source_target_pairs={{0,2},{1,3},{2,0},{3,1},{4,6},{5,7},{6,4},{7,5},{8,10},{9,11},{10,... | collective-permute-start | bytes 98312 | tf_op jit(solution)/shard_map/ppermute | solution.py:612
  83.8 7.8 %collective-permute-start.32 = (bf16[256,64]{1,0:T(8,128)(2,1)S(1)}, bf16[256,64]{1,0:T(8,128)(2,1)S(1)}, u32[]{:S(2)}, u32[]{:S(2)}) collective-permute-start(bf16[256,64]{1,0:T(8,128)(2,1)S(1)} %get-tuple-element.85.back0), channel_id=1, source_target_pairs={{0,3},{1,0},{2,1},{3,2},{4,7},{5,4},{6,5},{7,6},{8,11},{9,8},{10,9... | collective-permute-start | bytes 98312 | tf_op jit(solution)/shard_map/ppermute | solution.py:612
  85.4 6.2 %collective-permute-start.31 = (bf16[256,64]{1,0:T(8,128)(2,1)S(1)}, bf16[256,64]{1,0:T(8,128)(2,1)S(1)}, u32[]{:S(2)}, u32[]{:S(2)}) collective-permute-start(bf16[256,64]{1,0:T(8,128)(2,1)S(1)} %get-tuple-element.85.back0), channel_id=1, source_target_pairs={{0,1},{1,2},{2,3},{3,0},{4,5},{5,6},{6,7},{7,4},{8,9},{9,10},{10,1... | collective-permute-start | bytes 98312 | tf_op jit(solution)/shard_map/ppermute | solution.py:612
  88.8 14.7 %collective-permute-start.37 = (bf16[256,768]{1,0:T(8,128)(2,1)S(1)}, bf16[256,768]{1,0:T(8,128)(2,1)S(1)}, u32[]{:S(2)}, u32[]{:S(2)}) collective-permute-start(bf16[256,768]{1,0:T(8,128)(2,1)S(1)} %shard_map.148.unread), channel_id=1, source_target_pairs={{0,2},{1,3},{2,0},{3,1},{4,6},{5,7},{6,4},{7,5},{8,10},{9,11},{10,... | collective-permute-start | bytes 1179656 | tf_op jit(solution)/shard_map/ppermute | solution.py:612
  92.1 2.8 %collective-permute-start.33 = (bf16[28,16,128]{2,1,0:T(8,128)(2,1)S(1)}, bf16[28,16,128]{2,1,0:T(8,128)(2,1)S(1)}, u32[]{:S(2)}, u32[]{:S(2)}) collective-permute-start(bf16[28,16,128]{2,1,0:T(8,128)(2,1)S(1)} %get-tuple-element.89), channel_id=1, source_target_pairs={{0,4},{4,0},{8,12},{12,8},{16,20},{20,16},{24,28},{28,24},{32,36},... | collective-permute-start | bytes 344072 | tf_op jit(solution)/shard_map/ppermute | solution.py:621
  94.9 6.0 %collective-permute-start.36 = (bf16[28,16,128]{2,1,0:T(8,128)(2,1)S(1)}, bf16[28,16,128]{2,1,0:T(8,128)(2,1)S(1)}, u32[]{:S(2)}, u32[]{:S(2)}) collective-permute-start(bf16[28,16,128]{2,1,0:T(8,128)(2,1)S(1)} %shard_map.152), channel_id=1, source_target_pairs={{0,16},{4,20},{8,24},{12,28},{16,0},{20,4},{24,8},{28,12},{32,48},... | collective-permute-start | bytes 344072 | tf_op jit(solution)/shard_map/ppermute | solution.py:642
  96.1 6.8 %collective-permute-start.35 = (bf16[28,16,128]{2,1,0:T(8,128)(2,1)S(1)}, bf16[28,16,128]{2,1,0:T(8,128)(2,1)S(1)}, u32[]{:S(2)}, u32[]{:S(2)}) collective-permute-start(bf16[28,16,128]{2,1,0:T(8,128)(2,1)S(1)} %shard_map.152), channel_id=1, source_target_pairs={{0,24},{4,28},{8,0},{12,4},{16,8},{20,12},{24,16},{28,20},{32,56},... | collective-permute-start | bytes 344072 | tf_op jit(solution)/shard_map/ppermute | solution.py:642
  98.0 5.4 %collective-permute-start.34 = (bf16[28,16,128]{2,1,0:T(8,128)(2,1)S(1)}, bf16[28,16,128]{2,1,0:T(8,128)(2,1)S(1)}, u32[]{:S(2)}, u32[]{:S(2)}) collective-permute-start(bf16[28,16,128]{2,1,0:T(8,128)(2,1)S(1)} %shard_map.152), channel_id=1, source_target_pairs={{0,8},{4,12},{8,16},{12,20},{16,24},{20,28},{24,0},{28,4},{32,40},... | collective-permute-start | bytes 344072 | tf_op jit(solution)/shard_map/ppermute | solution.py:642
  98.0 24.5 %collective-permute-start.24 = (bf16[256,768]{1,0:T(8,128)(2,1)S(1)}, bf16[256,768]{1,0:T(8,128)(2,1)S(1)}, u32[]{:S(2)}, u32[]{:S(2)}) collective-permute-start(bf16[256,768]{1,0:T(8,128)(2,1)S(1)} %get-tuple-element.75), channel_id=1, source_target_pairs={{0,1},{1,2},{2,3},{3,0},{4,5},{5,6},{6,7},{7,4},{8,9},{9,10},{10,1... | collective-permute-start | bytes 1179656 | tf_op jit(solution)/shard_map/ppermute | solution.py:612
  101.0 21.6 %collective-permute-start.25 = (bf16[256,768]{1,0:T(8,128)(2,1)S(1)}, bf16[256,768]{1,0:T(8,128)(2,1)S(1)}, u32[]{:S(2)}, u32[]{:S(2)}) collective-permute-start(bf16[256,768]{1,0:T(8,128)(2,1)S(1)} %get-tuple-element.76), channel_id=1, source_target_pairs={{0,3},{1,0},{2,1},{3,2},{4,7},{5,4},{6,5},{7,6},{8,11},{9,8},{10,9... | collective-permute-start | bytes 1179656 | tf_op jit(solution)/shard_map/ppermute | solution.py:612
  103.5 5.2 %collective-permute-start.42 = (bf16[28,16,128]{2,1,0:T(8,128)(2,1)S(1)}, bf16[28,16,128]{2,1,0:T(8,128)(2,1)S(1)}, u32[]{:S(2)}, u32[]{:S(2)}) collective-permute-start(bf16[28,16,128]{2,1,0:T(8,128)(2,1)S(1)} %shard_map.153.unread.mine_ref), channel_id=1, source_target_pairs={{0,64},{4,68},{8,72},{12,76},{16,80},{20,84},{24,88},{28,92},{32,9... | collective-permute-start | bytes 344072 | tf_op jit(solution)/shard_map/ppermute | solution.py:642
  104.6 20.0 %collective-permute-start.39 = (bf16[256,768]{1,0:T(8,128)(2,1)S(1)}, bf16[256,768]{1,0:T(8,128)(2,1)S(1)}, u32[]{:S(2)}, u32[]{:S(2)}) collective-permute-start(bf16[256,768]{1,0:T(8,128)(2,1)S(1)} %shard_map.150.refs_0_), channel_id=1, source_target_pairs={{0,3},{1,0},{2,1},{3,2},{4,7},{5,4},{6,5},{7,6},{8,11},{9,8},{10,9... | collective-permute-start | bytes 1179656 | tf_op jit(solution)/shard_map/ppermute | solution.py:612
  107.2 17.4 %collective-permute-start.38 = (bf16[256,768]{1,0:T(8,128)(2,1)S(1)}, bf16[256,768]{1,0:T(8,128)(2,1)S(1)}, u32[]{:S(2)}, u32[]{:S(2)}) collective-permute-start(bf16[256,768]{1,0:T(8,128)(2,1)S(1)} %shard_map.149.unread), channel_id=1, source_target_pairs={{0,1},{1,2},{2,3},{3,0},{4,5},{5,6},{6,7},{7,4},{8,9},{9,10},{10,1... | collective-permute-start | bytes 1179656 | tf_op jit(solution)/shard_map/ppermute | solution.py:612
  108.8 3.9 %collective-permute-start.41 = (bf16[28,16,128]{2,1,0:T(8,128)(2,1)S(1)}, bf16[28,16,128]{2,1,0:T(8,128)(2,1)S(1)}, u32[]{:S(2)}, u32[]{:S(2)}) collective-permute-start(bf16[28,16,128]{2,1,0:T(8,128)(2,1)S(1)} %shard_map.153.unread.mine_ref), channel_id=1, source_target_pairs={{0,96},{4,100},{8,104},{12,108},{16,112},{20,116},{24,120},{28,124... | collective-permute-start | bytes 344072 | tf_op jit(solution)/shard_map/ppermute | solution.py:642
  112.7 5.1 %collective-permute-start.40 = (bf16[28,16,128]{2,1,0:T(8,128)(2,1)S(1)}, bf16[28,16,128]{2,1,0:T(8,128)(2,1)S(1)}, u32[]{:S(2)}, u32[]{:S(2)}) collective-permute-start(bf16[28,16,128]{2,1,0:T(8,128)(2,1)S(1)} %shard_map.153.unread.mine_ref), channel_id=1, source_target_pairs={{0,32},{4,36},{8,40},{12,44},{16,48},{20,52},{24,56},{28,60},{32,6... | collective-permute-start | bytes 344072 | tf_op jit(solution)/shard_map/ppermute | solution.py:642
  117.9 7.8 %collective-permute-start.43 = (bf16[28,16,128]{2,1,0:T(8,128)(2,1)S(1)}, bf16[28,16,128]{2,1,0:T(8,128)(2,1)S(1)}, u32[]{:S(2)}, u32[]{:S(2)}) collective-permute-start(bf16[28,16,128]{2,1,0:T(8,128)(2,1)S(1)} %shard_map.157.own_ref), channel_id=1, source_target_pairs={{0,4},{4,0},{8,12},{12,8},{16,20},{20,16},{24,28},{28,24},{32,36},... | collective-permute-start | bytes 344072 | tf_op jit(solution)/shard_map/ppermute | solution.py:621
  (11 other events, 38.4 us)
where the time goes:
time: 127 us
  starting transfers between devices  63 us (50%)
  waiting for transfers between devices  32.5 us (26%)
  Pallas kernels  27.6 us (22%)
  local copies, waits for them, and re-layouts  2.31 us (2%)
    ppermute x20, starting transfers between devices, shift(): return lax.ppermute(array, 'head', [(i, (i + by) % n) for i in range(n)])  25.3 us
    ppermute x18, starting transfers between devices, along(): return lax.ppermute(array, 'ctx', pairs)  23.4 us
    ppermute x18, waiting for transfers between devices, along(): return lax.ppermute(array, 'ctx', pairs)  19.1 us
    ppermute x6, starting transfers between devices, swap_cores(): return lax.ppermute(array, 'ctx', [(i, i ^ 1) for i in range(n)])  14.3 us
    ppermute x20, waiting for transfers between devices, shift(): return lax.ppermute(array, 'head', [(i, (i + by) % n) for i in range(n)])  9.12 us
    ppermute x6, waiting for transfers between devices, swap_cores(): return lax.ppermute(array, 'ctx', [(i, i ^ 1) for i in range(n)])  4.26 us
    pallas_call x4, Pallas kernels, input_call(): call(kernel, [IN_VMEM] * 3 + [UNREAD] * len(more), out, 4 * rows * cols *...  4.06 us
    pallas_call x2, Pallas kernels, project_next(): call(functools.partial(project_next_kernel, by), [IN_VMEM] * 4, struct((3...  3.21 us
  transfers between devices with their start and end apart: 44, of which 19 were waited for; matrix products, arithmetic and copies ran while one was open for 0% of the time, Pallas kernels for 19%

commit v1 on v0

--- a/solution.py
+++ b/solution.py
@@ -369,7 +369,7 @@
 
 
 def across_kernel(
-    qkv_ref, own_ref, back_ref, dk_ref, dv_ref, back_q_ref, mid_ref, up_ref, out_ref, low_ref
+    qkv_ref, own_ref, back_ref, dk_ref, dv_ref, back_q_ref, mid_ref, up_ref, unread, out_ref, low_ref
 ):
     for h in range(out_ref.shape[2] // HEAD_DIM):
         at = lanes_of(h)
@@ -382,15 +382,15 @@
         low_ref[:, m * RANK : (m + 1) * RANK] = mm(out_ref[m - 1], up_ref[m], NT).astype(bf16)
 
 
-def across_blocks(qkv, held, dk, dv, back_q, mid, up):
+def across_blocks(qkv, held, dk, dv, back_q, mid, up, unread):
     _, rows, cols = qkv.shape
     return call(
         across_kernel,
-        [IN_VMEM] * 8,
+        [IN_VMEM] * 8 + [UNREAD],
         [struct((2, rows, cols), bf16), struct((rows, 4 * RANK), bf16)],
         8 * rows * cols * HEAD_DIM,
         18 * rows * cols,
-    )(qkv, *held, dk, dv, back_q, mid, up)
+    )(qkv, *held, dk, dv, back_q, mid, up, unread)
 
 
 def output_product(by, att_ref, weight_ref, width):
@@ -398,22 +398,22 @@
     return mm(att_ref[...], weight_ref[:, chunk])
 
 
-def output_far_kernel(att_ref, weight_ref, unread0, unread1, top_ref, bottom_ref):
+def output_far_kernel(att_ref, weight_ref, top_ref, bottom_ref):
     half, width = top_ref.shape
     part = output_product(2, att_ref, weight_ref, width).astype(bf16)
     top_ref[...] = part[:half]
     bottom_ref[...] = part[half:]
 
 
-def output_far(att, weight, width, unread):
+def output_far(att, weight, width):
     rows, cols = att.shape
     return call(
         output_far_kernel,
-        [IN_VMEM] * 2 + [UNREAD] * 2,
+        [IN_VMEM] * 2,
         [struct((rows // 2, width), bf16)] * 2,
         2 * rows * cols * width,
         2 * cols * width,
-    )(att, weight, *unread)
+    )(att, weight)
 
 
 def output_near_kernel(
@@ -441,21 +441,34 @@
     )(att, *relays, weight, unread)
 
 
-def output_sum_kernel(own_ref, one_ref, three_ref, low_ref, up_ref, unread, out_ref):
-    total = own_ref[...] + one_ref[...].astype(f32) + three_ref[...].astype(f32)
-    total = total + adapter_scale * mm(low_ref[:, 3 * RANK :], up_ref[...])
+def output_merge_kernel(own_ref, one_ref, three_ref, unread, out_ref):
+    out_ref[...] = own_ref[...] + one_ref[...].astype(f32) + three_ref[...].astype(f32)
+
+
+def output_merge(own, parts, unread):
+    return call(
+        output_merge_kernel,
+        [IN_VMEM] * 3 + [UNREAD],
+        struct(own.shape, f32),
+        2 * own.size,
+        12 * own.size,
+    )(own, *parts, unread)
+
+
+def output_sum_kernel(merged_ref, low_ref, up_ref, unread, out_ref):
+    total = merged_ref[...] + adapter_scale * mm(low_ref[:, 3 * RANK :], up_ref[...])
     out_ref[...] = total.astype(bf16)
 
 
-def output_sum(own, parts, low, up, unread):
-    rows, width = own.shape
+def output_sum(merged, low, up, unread):
+    rows, width = merged.shape
     return call(
         output_sum_kernel,
-        [IN_VMEM] * 5 + [UNREAD],
+        [IN_VMEM] * 3 + [UNREAD],
         struct((rows, width), bf16),
         2 * rows * width * RANK,
-        10 * rows * width,
-    )(own, *parts, low, up, unread)
+        6 * rows * width,
+    )(merged, low, up, unread)
 
 
 def query_kernel(dq_ref, weight_ref, unread, out_ref):
@@ -730,8 +743,10 @@
     )[0]
 
 
-def sum_rest(row):
-    (total,) = glue(functools.partial(row_sum_kernel, 3), [row] + from_axis(row, "z"), [bf16])
+def sum_rest(row, during):
+    (total,) = glue(
+        functools.partial(row_sum_kernel, 3), [row] + from_axis(row, "z"), [bf16], during
+    )
     return total, swap_cores(total)
 
 
@@ -780,20 +795,29 @@
 
     attended, d_raw, mine, given = forward_heads(qkv, raw, held, grad)
     pair, got = scan_pair(mine, given)
+    far_top, far_bottom = output_far(attended, output_weight, width)
+    relays = shift(far_top, 1), shift(far_bottom, 3)
+    out_own, out_one, out_three = output_near(attended, relays, output_weight, pair)
+    out_got = shift(out_one, 1), shift(out_three, 3)
+    middle = scan_row(mine, got, from_axis(pair, "x"), True, [out_own])
     dq, dk_within, dv_within, back_q, mid, early = within_block(
-        qkv, scores, held, d_raw, attended, back_mid, low, input_up_weights, down_out_t, pair
-    )
-    arrived = from_axis(pair, "x")
-    far_top, far_bottom = output_far(attended, output_weight, width, [arrived[0], early])
-    relays = shift(far_top, 1), shift(far_bottom, 3)
-    middle = scan_row(mine, got, arrived, True, [early, far_top])
+        qkv,
+        scores,
+        held,
+        d_raw,
+        attended,
+        back_mid,
+        low,
+        input_up_weights,
+        down_out_t,
+        middle[2],
+    )
     dq_parts = query_part(dq, weight, width, middle[2])
-    out_own, out_one, out_three = output_near(attended, relays, output_weight, middle[2])
-    out_got = shift(out_one, 1), shift(out_three, 3)
-    suffix = scan_rest(middle, from_axis(middle[2], "z"), True, [dq_parts, out_own])
+    merged = output_merge(out_own, out_got, early)
+    suffix = scan_rest(middle, from_axis(middle[2], "z"), True, [dq_parts])
 
     dkv, back_part = across_blocks(
-        qkv, suffix, dk_within, dv_within, back_q, mid, input_up_weights
+        qkv, suffix, dk_within, dv_within, back_q, mid, input_up_weights, merged
     )
     back_got = from_head(back_part)
     piece, near = struct((rows, width), bf16), struct((rows, width), f32)
@@ -812,9 +836,9 @@
     pair, got = sum_pair(mine, given)
     row = sum_row(mine, got, from_axis(pair, "x"), [got_two])
     grad_own = input_call(input_own_kernel, dkv, dq_parts, weight, near, row)
-    output = output_sum(out_own, out_got, back_low, output_up_weight, row)
+    output = output_sum(merged, back_low, output_up_weight, row)
     grad_got = [got_two, got_one, got_three]
-    sums = sum_rest(row)
+    sums = sum_rest(row, [grad_own, output])
     input_grad = input_sum(grad_own, grad_got, back_low, down_t)
     grad_down_qkv, grad_up_qkv, grad_down_out, grad_up_out = unpack(
         *sums, scale_factor, width, cols

time: 127 us -> 121 us (0.953)
  waiting for transfers between devices: 32.5 us -> 27.5 us
    ppermute x18, waiting for transfers between devices: 19.1 us -> 16.6 us  [along(): return lax.ppermute(array, 'ctx', pairs)]
    ppermute x20, waiting for transfers between devices: 9.12 us -> 7.04 us  [shift(): return lax.ppermute(array, 'head', [(i, (i + by) % n) for i in range(n)])]
    pallas_call x3 -> x4, Pallas kernels: 2.5 us -> 2.59 us  [the longest x1 1.05 us: output_sum(): call(output_sum_kernel, [IN_VMEM] * 3 + [UNREAD], struct((rows, width), b...]
  transfers between devices with their start and end apart: 44 -> 44, of which waited for: 19 -> 19; matrix products, arithmetic and copies ran while one was open for 0% -> 0% of each run, Pallas kernels for 19% -> 20%
where the time goes in v1:
time: 121 us
  starting transfers between devices  62.6 us (52%)
  Pallas kernels  27.7 us (23%)
  waiting for transfers between devices  27.5 us (23%)
  local copies, waits for them, and re-layouts  2.32 us (2%)
    ppermute x20, starting transfers between devices, shift(): return lax.ppermute(array, 'head', [(i, (i + by) % n) for i in range(n)])  26 us
    ppermute x18, starting transfers between devices, along(): return lax.ppermute(array, 'ctx', pairs)  23 us
    ppermute x18, waiting for transfers between devices, along(): return lax.ppermute(array, 'ctx', pairs)  16.6 us
    ppermute x6, starting transfers between devices, swap_cores(): return lax.ppermute(array, 'ctx', [(i, i ^ 1) for i in range(n)])  13.5 us
    ppermute x20, waiting for transfers between devices, shift(): return lax.ppermute(array, 'head', [(i, (i + by) % n) for i in range(n)])  7.04 us
    pallas_call x4, Pallas kernels, input_call(): call(kernel, [IN_VMEM] * 3 + [UNREAD] * len(more), out, 4 * rows * cols *...  4.06 us
    ppermute x6, waiting for transfers between devices, swap_cores(): return lax.ppermute(array, 'ctx', [(i, i ^ 1) for i in range(n)])  3.81 us
    pallas_call x2, Pallas kernels, project_next(): call(functools.partial(project_next_kernel, by), [IN_VMEM] * 4, struct((3...  3.21 us
  transfers between devices with their start and end apart: 44, of which 19 were waited for; matrix products, arithmetic and copies ran while one was open for 0% of the time, Pallas kernels for 20%

profile of v1, /device:TPU:1, one launch (start us, length us, event | category | flops | bytes accessed | tf_op | source)
XLA Modules:
  0.0 121.2 jit_solution(5029303246073246386)
XLA Ops:
  0.7 1.1 copy-done.1
  1.8 1.1 copy-done.7
  3.2 2.2 %collective-permute-start = (bf16[128,1024]{1,0:T(8,128)(2,1)S(1)}, bf16[128,1024]{1,0:T(8,128)(2,1)S(1)}, u32[]{:S(2)}, u32[]{:S(2)}) collective-permute-start(bf16[128,1024]{1,0:T(8,128)(2,1)S(1)} %get-tuple-element.50.own_ref), channel_id=1, source_target_pairs={{0,1},{1,2},{2,3},{3,0},{4,5},{5,6},{6,7},{7,4},{8,9},{9,10},{10,1... | collective-permute-start | bytes 786440 | tf_op jit(solution)/shard_map/ppermute | solution.py:625
  5.4 1.5 %collective-permute-start.2 = (bf16[128,1024]{1,0:T(8,128)(2,1)S(1)}, bf16[128,1024]{1,0:T(8,128)(2,1)S(1)}, u32[]{:S(2)}, u32[]{:S(2)}) collective-permute-start(bf16[128,1024]{1,0:T(8,128)(2,1)S(1)} %get-tuple-element.51), channel_id=1, source_target_pairs={{0,3},{1,0},{2,1},{3,2},{4,7},{5,4},{6,5},{7,6},{8,11},{9,8},{10,9... | collective-permute-start | bytes 786440 | tf_op jit(solution)/shard_map/ppermute | solution.py:625
  7.0 2.7 %collective-permute-start.4 = (bf16[128,1024]{1,0:T(8,128)(2,1)S(1)}, bf16[128,1024]{1,0:T(8,128)(2,1)S(1)}, u32[]{:S(2)}, u32[]{:S(2)}) collective-permute-start(bf16[128,1024]{1,0:T(8,128)(2,1)S(1)} %get-tuple-element.50.own_ref), channel_id=1, source_target_pairs={{0,3},{1,0},{2,1},{3,2},{4,7},{5,4},{6,5},{7,6},{8,11},{9,8},{10,9... | collective-permute-start | bytes 786440 | tf_op jit(solution)/shard_map/ppermute | solution.py:625
  9.7 1.4 %shard_map.128.sum_ref = f32[3,256,1024]{2,1,0:T(8,128)S(1)} custom-call(bf16[256,768]{1,0:T(8,128)(2,1)S(1)} %copy-done.1, bf16[3,3072,1024]{2,1,0:T(8,128)(2,1)S(1)} %bitcast.7), custom_call_target="tpu_custom_call" | custom-call | flops 1207959552 | bytes 4718592 | tf_op jit(solution)/shard_map/pallas_call | solution.py:99
  11.1 1.7 %collective-permute-done.top_ref.one_ref = bf16[128,1024]{1,0:T(8,128)(2,1)S(1)} collective-permute-done((bf16[128,1024]{1,0:T(8,128)(2,1)S(1)}, bf16[128,1024]{1,0:T(8,128)(2,1)S(1)}, u32[]{:S(2)}, u32[]{:S(2)}) %collective-permute-start) | collective-permute-done | bytes 262176 | tf_op jit(solution)/shard_map/ppermute | solution.py:625
  12.8 2.7 %collective-permute-start.3 = (bf16[128,1024]{1,0:T(8,128)(2,1)S(1)}, bf16[128,1024]{1,0:T(8,128)(2,1)S(1)}, u32[]{:S(2)}, u32[]{:S(2)}) collective-permute-start(bf16[128,1024]{1,0:T(8,128)(2,1)S(1)} %collective-permute-done.2.bottom_ref), channel_id=1, source_target_pairs={{0,3},{1,0},{2,1},{3,2},{4,7},{5,4},{6,5},{7,6},{8,11},{9,8},{10,9... | collective-permute-start | bytes 786440 | tf_op jit(solution)/shard_map/ppermute | solution.py:625
  15.4 2.9 %collective-permute-done.5.bottom_ref = bf16[128,1024]{1,0:T(8,128)(2,1)S(1)} collective-permute-done((bf16[128,1024]{1,0:T(8,128)(2,1)S(1)}, bf16[128,1024]{1,0:T(8,128)(2,1)S(1)}, u32[]{:S(2)}, u32[]{:S(2)}) %collective-permute-start.5) | collective-permute-done | bytes 262176 | tf_op jit(solution)/shard_map/ppermute | solution.py:625
  18.4 1.6 %shard_map.129.sum_ref = f32[3,256,1024]{2,1,0:T(8,128)S(1)} custom-call(bf16[128,1024]{1,0:T(8,128)(2,1)S(1)} %collective-permute-done.top_ref.one_ref, bf16[128,1024]{1,0:T(8,128)(2,1)S(1)} %collective-permute-done.5.bottom_ref, f32[3,256,1024]{2,1,0:T(8,128)S(1)} %shard_map.128.sum_ref, ...), custom_call_target="tpu_custom_call", output_to_operand_aliasing={{}: (2, {})} | custom-call | flops 1207959552 | bytes 4718592 | tf_op jit(solution)/shard_map/pallas_call | solution.py:123
  20.0 1.6 %shard_map.130.sum_ref.unread = f32[3,256,1024]{2,1,0:T(8,128)S(1)} custom-call(bf16[128,1024]{1,0:T(8,128)(2,1)S(1)} %collective-permute-done.4.top_ref.three_ref, bf16[128,1024]{1,0:T(8,128)(2,1)S(1)} %collective-permute-done.2.bottom_ref, f32[3,256,1024]{2,1,0:T(8,128)S(1)} %shard_map.129.sum_ref, ...), custom_call_target="tpu_custom_call", output_to_operand_aliasing={{}: (2, {})} | custom-call | flops 1207959552 | bytes 4718592 | tf_op jit(solution)/shard_map/pallas_call | solution.py:123
  22.0 2.7 %collective-permute-start.11 = (bf16[256,896]{1,0:T(8,128)(2,1)S(1)}, bf16[256,896]{1,0:T(8,128)(2,1)S(1)}, u32[]{:S(2)}, u32[]{:S(2)}) collective-permute-start(bf16[256,896]{1,0:T(8,128)(2,1)S(1)} %shard_map.134.cot0), channel_id=1, source_target_pairs={{0,3},{1,0},{2,1},{3,2},{4,7},{5,4},{6,5},{7,6},{8,11},{9,8},{10,9... | collective-permute-start | bytes 1376264 | tf_op jit(solution)/shard_map/ppermute | solution.py:625
  24.7 2.2 %shard_map.131 = (bf16[3,256,1024]{2,1,0:T(8,128)(2,1)S(1)}, f32[4,128,128]{2,1,0:T(8,128)S(1)}, bf16[4,128,128]{2,1,0:T(8,128)(2,1)S(1)}, bf16[256,48]{1,0:T(8,128)(2,1)S(1)}) custom-call(bf16[128,1024]{1,0:T(8,128)(2,1)S(1)} %collective-permute-done.1.top_ref, bf16[128,1024]{1,0:T(8,128)(2,1)S(1)} %collective-permute-done.3.bottom_ref, ...), custom_call_target="tpu_custom_call" | custom-call | flops 1207959552 | bytes 4718592 | tf_op jit(solution)/shard_map/pallas_call | solution.py:189
  26.9 3.0 %collective-permute-start.6 = (bf16[4,128,128]{2,1,0:T(8,128)(2,1)S(1)}, bf16[4,128,128]{2,1,0:T(8,128)(2,1)S(1)}, u32[]{:S(2)}, u32[]{:S(2)}) collective-permute-start(bf16[4,128,128]{2,1,0:T(8,128)(2,1)S(1)} %get-tuple-element.54), channel_id=1, source_target_pairs={{0,4},{4,0},{8,12},{12,8},{16,20},{20,16},{24,28},{28,24},{32,36},... | collective-permute-start | bytes 393224 | tf_op jit(solution)/shard_map/ppermute | solution.py:634
  31.0 1.4 %collective-permute-start.7 = (bf16[4,128,128]{2,1,0:T(8,128)(2,1)S(1)}, bf16[4,128,128]{2,1,0:T(8,128)(2,1)S(1)}, u32[]{:S(2)}, u32[]{:S(2)}) collective-permute-start(bf16[4,128,128]{2,1,0:T(8,128)(2,1)S(1)} %shard_map.132.unread), channel_id=1, source_target_pairs={{0,8},{4,12},{8,16},{12,20},{16,24},{20,28},{24,0},{28,4},{32,40},... | collective-permute-start | bytes 393224 | tf_op jit(solution)/shard_map/ppermute | solution.py:655
  32.4 1.4 %collective-permute-start.8 = (bf16[4,128,128]{2,1,0:T(8,128)(2,1)S(1)}, bf16[4,128,128]{2,1,0:T(8,128)(2,1)S(1)}, u32[]{:S(2)}, u32[]{:S(2)}) collective-permute-start(bf16[4,128,128]{2,1,0:T(8,128)(2,1)S(1)} %shard_map.132.unread), channel_id=1, source_target_pairs={{0,24},{4,28},{8,0},{12,4},{16,8},{20,12},{24,16},{28,20},{32,56},... | collective-permute-start | bytes 393224 | tf_op jit(solution)/shard_map/ppermute | solution.py:655
  33.7 1.6 %collective-permute-start.9 = (bf16[4,128,128]{2,1,0:T(8,128)(2,1)S(1)}, bf16[4,128,128]{2,1,0:T(8,128)(2,1)S(1)}, u32[]{:S(2)}, u32[]{:S(2)}) collective-permute-start(bf16[4,128,128]{2,1,0:T(8,128)(2,1)S(1)} %shard_map.132.unread), channel_id=1, source_target_pairs={{0,16},{4,20},{8,24},{12,28},{16,0},{20,4},{24,8},{28,12},{32,48},... | collective-permute-start | bytes 393224 | tf_op jit(solution)/shard_map/ppermute | solution.py:655
  35.4 1.6 %collective-permute-done.7.unread.one_ref = bf16[4,128,128]{2,1,0:T(8,128)(2,1)S(1)} collective-permute-done((bf16[4,128,128]{2,1,0:T(8,128)(2,1)S(1)}, bf16[4,128,128]{2,1,0:T(8,128)(2,1)S(1)}, u32[]{:S(2)}, u32[]{:S(2)}) %collective-permute-start.7) | collective-permute-done | bytes 131104 | tf_op jit(solution)/shard_map/ppermute | solution.py:655
  37.1 2.7 %collective-permute-start.17 = (bf16[128,896]{1,0:T(8,128)(2,1)S(1)}, bf16[128,896]{1,0:T(8,128)(2,1)S(1)}, u32[]{:S(2)}, u32[]{:S(2)}) collective-permute-start(bf16[128,896]{1,0:T(8,128)(2,1)S(1)} %get-tuple-element.61), channel_id=1, source_target_pairs={{0,3},{1,0},{2,1},{3,2},{4,7},{5,4},{6,5},{7,6},{8,11},{9,8},{10,9... | collective-permute-start | bytes 688136 | tf_op jit(solution)/shard_map/ppermute | solution.py:625
  41.0 1.9 %collective-permute-start.12 = (bf16[4,128,128]{2,1,0:T(8,128)(2,1)S(1)}, bf16[4,128,128]{2,1,0:T(8,128)(2,1)S(1)}, u32[]{:S(2)}, u32[]{:S(2)}) collective-permute-start(bf16[4,128,128]{2,1,0:T(8,128)(2,1)S(1)} %get-tuple-element.58), channel_id=1, source_target_pairs={{0,32},{4,36},{8,40},{12,44},{16,48},{20,52},{24,56},{28,60},{32,6... | collective-permute-start | bytes 393224 | tf_op jit(solution)/shard_map/ppermute | solution.py:655
  42.9 2.2 %collective-permute-start.13 = (bf16[4,128,128]{2,1,0:T(8,128)(2,1)S(1)}, bf16[4,128,128]{2,1,0:T(8,128)(2,1)S(1)}, u32[]{:S(2)}, u32[]{:S(2)}) collective-permute-start(bf16[4,128,128]{2,1,0:T(8,128)(2,1)S(1)} %get-tuple-element.58), channel_id=1, source_target_pairs={{0,96},{4,100},{8,104},{12,108},{16,112},{20,116},{24,120},{28,124... | collective-permute-start | bytes 393224 | tf_op jit(solution)/shard_map/ppermute | solution.py:655
  45.1 1.2 %collective-permute-start.14 = (bf16[4,128,128]{2,1,0:T(8,128)(2,1)S(1)}, bf16[4,128,128]{2,1,0:T(8,128)(2,1)S(1)}, u32[]{:S(2)}, u32[]{:S(2)}) collective-permute-start(bf16[4,128,128]{2,1,0:T(8,128)(2,1)S(1)} %get-tuple-element.58), channel_id=1, source_target_pairs={{0,64},{4,68},{8,72},{12,76},{16,80},{20,84},{24,88},{28,92},{32,9... | collective-permute-start | bytes 393224 | tf_op jit(solution)/shard_map/ppermute | solution.py:655
  46.3 1.1 collective-permute-done.12.one_ref
  47.4 4.2 %collective-permute-done.14.two_ref = bf16[4,128,128]{2,1,0:T(8,128)(2,1)S(1)} collective-permute-done((bf16[4,128,128]{2,1,0:T(8,128)(2,1)S(1)}, bf16[4,128,128]{2,1,0:T(8,128)(2,1)S(1)}, u32[]{:S(2)}, u32[]{:S(2)}) %collective-permute-start.14) | collective-permute-done | bytes 131104 | tf_op jit(solution)/shard_map/ppermute | solution.py:655
  51.7 2.5 %collective-permute-start.15 = (bf16[4,128,128]{2,1,0:T(8,128)(2,1)S(1)}, bf16[4,128,128]{2,1,0:T(8,128)(2,1)S(1)}, u32[]{:S(2)}, u32[]{:S(2)}) collective-permute-start(bf16[4,128,128]{2,1,0:T(8,128)(2,1)S(1)} %get-tuple-element.60), channel_id=1, source_target_pairs={{0,4},{4,0},{8,12},{12,8},{16,20},{20,16},{24,28},{28,24},{32,36},... | collective-permute-start | bytes 393224 | tf_op jit(solution)/shard_map/ppermute | solution.py:634
  54.2 1.9 %shard_map.138 = (f32[256,1024]{1,0:T(8,128)S(1)}, bf16[256,16]{1,0:T(8,128)(2,1)S(1)}) custom-call(bf16[256,896]{1,0:T(8,128)(2,1)S(1)} %shard_map.134.cot0, bf16[256,896]{1,0:T(8,128)(2,1)S(1)} %collective-permute-done.10.one_ref.cot1, bf16[256,896]{1,0:T(8,128)(2,1)S(1)} %collective-permute-done.11.three_ref.cot3, ...), custom_call_target="tpu_custom_call" | custom-call | flops 1610612736 | bytes 6291456 | tf_op jit(solution)/shard_map/pallas_call | solution.py:222
  56.2 1.3 %shard_map.139 = (bf16[256,1024]{1,0:T(8,128)(2,1)S(1)}, bf16[256,1024]{1,0:T(8,128)(2,1)S(1)}, f32[4,128,128]{2,1,0:T(8,128)S(1)}, bf16[4,128,128]{2,1,0:T(8,128)(2,1)S(1)}) custom-call(bf16[3,256,1024]{2,1,0:T(8,128)(2,1)S(1)} %get-tuple-element.52.qkv_ref, f32[256,1024]{1,0:T(8,128)S(1)} %get-tuple-element.55.refs_0_.raw_ref, ...), custom_call_target="tpu_custom_call" | custom-call | flops 268435456 | bytes 3670016 | tf_op jit(solution)/shard_map/pallas_call | solution.py:310
  58.2 2.7 %collective-permute-start.19 = (bf16[128,768]{1,0:T(8,128)(2,1)S(1)}, bf16[128,768]{1,0:T(8,128)(2,1)S(1)}, u32[]{:S(2)}, u32[]{:S(2)}) collective-permute-start(bf16[128,768]{1,0:T(8,128)(2,1)S(1)} %get-tuple-element.65), channel_id=1, source_target_pairs={{0,3},{1,0},{2,1},{3,2},{4,7},{5,4},{6,5},{7,6},{8,11},{9,8},{10,9... | collective-permute-start | bytes 589832 | tf_op jit(solution)/shard_map/ppermute | solution.py:625
  63.1 2.1 %collective-permute-start.24 = (bf16[4,128,128]{2,1,0:T(8,128)(2,1)S(1)}, bf16[4,128,128]{2,1,0:T(8,128)(2,1)S(1)}, u32[]{:S(2)}, u32[]{:S(2)}) collective-permute-start(bf16[4,128,128]{2,1,0:T(8,128)(2,1)S(1)} %shard_map.141.unread), channel_id=1, source_target_pairs={{0,24},{4,28},{8,0},{12,4},{16,8},{20,12},{24,16},{28,20},{32,56},... | collective-permute-start | bytes 393224 | tf_op jit(solution)/shard_map/ppermute | solution.py:655
  65.9 1.4 %shard_map.142 = (f32[256,768]{1,0:T(8,128)S(1)}, bf16[256,768]{1,0:T(8,128)(2,1)S(1)}, bf16[256,768]{1,0:T(8,128)(2,1)S(1)}) custom-call(bf16[256,1024]{1,0:T(8,128)(2,1)S(1)} %get-tuple-element.63.att_ref, bf16[128,768]{1,0:T(8,128)(2,1)S(1)} %collective-permute-done.18.relay_top, bf16[128,768]{1,0:T(8,128)(2,1)S(1)} %collective-permute-done.19.relay_bottom, ...), custom_call_target="tpu_custom_call" | custom-call | flops 1207959552 | bytes 4718592 | tf_op jit(solution)/shard_map/pallas_call | solution.py:435
  67.4 2.7 %collective-permute-start.22 = (bf16[256,768]{1,0:T(8,128)(2,1)S(1)}, bf16[256,768]{1,0:T(8,128)(2,1)S(1)}, u32[]{:S(2)}, u32[]{:S(2)}) collective-permute-start(bf16[256,768]{1,0:T(8,128)(2,1)S(1)} %get-tuple-element.70), channel_id=1, source_target_pairs={{0,3},{1,0},{2,1},{3,2},{4,7},{5,4},{6,5},{7,6},{8,11},{9,8},{10,9... | collective-permute-start | bytes 1179656 | tf_op jit(solution)/shard_map/ppermute | solution.py:625
  71.2 2.3 %collective-permute-start.27 = (bf16[4,128,128]{2,1,0:T(8,128)(2,1)S(1)}, bf16[4,128,128]{2,1,0:T(8,128)(2,1)S(1)}, u32[]{:S(2)}, u32[]{:S(2)}) collective-permute-start(bf16[4,128,128]{2,1,0:T(8,128)(2,1)S(1)} %get-tuple-element.75.unread), channel_id=1, source_target_pairs={{0,96},{4,100},{8,104},{12,108},{16,112},{20,116},{24,120},{28,124... | collective-permute-start | bytes 393224 | tf_op jit(solution)/shard_map/ppermute | solution.py:655
  74.4 3.0 %shard_map.144 = (bf16[256,1024]{1,0:T(8,128)(2,1)S(1)}, f32[256,1024]{1,0:T(8,128)S(1)}, f32[256,1024]{1,0:T(8,128)S(1)}, f32[256,16]{1,0:T(8,128)S(1)}, f32[25...) custom-call(bf16[3,256,1024]{2,1,0:T(8,128)(2,1)S(1)} %get-tuple-element.52.qkv_ref, ...), custom_call_target="tpu_custom_call" | custom-call | flops 1073741824 | bytes 4718592 | tf_op jit(solution)/shard_map/pallas_call | solution.py:355
  77.4 1.8 %shard_map.146.refs_0_.dq_ref = f32[4,256,768]{2,1,0:T(8,128)S(1)} custom-call(bf16[256,1024]{1,0:T(8,128)(2,1)S(1)} %get-tuple-element.78.dq_ref, bf16[3,3072,1024]{2,1,0:T(8,128)(2,1)S(1)} %bitcast.7, bf16[4,128,128]{2,1,0:T(8,128)(2,1)S(1)} %get-tuple-element.75.unread), custom_call_target="tpu_custom_call" | custom-call | flops 1610612736 | bytes 6291456 | tf_op jit(solution)/shard_map/pallas_call | solution.py:483
  80.1 2.7 %collective-permute-start.29 = (bf16[4,128,128]{2,1,0:T(8,128)(2,1)S(1)}, bf16[4,128,128]{2,1,0:T(8,128)(2,1)S(1)}, u32[]{:S(2)}, u32[]{:S(2)}) collective-permute-start(bf16[4,128,128]{2,1,0:T(8,128)(2,1)S(1)} %get-tuple-element.80), channel_id=1, source_target_pairs={{0,4},{4,0},{8,12},{12,8},{16,20},{20,16},{24,28},{28,24},{32,36},... | collective-permute-start | bytes 393224 | tf_op jit(solution)/shard_map/ppermute | solution.py:634
  85.6 1.9 %collective-permute-start.32 = (bf16[256,64]{1,0:T(8,128)(2,1)S(1)}, bf16[256,64]{1,0:T(8,128)(2,1)S(1)}, u32[]{:S(2)}, u32[]{:S(2)}) collective-permute-start(bf16[256,64]{1,0:T(8,128)(2,1)S(1)} %get-tuple-element.85.back0), channel_id=1, source_target_pairs={{0,3},{1,0},{2,1},{3,2},{4,7},{5,4},{6,5},{7,6},{8,11},{9,8},{10,9... | collective-permute-start | bytes 98312 | tf_op jit(solution)/shard_map/ppermute | solution.py:625
  87.5 2.0 %collective-permute-done.30.unread.back2 = bf16[256,64]{1,0:T(8,128)(2,1)S(1)} collective-permute-done((bf16[256,64]{1,0:T(8,128)(2,1)S(1)}, bf16[256,64]{1,0:T(8,128)(2,1)S(1)}, u32[]{:S(2)}, u32[]{:S(2)}) %collective-permute-start.30) | collective-permute-done | bytes 32800 | tf_op jit(solution)/shard_map/ppermute | solution.py:625
  90.5 1.0 shard_map.150.unread
  93.5 1.7 %collective-permute-start.33 = (bf16[28,16,128]{2,1,0:T(8,128)(2,1)S(1)}, bf16[28,16,128]{2,1,0:T(8,128)(2,1)S(1)}, u32[]{:S(2)}, u32[]{:S(2)}) collective-permute-start(bf16[28,16,128]{2,1,0:T(8,128)(2,1)S(1)} %get-tuple-element.89), channel_id=1, source_target_pairs={{0,4},{4,0},{8,12},{12,8},{16,20},{20,16},{24,28},{28,24},{32,36},... | collective-permute-start | bytes 344072 | tf_op jit(solution)/shard_map/ppermute | solution.py:634
  97.4 2.5 %collective-permute-start.39 = (bf16[256,768]{1,0:T(8,128)(2,1)S(1)}, bf16[256,768]{1,0:T(8,128)(2,1)S(1)}, u32[]{:S(2)}, u32[]{:S(2)}) collective-permute-start(bf16[256,768]{1,0:T(8,128)(2,1)S(1)} %shard_map.151.refs_0_), channel_id=1, source_target_pairs={{0,3},{1,0},{2,1},{3,2},{4,7},{5,4},{6,5},{7,6},{8,11},{9,8},{10,9... | collective-permute-start | bytes 1179656 | tf_op jit(solution)/shard_map/ppermute | solution.py:625
  99.8 1.8 %collective-permute-start.35 = (bf16[28,16,128]{2,1,0:T(8,128)(2,1)S(1)}, bf16[28,16,128]{2,1,0:T(8,128)(2,1)S(1)}, u32[]{:S(2)}, u32[]{:S(2)}) collective-permute-start(bf16[28,16,128]{2,1,0:T(8,128)(2,1)S(1)} %shard_map.153), channel_id=1, source_target_pairs={{0,24},{4,28},{8,0},{12,4},{16,8},{20,12},{24,16},{28,20},{32,56},... | collective-permute-start | bytes 344072 | tf_op jit(solution)/shard_map/ppermute | solution.py:655
  102.7 1.1 collective-permute-done.35.refs_2_
  103.8 3.3 %collective-permute-done.36.refs_3_ = bf16[28,16,128]{2,1,0:T(8,128)(2,1)S(1)} collective-permute-done((bf16[28,16,128]{2,1,0:T(8,128)(2,1)S(1)}, bf16[28,16,128]{2,1,0:T(8,128)(2,1)S(1)}, u32[]{:S(2)}, u32[]{:S(2)}) %collective-permute-start.36) | collective-permute-done | bytes 114720 | tf_op jit(solution)/shard_map/ppermute | solution.py:655
  107.2 2.7 %collective-permute-start.41 = (bf16[28,16,128]{2,1,0:T(8,128)(2,1)S(1)}, bf16[28,16,128]{2,1,0:T(8,128)(2,1)S(1)}, u32[]{:S(2)}, u32[]{:S(2)}) collective-permute-start(bf16[28,16,128]{2,1,0:T(8,128)(2,1)S(1)} %shard_map.154.unread.mine_ref), channel_id=1, source_target_pairs={{0,96},{4,100},{8,104},{12,108},{16,112},{20,116},{24,120},{28,124... | collective-permute-start | bytes 344072 | tf_op jit(solution)/shard_map/ppermute | solution.py:655
  110.3 1.0 shard_map.155.refs_4_
  112.8 3.3 %collective-permute-done.42.refs_2_ = bf16[28,16,128]{2,1,0:T(8,128)(2,1)S(1)} collective-permute-done((bf16[28,16,128]{2,1,0:T(8,128)(2,1)S(1)}, bf16[28,16,128]{2,1,0:T(8,128)(2,1)S(1)}, u32[]{:S(2)}, u32[]{:S(2)}) %collective-permute-start.42) | collective-permute-done | bytes 114720 | tf_op jit(solution)/shard_map/ppermute | solution.py:655
  116.2 3.0 %collective-permute-start.43 = (bf16[28,16,128]{2,1,0:T(8,128)(2,1)S(1)}, bf16[28,16,128]{2,1,0:T(8,128)(2,1)S(1)}, u32[]{:S(2)}, u32[]{:S(2)}) collective-permute-start(bf16[28,16,128]{2,1,0:T(8,128)(2,1)S(1)} %shard_map.158.own_ref), channel_id=1, source_target_pairs={{0,4},{4,0},{8,12},{12,8},{16,20},{20,16},{24,28},{28,24},{32,36},... | collective-permute-start | bytes 344072 | tf_op jit(solution)/shard_map/ppermute | solution.py:634
  119.3 1.1 shard_map.157
  (107 shorter events, 21.6 us)
Async XLA Ops:
  0.6 9.0 %slice-start = ((s8[18874368]{0:T(1024)(128)(4,1)}), s8[4194304]{0:T(1024)(128)(4,1)S(1)}, s32[]{:S(2)}) async-start(s8[18874368]{0:T(1024)(128)(4,1)} %bitcast.6), calls=%async_computation | async-start | bytes 8388608
  3.2 9.5 %collective-permute-start = (bf16[128,1024]{1,0:T(8,128)(2,1)S(1)}, bf16[128,1024]{1,0:T(8,128)(2,1)S(1)}, u32[]{:S(2)}, u32[]{:S(2)}) collective-permute-start(bf16[128,1024]{1,0:T(8,128)(2,1)S(1)} %get-tuple-element.50.own_ref), channel_id=1, source_target_pairs={{0,1},{1,2},{2,3},{3,0},{4,5},{5,6},{6,7},{7,4},{8,9},{9,10},{10,1... | collective-permute-start | bytes 786440 | tf_op jit(solution)/shard_map/ppermute | solution.py:625
  5.4 7.3 %collective-permute-start.2 = (bf16[128,1024]{1,0:T(8,128)(2,1)S(1)}, bf16[128,1024]{1,0:T(8,128)(2,1)S(1)}, u32[]{:S(2)}, u32[]{:S(2)}) collective-permute-start(bf16[128,1024]{1,0:T(8,128)(2,1)S(1)} %get-tuple-element.51), channel_id=1, source_target_pairs={{0,3},{1,0},{2,1},{3,2},{4,7},{5,4},{6,5},{7,6},{8,11},{9,8},{10,9... | collective-permute-start | bytes 786440 | tf_op jit(solution)/shard_map/ppermute | solution.py:625
  7.0 11.4 %collective-permute-start.5 = (bf16[128,1024]{1,0:T(8,128)(2,1)S(1)}, bf16[128,1024]{1,0:T(8,128)(2,1)S(1)}, u32[]{:S(2)}, u32[]{:S(2)}) collective-permute-start(bf16[128,1024]{1,0:T(8,128)(2,1)S(1)} %get-tuple-element.51), channel_id=1, source_target_pairs={{0,1},{1,2},{2,3},{3,0},{4,5},{5,6},{6,7},{7,4},{8,9},{9,10},{10,1... | collective-permute-start | bytes 786440 | tf_op jit(solution)/shard_map/ppermute | solution.py:625
  7.0 13.0 %collective-permute-start.4 = (bf16[128,1024]{1,0:T(8,128)(2,1)S(1)}, bf16[128,1024]{1,0:T(8,128)(2,1)S(1)}, u32[]{:S(2)}, u32[]{:S(2)}) collective-permute-start(bf16[128,1024]{1,0:T(8,128)(2,1)S(1)} %get-tuple-element.50.own_ref), channel_id=1, source_target_pairs={{0,3},{1,0},{2,1},{3,2},{4,7},{5,4},{6,5},{7,6},{8,11},{9,8},{10,9... | collective-permute-start | bytes 786440 | tf_op jit(solution)/shard_map/ppermute | solution.py:625
  12.7 11.9 %collective-permute-start.1 = (bf16[128,1024]{1,0:T(8,128)(2,1)S(1)}, bf16[128,1024]{1,0:T(8,128)(2,1)S(1)}, u32[]{:S(2)}, u32[]{:S(2)}) collective-permute-start(bf16[128,1024]{1,0:T(8,128)(2,1)S(1)} %collective-permute-done.top_ref.one_ref), channel_id=1, source_target_pairs={{0,1},{1,2},{2,3},{3,0},{4,5},{5,6},{6,7},{7,4},{8,9},{9,10},{10,1... | collective-permute-start | bytes 786440 | tf_op jit(solution)/shard_map/ppermute | solution.py:625
  12.8 11.9 %collective-permute-start.3 = (bf16[128,1024]{1,0:T(8,128)(2,1)S(1)}, bf16[128,1024]{1,0:T(8,128)(2,1)S(1)}, u32[]{:S(2)}, u32[]{:S(2)}) collective-permute-start(bf16[128,1024]{1,0:T(8,128)(2,1)S(1)} %collective-permute-done.2.bottom_ref), channel_id=1, source_target_pairs={{0,3},{1,0},{2,1},{3,2},{4,7},{5,4},{6,5},{7,6},{8,11},{9,8},{10,9... | collective-permute-start | bytes 786440 | tf_op jit(solution)/shard_map/ppermute | solution.py:625
  21.7 32.5 %slice-start.5 = ((s8[6291456]{0:T(1024)(128)(4,1)}), s8[4194304]{0:T(1024)(128)(4,1)S(1)}, s32[]{:S(2)}) async-start(s8[6291456]{0:T(1024)(128)(4,1)} %bitcast.8), calls=%async_computation.5 | async-start | bytes 8388608
  21.9 32.3 %slice-start.6 = ((s8[6291456]{0:T(1024)(128)(4,1)}), s8[2097152]{0:T(1024)(128)(4,1)S(1)}, s32[]{:S(2)}) async-start(s8[6291456]{0:T(1024)(128)(4,1)} %bitcast.8), calls=%async_computation.6 | async-start | bytes 4194304
  21.9 13.4 %collective-permute-start.10 = (bf16[256,896]{1,0:T(8,128)(2,1)S(1)}, bf16[256,896]{1,0:T(8,128)(2,1)S(1)}, u32[]{:S(2)}, u32[]{:S(2)}) collective-permute-start(bf16[256,896]{1,0:T(8,128)(2,1)S(1)} %shard_map.134.cot0), channel_id=1, source_target_pairs={{0,1},{1,2},{2,3},{3,0},{4,5},{5,6},{6,7},{7,4},{8,9},{9,10},{10,1... | collective-permute-start | bytes 1376264 | tf_op jit(solution)/shard_map/ppermute | solution.py:625
  22.0 13.3 %collective-permute-start.11 = (bf16[256,896]{1,0:T(8,128)(2,1)S(1)}, bf16[256,896]{1,0:T(8,128)(2,1)S(1)}, u32[]{:S(2)}, u32[]{:S(2)}) collective-permute-start(bf16[256,896]{1,0:T(8,128)(2,1)S(1)} %shard_map.134.cot0), channel_id=1, source_target_pairs={{0,3},{1,0},{2,1},{3,2},{4,7},{5,4},{6,5},{7,6},{8,11},{9,8},{10,9... | collective-permute-start | bytes 1376264 | tf_op jit(solution)/shard_map/ppermute | solution.py:625
  26.9 4.0 %collective-permute-start.6 = (bf16[4,128,128]{2,1,0:T(8,128)(2,1)S(1)}, bf16[4,128,128]{2,1,0:T(8,128)(2,1)S(1)}, u32[]{:S(2)}, u32[]{:S(2)}) collective-permute-start(bf16[4,128,128]{2,1,0:T(8,128)(2,1)S(1)} %get-tuple-element.54), channel_id=1, source_target_pairs={{0,4},{4,0},{8,12},{12,8},{16,20},{20,16},{24,28},{28,24},{32,36},... | collective-permute-start | bytes 393224 | tf_op jit(solution)/shard_map/ppermute | solution.py:634
  31.0 23.2 %copy-start.5 = (bf16[1024,16]{0,1:T(8,128)(2,1)S(1)}, bf16[1024,16]{0,1:T(8,128)(2,1)}, u32[]{:S(2)}) copy-start(bf16[1024,16]{0,1:T(8,128)(2,1)} %param.13) | copy-start | bytes 98308
  31.0 6.0 %collective-permute-start.7 = (bf16[4,128,128]{2,1,0:T(8,128)(2,1)S(1)}, bf16[4,128,128]{2,1,0:T(8,128)(2,1)S(1)}, u32[]{:S(2)}, u32[]{:S(2)}) collective-permute-start(bf16[4,128,128]{2,1,0:T(8,128)(2,1)S(1)} %shard_map.132.unread), channel_id=1, source_target_pairs={{0,8},{4,12},{8,16},{12,20},{16,24},{20,28},{24,0},{28,4},{32,40},... | collective-permute-start | bytes 393224 | tf_op jit(solution)/shard_map/ppermute | solution.py:655
  32.4 8.4 %collective-permute-start.8 = (bf16[4,128,128]{2,1,0:T(8,128)(2,1)S(1)}, bf16[4,128,128]{2,1,0:T(8,128)(2,1)S(1)}, u32[]{:S(2)}, u32[]{:S(2)}) collective-permute-start(bf16[4,128,128]{2,1,0:T(8,128)(2,1)S(1)} %shard_map.132.unread), channel_id=1, source_target_pairs={{0,24},{4,28},{8,0},{12,4},{16,8},{20,12},{24,16},{28,20},{32,56},... | collective-permute-start | bytes 393224 | tf_op jit(solution)/shard_map/ppermute | solution.py:655
  33.7 7.1 %collective-permute-start.9 = (bf16[4,128,128]{2,1,0:T(8,128)(2,1)S(1)}, bf16[4,128,128]{2,1,0:T(8,128)(2,1)S(1)}, u32[]{:S(2)}, u32[]{:S(2)}) collective-permute-start(bf16[4,128,128]{2,1,0:T(8,128)(2,1)S(1)} %shard_map.132.unread), channel_id=1, source_target_pairs={{0,16},{4,20},{8,24},{12,28},{16,0},{20,4},{24,8},{28,12},{32,48},... | collective-permute-start | bytes 393224 | tf_op jit(solution)/shard_map/ppermute | solution.py:655
  37.0 17.2 %collective-permute-start.16 = (bf16[128,896]{1,0:T(8,128)(2,1)S(1)}, bf16[128,896]{1,0:T(8,128)(2,1)S(1)}, u32[]{:S(2)}, u32[]{:S(2)}) collective-permute-start(bf16[128,896]{1,0:T(8,128)(2,1)S(1)} %get-tuple-element.56.refs_1_), channel_id=1, source_target_pairs={{0,1},{1,2},{2,3},{3,0},{4,5},{5,6},{6,7},{7,4},{8,9},{9,10},{10,1... | collective-permute-start | bytes 688136 | tf_op jit(solution)/shard_map/ppermute | solution.py:625
  37.1 17.1 %collective-permute-start.17 = (bf16[128,896]{1,0:T(8,128)(2,1)S(1)}, bf16[128,896]{1,0:T(8,128)(2,1)S(1)}, u32[]{:S(2)}, u32[]{:S(2)}) collective-permute-start(bf16[128,896]{1,0:T(8,128)(2,1)S(1)} %get-tuple-element.61), channel_id=1, source_target_pairs={{0,3},{1,0},{2,1},{3,2},{4,7},{5,4},{6,5},{7,6},{8,11},{9,8},{10,9... | collective-permute-start | bytes 688136 | tf_op jit(solution)/shard_map/ppermute | solution.py:625
  41.0 6.4 %collective-permute-start.12 = (bf16[4,128,128]{2,1,0:T(8,128)(2,1)S(1)}, bf16[4,128,128]{2,1,0:T(8,128)(2,1)S(1)}, u32[]{:S(2)}, u32[]{:S(2)}) collective-permute-start(bf16[4,128,128]{2,1,0:T(8,128)(2,1)S(1)} %get-tuple-element.58), channel_id=1, source_target_pairs={{0,32},{4,36},{8,40},{12,44},{16,48},{20,52},{24,56},{28,60},{32,6... | collective-permute-start | bytes 393224 | tf_op jit(solution)/shard_map/ppermute | solution.py:655
  42.9 4.5 %collective-permute-start.13 = (bf16[4,128,128]{2,1,0:T(8,128)(2,1)S(1)}, bf16[4,128,128]{2,1,0:T(8,128)(2,1)S(1)}, u32[]{:S(2)}, u32[]{:S(2)}) collective-permute-start(bf16[4,128,128]{2,1,0:T(8,128)(2,1)S(1)} %get-tuple-element.58), channel_id=1, source_target_pairs={{0,96},{4,100},{8,104},{12,108},{16,112},{20,116},{24,120},{28,124... | collective-permute-start | bytes 393224 | tf_op jit(solution)/shard_map/ppermute | solution.py:655
  45.1 6.4 %collective-permute-start.14 = (bf16[4,128,128]{2,1,0:T(8,128)(2,1)S(1)}, bf16[4,128,128]{2,1,0:T(8,128)(2,1)S(1)}, u32[]{:S(2)}, u32[]{:S(2)}) collective-permute-start(bf16[4,128,128]{2,1,0:T(8,128)(2,1)S(1)} %get-tuple-element.58), channel_id=1, source_target_pairs={{0,64},{4,68},{8,72},{12,76},{16,80},{20,84},{24,88},{28,92},{32,9... | collective-permute-start | bytes 393224 | tf_op jit(solution)/shard_map/ppermute | solution.py:655
  51.7 4.4 %collective-permute-start.15 = (bf16[4,128,128]{2,1,0:T(8,128)(2,1)S(1)}, bf16[4,128,128]{2,1,0:T(8,128)(2,1)S(1)}, u32[]{:S(2)}, u32[]{:S(2)}) collective-permute-start(bf16[4,128,128]{2,1,0:T(8,128)(2,1)S(1)} %get-tuple-element.60), channel_id=1, source_target_pairs={{0,4},{4,0},{8,12},{12,8},{16,20},{20,16},{24,28},{28,24},{32,36},... | collective-permute-start | bytes 393224 | tf_op jit(solution)/shard_map/ppermute | solution.py:634
  58.1 7.8 %collective-permute-start.18 = (bf16[128,768]{1,0:T(8,128)(2,1)S(1)}, bf16[128,768]{1,0:T(8,128)(2,1)S(1)}, u32[]{:S(2)}, u32[]{:S(2)}) collective-permute-start(bf16[128,768]{1,0:T(8,128)(2,1)S(1)} %get-tuple-element.64), channel_id=1, source_target_pairs={{0,1},{1,2},{2,3},{3,0},{4,5},{5,6},{6,7},{7,4},{8,9},{9,10},{10,1... | collective-permute-start | bytes 589832 | tf_op jit(solution)/shard_map/ppermute | solution.py:625
  58.2 7.7 %collective-permute-start.19 = (bf16[128,768]{1,0:T(8,128)(2,1)S(1)}, bf16[128,768]{1,0:T(8,128)(2,1)S(1)}, u32[]{:S(2)}, u32[]{:S(2)}) collective-permute-start(bf16[128,768]{1,0:T(8,128)(2,1)S(1)} %get-tuple-element.65), channel_id=1, source_target_pairs={{0,3},{1,0},{2,1},{3,2},{4,7},{5,4},{6,5},{7,6},{8,11},{9,8},{10,9... | collective-permute-start | bytes 589832 | tf_op jit(solution)/shard_map/ppermute | solution.py:625
  60.9 1.6 %collective-permute-start.20 = (bf16[4,128,128]{2,1,0:T(8,128)(2,1)S(1)}, bf16[4,128,128]{2,1,0:T(8,128)(2,1)S(1)}, u32[]{:S(2)}, u32[]{:S(2)}) collective-permute-start(bf16[4,128,128]{2,1,0:T(8,128)(2,1)S(1)} %get-tuple-element.67), channel_id=1, source_target_pairs={{0,4},{4,0},{8,12},{12,8},{16,20},{20,16},{24,28},{28,24},{32,36},... | collective-permute-start | bytes 393224 | tf_op jit(solution)/shard_map/ppermute | solution.py:634
  62.5 7.6 %collective-permute-start.23 = (bf16[4,128,128]{2,1,0:T(8,128)(2,1)S(1)}, bf16[4,128,128]{2,1,0:T(8,128)(2,1)S(1)}, u32[]{:S(2)}, u32[]{:S(2)}) collective-permute-start(bf16[4,128,128]{2,1,0:T(8,128)(2,1)S(1)} %shard_map.141.unread), channel_id=1, source_target_pairs={{0,8},{4,12},{8,16},{12,20},{16,24},{20,28},{24,0},{28,4},{32,40},... | collective-permute-start | bytes 393224 | tf_op jit(solution)/shard_map/ppermute | solution.py:655
  63.1 7.0 %collective-permute-start.24 = (bf16[4,128,128]{2,1,0:T(8,128)(2,1)S(1)}, bf16[4,128,128]{2,1,0:T(8,128)(2,1)S(1)}, u32[]{:S(2)}, u32[]{:S(2)}) collective-permute-start(bf16[4,128,128]{2,1,0:T(8,128)(2,1)S(1)} %shard_map.141.unread), channel_id=1, source_target_pairs={{0,24},{4,28},{8,0},{12,4},{16,8},{20,12},{24,16},{28,20},{32,56},... | collective-permute-start | bytes 393224 | tf_op jit(solution)/shard_map/ppermute | solution.py:655
  65.2 5.4 %collective-permute-start.25 = (bf16[4,128,128]{2,1,0:T(8,128)(2,1)S(1)}, bf16[4,128,128]{2,1,0:T(8,128)(2,1)S(1)}, u32[]{:S(2)}, u32[]{:S(2)}) collective-permute-start(bf16[4,128,128]{2,1,0:T(8,128)(2,1)S(1)} %shard_map.141.unread), channel_id=1, source_target_pairs={{0,16},{4,20},{8,24},{12,28},{16,0},{20,4},{24,8},{28,12},{32,48},... | collective-permute-start | bytes 393224 | tf_op jit(solution)/shard_map/ppermute | solution.py:655
  67.4 15.5 %collective-permute-start.21 = (bf16[256,768]{1,0:T(8,128)(2,1)S(1)}, bf16[256,768]{1,0:T(8,128)(2,1)S(1)}, u32[]{:S(2)}, u32[]{:S(2)}) collective-permute-start(bf16[256,768]{1,0:T(8,128)(2,1)S(1)} %get-tuple-element.69), channel_id=1, source_target_pairs={{0,1},{1,2},{2,3},{3,0},{4,5},{5,6},{6,7},{7,4},{8,9},{9,10},{10,1... | collective-permute-start | bytes 1179656 | tf_op jit(solution)/shard_map/ppermute | solution.py:625
  67.4 15.4 %collective-permute-start.22 = (bf16[256,768]{1,0:T(8,128)(2,1)S(1)}, bf16[256,768]{1,0:T(8,128)(2,1)S(1)}, u32[]{:S(2)}, u32[]{:S(2)}) collective-permute-start(bf16[256,768]{1,0:T(8,128)(2,1)S(1)} %get-tuple-element.70), channel_id=1, source_target_pairs={{0,3},{1,0},{2,1},{3,2},{4,7},{5,4},{6,5},{7,6},{8,11},{9,8},{10,9... | collective-permute-start | bytes 1179656 | tf_op jit(solution)/shard_map/ppermute | solution.py:625
  70.7 8.5 %collective-permute-start.26 = (bf16[4,128,128]{2,1,0:T(8,128)(2,1)S(1)}, bf16[4,128,128]{2,1,0:T(8,128)(2,1)S(1)}, u32[]{:S(2)}, u32[]{:S(2)}) collective-permute-start(bf16[4,128,128]{2,1,0:T(8,128)(2,1)S(1)} %get-tuple-element.75.unread), channel_id=1, source_target_pairs={{0,32},{4,36},{8,40},{12,44},{16,48},{20,52},{24,56},{28,60},{32,6... | collective-permute-start | bytes 393224 | tf_op jit(solution)/shard_map/ppermute | solution.py:655
  71.2 8.0 %collective-permute-start.27 = (bf16[4,128,128]{2,1,0:T(8,128)(2,1)S(1)}, bf16[4,128,128]{2,1,0:T(8,128)(2,1)S(1)}, u32[]{:S(2)}, u32[]{:S(2)}) collective-permute-start(bf16[4,128,128]{2,1,0:T(8,128)(2,1)S(1)} %get-tuple-element.75.unread), channel_id=1, source_target_pairs={{0,96},{4,100},{8,104},{12,108},{16,112},{20,116},{24,120},{28,124... | collective-permute-start | bytes 393224 | tf_op jit(solution)/shard_map/ppermute | solution.py:655
  73.5 6.5 %collective-permute-start.28 = (bf16[4,128,128]{2,1,0:T(8,128)(2,1)S(1)}, bf16[4,128,128]{2,1,0:T(8,128)(2,1)S(1)}, u32[]{:S(2)}, u32[]{:S(2)}) collective-permute-start(bf16[4,128,128]{2,1,0:T(8,128)(2,1)S(1)} %get-tuple-element.75.unread), channel_id=1, source_target_pairs={{0,64},{4,68},{8,72},{12,76},{16,80},{20,84},{24,88},{28,92},{32,9... | collective-permute-start | bytes 393224 | tf_op jit(solution)/shard_map/ppermute | solution.py:655
  80.1 3.7 %collective-permute-start.29 = (bf16[4,128,128]{2,1,0:T(8,128)(2,1)S(1)}, bf16[4,128,128]{2,1,0:T(8,128)(2,1)S(1)}, u32[]{:S(2)}, u32[]{:S(2)}) collective-permute-start(bf16[4,128,128]{2,1,0:T(8,128)(2,1)S(1)} %get-tuple-element.80), channel_id=1, source_target_pairs={{0,4},{4,0},{8,12},{12,8},{16,20},{20,16},{24,28},{28,24},{32,36},... | collective-permute-start | bytes 393224 | tf_op jit(solution)/shard_map/ppermute | solution.py:634
  84.7 4.8 %collective-permute-start.30 = (bf16[256,64]{1,0:T(8,128)(2,1)S(1)}, bf16[256,64]{1,0:T(8,128)(2,1)S(1)}, u32[]{:S(2)}, u32[]{:S(2)}) collective-permute-start(bf16[256,64]{1,0:T(8,128)(2,1)S(1)} %get-tuple-element.85.back0), channel_id=1, source_target_pairs={{0,2},{1,3},{2,0},{3,1},{4,6},{5,7},{6,4},{7,5},{8,10},{9,11},{10,... | collective-permute-start | bytes 98312 | tf_op jit(solution)/shard_map/ppermute | solution.py:625
  84.7 8.3 %collective-permute-start.31 = (bf16[256,64]{1,0:T(8,128)(2,1)S(1)}, bf16[256,64]{1,0:T(8,128)(2,1)S(1)}, u32[]{:S(2)}, u32[]{:S(2)}) collective-permute-start(bf16[256,64]{1,0:T(8,128)(2,1)S(1)} %get-tuple-element.85.back0), channel_id=1, source_target_pairs={{0,1},{1,2},{2,3},{3,0},{4,5},{5,6},{6,7},{7,4},{8,9},{9,10},{10,1... | collective-permute-start | bytes 98312 | tf_op jit(solution)/shard_map/ppermute | solution.py:625
  85.6 7.4 %collective-permute-start.32 = (bf16[256,64]{1,0:T(8,128)(2,1)S(1)}, bf16[256,64]{1,0:T(8,128)(2,1)S(1)}, u32[]{:S(2)}, u32[]{:S(2)}) collective-permute-start(bf16[256,64]{1,0:T(8,128)(2,1)S(1)} %get-tuple-element.85.back0), channel_id=1, source_target_pairs={{0,3},{1,0},{2,1},{3,2},{4,7},{5,4},{6,5},{7,6},{8,11},{9,8},{10,9... | collective-permute-start | bytes 98312 | tf_op jit(solution)/shard_map/ppermute | solution.py:625
  91.5 15.5 %collective-permute-start.37 = (bf16[256,768]{1,0:T(8,128)(2,1)S(1)}, bf16[256,768]{1,0:T(8,128)(2,1)S(1)}, u32[]{:S(2)}, u32[]{:S(2)}) collective-permute-start(bf16[256,768]{1,0:T(8,128)(2,1)S(1)} %shard_map.149.unread), channel_id=1, source_target_pairs={{0,2},{1,3},{2,0},{3,1},{4,6},{5,7},{6,4},{7,5},{8,10},{9,11},{10,... | collective-permute-start | bytes 1179656 | tf_op jit(solution)/shard_map/ppermute | solution.py:625
  93.5 2.7 %collective-permute-start.33 = (bf16[28,16,128]{2,1,0:T(8,128)(2,1)S(1)}, bf16[28,16,128]{2,1,0:T(8,128)(2,1)S(1)}, u32[]{:S(2)}, u32[]{:S(2)}) collective-permute-start(bf16[28,16,128]{2,1,0:T(8,128)(2,1)S(1)} %get-tuple-element.89), channel_id=1, source_target_pairs={{0,4},{4,0},{8,12},{12,8},{16,20},{20,16},{24,28},{28,24},{32,36},... | collective-permute-start | bytes 344072 | tf_op jit(solution)/shard_map/ppermute | solution.py:634
  96.2 5.7 %collective-permute-start.34 = (bf16[28,16,128]{2,1,0:T(8,128)(2,1)S(1)}, bf16[28,16,128]{2,1,0:T(8,128)(2,1)S(1)}, u32[]{:S(2)}, u32[]{:S(2)}) collective-permute-start(bf16[28,16,128]{2,1,0:T(8,128)(2,1)S(1)} %shard_map.153), channel_id=1, source_target_pairs={{0,8},{4,12},{8,16},{12,20},{16,24},{20,28},{24,0},{28,4},{32,40},... | collective-permute-start | bytes 344072 | tf_op jit(solution)/shard_map/ppermute | solution.py:655
  97.2 22.1 %collective-permute-start.38 = (bf16[256,768]{1,0:T(8,128)(2,1)S(1)}, bf16[256,768]{1,0:T(8,128)(2,1)S(1)}, u32[]{:S(2)}, u32[]{:S(2)}) collective-permute-start(bf16[256,768]{1,0:T(8,128)(2,1)S(1)} %shard_map.150.unread), channel_id=1, source_target_pairs={{0,1},{1,2},{2,3},{3,0},{4,5},{5,6},{6,7},{7,4},{8,9},{9,10},{10,1... | collective-permute-start | bytes 1179656 | tf_op jit(solution)/shard_map/ppermute | solution.py:625
  97.4 21.9 %collective-permute-start.39 = (bf16[256,768]{1,0:T(8,128)(2,1)S(1)}, bf16[256,768]{1,0:T(8,128)(2,1)S(1)}, u32[]{:S(2)}, u32[]{:S(2)}) collective-permute-start(bf16[256,768]{1,0:T(8,128)(2,1)S(1)} %shard_map.151.refs_0_), channel_id=1, source_target_pairs={{0,3},{1,0},{2,1},{3,2},{4,7},{5,4},{6,5},{7,6},{8,11},{9,8},{10,9... | collective-permute-start | bytes 1179656 | tf_op jit(solution)/shard_map/ppermute | solution.py:625
  99.8 3.9 %collective-permute-start.35 = (bf16[28,16,128]{2,1,0:T(8,128)(2,1)S(1)}, bf16[28,16,128]{2,1,0:T(8,128)(2,1)S(1)}, u32[]{:S(2)}, u32[]{:S(2)}) collective-permute-start(bf16[28,16,128]{2,1,0:T(8,128)(2,1)S(1)} %shard_map.153), channel_id=1, source_target_pairs={{0,24},{4,28},{8,0},{12,4},{16,8},{20,12},{24,16},{28,20},{32,56},... | collective-permute-start | bytes 344072 | tf_op jit(solution)/shard_map/ppermute | solution.py:655
  101.9 5.1 %collective-permute-start.36 = (bf16[28,16,128]{2,1,0:T(8,128)(2,1)S(1)}, bf16[28,16,128]{2,1,0:T(8,128)(2,1)S(1)}, u32[]{:S(2)}, u32[]{:S(2)}) collective-permute-start(bf16[28,16,128]{2,1,0:T(8,128)(2,1)S(1)} %shard_map.153), channel_id=1, source_target_pairs={{0,16},{4,20},{8,24},{12,28},{16,0},{20,4},{24,8},{28,12},{32,48},... | collective-permute-start | bytes 344072 | tf_op jit(solution)/shard_map/ppermute | solution.py:655
  107.1 5.2 %collective-permute-start.40 = (bf16[28,16,128]{2,1,0:T(8,128)(2,1)S(1)}, bf16[28,16,128]{2,1,0:T(8,128)(2,1)S(1)}, u32[]{:S(2)}, u32[]{:S(2)}) collective-permute-start(bf16[28,16,128]{2,1,0:T(8,128)(2,1)S(1)} %shard_map.154.unread.mine_ref), channel_id=1, source_target_pairs={{0,32},{4,36},{8,40},{12,44},{16,48},{20,52},{24,56},{28,60},{32,6... | collective-permute-start | bytes 344072 | tf_op jit(solution)/shard_map/ppermute | solution.py:655
  107.2 5.6 %collective-permute-start.41 = (bf16[28,16,128]{2,1,0:T(8,128)(2,1)S(1)}, bf16[28,16,128]{2,1,0:T(8,128)(2,1)S(1)}, u32[]{:S(2)}, u32[]{:S(2)}) collective-permute-start(bf16[28,16,128]{2,1,0:T(8,128)(2,1)S(1)} %shard_map.154.unread.mine_ref), channel_id=1, source_target_pairs={{0,96},{4,100},{8,104},{12,108},{16,112},{20,116},{24,120},{28,124... | collective-permute-start | bytes 344072 | tf_op jit(solution)/shard_map/ppermute | solution.py:655
  109.9 6.3 %collective-permute-start.42 = (bf16[28,16,128]{2,1,0:T(8,128)(2,1)S(1)}, bf16[28,16,128]{2,1,0:T(8,128)(2,1)S(1)}, u32[]{:S(2)}, u32[]{:S(2)}) collective-permute-start(bf16[28,16,128]{2,1,0:T(8,128)(2,1)S(1)} %shard_map.154.unread.mine_ref), channel_id=1, source_target_pairs={{0,64},{4,68},{8,72},{12,76},{16,80},{20,84},{24,88},{28,92},{32,9... | collective-permute-start | bytes 344072 | tf_op jit(solution)/shard_map/ppermute | solution.py:655
  116.2 4.2 %collective-permute-start.43 = (bf16[28,16,128]{2,1,0:T(8,128)(2,1)S(1)}, bf16[28,16,128]{2,1,0:T(8,128)(2,1)S(1)}, u32[]{:S(2)}, u32[]{:S(2)}) collective-permute-start(bf16[28,16,128]{2,1,0:T(8,128)(2,1)S(1)} %shard_map.158.own_ref), channel_id=1, source_target_pairs={{0,4},{4,0},{8,12},{12,8},{16,20},{20,16},{24,28},{28,24},{32,36},... | collective-permute-start | bytes 344072 | tf_op jit(solution)/shard_map/ppermute | solution.py:634
  (12 other events, 51.6 us)

commit v2 on v1

--- a/solution.py
+++ b/solution.py
@@ -201,32 +201,52 @@
     )(*halves, total, *smalls, up, weight)
 
 
-def attended_gradient_kernel(
-    cot0, cot1, cot3, top_ref, bottom_ref, down_ref, weight_ref, out_ref, back_ref, buffer
-):
+def gradient_near_kernel(cot0, cot1, cot3, unread, weight_ref, out_ref, back_ref):
     width = cot0.shape[1] - LANES
-    joined(buffer, top_ref, bottom_ref)
-    refs = ((0, cot0), (1, cot1), (3, cot3), (2, buffer))
-    back = sum(ref[:, width:].astype(f32) for _, ref in refs).astype(bf16)[:, :RANK]
-    back_ref[...] = back
-    total = adapter_scale * mm(back, down_ref[...])
+    refs = ((0, cot0), (1, cot1), (3, cot3))
+    back_ref[...] = sum(ref[:, width : width + RANK].astype(f32) for _, ref in refs)
+    total = jnp.zeros(out_ref.shape, f32)
     for by, ref in refs:
         chunk = pl.ds(pl.multiple_of(member(-by) * width, width), width)
         total = total + mm(ref[:, :width], weight_ref[:, chunk], NT)
     out_ref[...] = total
 
 
-def attended_gradient(cots, down_out, weight):
-    rows, wide = cots[0].shape
+def gradient_near(cots, weight, unread):
+    rows = cots[0].shape[0]
     cols, full = weight.shape
     return call(
-        attended_gradient_kernel,
-        [IN_VMEM] * 7,
+        gradient_near_kernel,
+        [IN_VMEM] * 3 + [UNREAD, IN_VMEM],
+        [struct((rows, cols), f32), struct((rows, RANK), f32)],
+        3 * rows * full * cols // 2,
+        2 * full * cols,
+    )(*cots, unread, weight)
+
+
+def gradient_far_kernel(
+    top_ref, bottom_ref, near_ref, part_ref, down_ref, weight_ref, out_ref, back_ref, buffer
+):
+    width = buffer.shape[1] - LANES
+    joined(buffer, top_ref, bottom_ref)
+    back = (part_ref[...] + buffer[:, width : width + RANK].astype(f32)).astype(bf16)
+    back_ref[...] = back
+    chunk = pl.ds(pl.multiple_of(member(-2) * width, width), width)
+    total = near_ref[...] + mm(buffer[:, :width], weight_ref[:, chunk], NT)
+    out_ref[...] = total + adapter_scale * mm(back, down_ref[...])
+
+
+def gradient_far(halves, near, part, down_out, weight):
+    rows, cols = near.shape
+    wide = halves[0].shape[1]
+    return call(
+        gradient_far_kernel,
+        [IN_VMEM] * 6,
         [struct((rows, cols), f32), struct((rows, RANK), bf16)],
-        2 * rows * full * cols,
-        2 * full * cols,
+        2 * rows * wide * cols,
+        2 * wide * cols,
         [pltpu.VMEM((rows, wide), bf16)],
-    )(*cots, down_out, weight)
+    )(*halves, near, part, down_out, weight)
 
 
 def lower_mask(rows):
@@ -398,57 +418,35 @@
     return mm(att_ref[...], weight_ref[:, chunk])
 
 
-def output_far_kernel(att_ref, weight_ref, top_ref, bottom_ref):
-    half, width = top_ref.shape
-    part = output_product(2, att_ref, weight_ref, width).astype(bf16)
-    top_ref[...] = part[:half]
-    bottom_ref[...] = part[half:]
-
-
-def output_far(att, weight, width):
+def output_piece_kernel(shifts, att_ref, weight_ref, *refs):
+    outs = refs[len(refs) - len(shifts) :]
+    for by, out_ref in zip(shifts, outs):
+        part = output_product(by, att_ref, weight_ref, out_ref.shape[1])
+        out_ref[...] = part.astype(out_ref.dtype)
+
+
+def output_pieces(shifts, att, weight, width, unread=()):
     rows, cols = att.shape
     return call(
-        output_far_kernel,
-        [IN_VMEM] * 2,
-        [struct((rows // 2, width), bf16)] * 2,
-        2 * rows * cols * width,
-        2 * cols * width,
-    )(att, weight)
-
-
-def output_near_kernel(
-    att_ref, relay_top, relay_bottom, weight_ref, unread, own_ref, one_ref, three_ref
-):
-    half, width = relay_top.shape
-    own_ref[...] = output_product(0, att_ref, weight_ref, width)
-    one = output_product(1, att_ref, weight_ref, width)
-    one_ref[:half] = (one[:half] + relay_top[...].astype(f32)).astype(bf16)
-    one_ref[half:] = one[half:].astype(bf16)
-    three = output_product(3, att_ref, weight_ref, width)
-    three_ref[:half] = three[:half].astype(bf16)
-    three_ref[half:] = (three[half:] + relay_bottom[...].astype(f32)).astype(bf16)
-
-
-def output_near(att, relays, weight, unread):
-    rows, cols = att.shape
-    width = relays[0].shape[1]
-    return call(
-        output_near_kernel,
+        functools.partial(output_piece_kernel, shifts),
+        [IN_VMEM] * 2 + [UNREAD] * len(unread),
+        [struct((rows, width), bf16 if by else f32) for by in shifts],
+        2 * rows * cols * width * len(shifts),
+        2 * cols * width * len(shifts),
+    )(att, weight, *unread)
+
+
+def output_merge_kernel(own_ref, two_ref, one_ref, three_ref, unread, out_ref):
+    total = own_ref[...]
+    for ref in (two_ref, one_ref, three_ref):
+        total = total + ref[...].astype(f32)
+    out_ref[...] = total
+
+
+def output_merge(own, parts, unread):
+    return call(
+        output_merge_kernel,
         [IN_VMEM] * 4 + [UNREAD],
-        [struct((rows, width), f32)] + [struct((rows, width), bf16)] * 2,
-        6 * rows * cols * width,
-        6 * cols * width,
-    )(att, *relays, weight, unread)
-
-
-def output_merge_kernel(own_ref, one_ref, three_ref, unread, out_ref):
-    out_ref[...] = own_ref[...] + one_ref[...].astype(f32) + three_ref[...].astype(f32)
-
-
-def output_merge(own, parts, unread):
-    return call(
-        output_merge_kernel,
-        [IN_VMEM] * 3 + [UNREAD],
         struct(own.shape, f32),
         2 * own.size,
         12 * own.size,
@@ -788,18 +786,20 @@
     cot_top, cot_bottom = halves(cot_one, cot_three, arrived[0])
     cot_two = shift(cot_top, 1), shift(cot_bottom, 3)
     middle = scan_row(mine, got, arrived, False, [raw, cot_top])
-    grad, back_mid = attended_gradient(
-        [cot_own, cot_one, cot_three, *cot_two], down_out_t, output_weight
-    )
-    held = scan_rest(middle, from_axis(middle[2], "z"), False, [])
+    near_grad, back_near = gradient_near(
+        [cot_own, cot_one, cot_three], output_weight, middle[2]
+    )
+    grad, back_mid = gradient_far(cot_two, near_grad, back_near, down_out_t, output_weight)
+    held = scan_rest(middle, from_axis(middle[2], "z"), False, [near_grad])
 
     attended, d_raw, mine, given = forward_heads(qkv, raw, held, grad)
     pair, got = scan_pair(mine, given)
-    far_top, far_bottom = output_far(attended, output_weight, width)
-    relays = shift(far_top, 1), shift(far_bottom, 3)
-    out_own, out_one, out_three = output_near(attended, relays, output_weight, pair)
-    out_got = shift(out_one, 1), shift(out_three, 3)
-    middle = scan_row(mine, got, from_axis(pair, "x"), True, [out_own])
+    (out_two,) = output_pieces((2,), attended, output_weight, width)
+    out_own, out_one, out_three = output_pieces(
+        (0, 1, 3), attended, output_weight, width, [pair]
+    )
+    out_got = [shift(part, by) for part, by in zip((out_two, out_one, out_three), (2, 1, 3))]
+    middle = scan_row(mine, got, from_axis(pair, "x"), True, [out_own, out_got[0]])
     dq, dk_within, dv_within, back_q, mid, early = within_block(
         qkv,
         scores,

time: 121 us -> 121 us (level)
  starting transfers between devices: 62.6 us -> 61 us
    ppermute x20 -> x19, starting transfers between devices: 26 us -> 24.4 us  [shift(): return lax.ppermute(array, 'head', [(i, (i + by) % n) for i in range(n)])]
    pallas_call x4 -> x5, Pallas kernels: 4.08 us -> 4.42 us  [the longest x2 2.04 us: output_pieces(): call(functools.partial(output_piece_kernel, shifts), [IN_VMEM] * 2 + [UNR...]
    ppermute x20 -> x19, waiting for transfers between devices: 7.04 us -> 6.99 us  [shift(): return lax.ppermute(array, 'head', [(i, (i + by) % n) for i in range(n)])]
  transfers between devices with their start and end apart: 44 -> 43, of which waited for: 19 -> 20; matrix products, arithmetic and copies ran while one was open for 0% -> 0% of each run, Pallas kernels for 20% -> 20%
where the time goes in v2:
time: 121 us
  starting transfers between devices  61 us (50%)
  waiting for transfers between devices  28.3 us (23%)
  Pallas kernels  27.9 us (23%)
  local copies, waits for them, and re-layouts  2.32 us (2%)
    ppermute x19, starting transfers between devices, shift(): return lax.ppermute(array, 'head', [(i, (i + by) % n) for i in range(n)])  24.4 us
    ppermute x18, starting transfers between devices, along(): return lax.ppermute(array, 'ctx', pairs)  22 us
    ppermute x18, waiting for transfers between devices, along(): return lax.ppermute(array, 'ctx', pairs)  17.4 us
    ppermute x6, starting transfers between devices, swap_cores(): return lax.ppermute(array, 'ctx', [(i, i ^ 1) for i in range(n)])  14.7 us
    ppermute x19, waiting for transfers between devices, shift(): return lax.ppermute(array, 'head', [(i, (i + by) % n) for i in range(n)])  6.99 us
    pallas_call x4, Pallas kernels, input_call(): call(kernel, [IN_VMEM] * 3 + [UNREAD] * len(more), out, 4 * rows * cols *...  4.06 us
    ppermute x6, waiting for transfers between devices, swap_cores(): return lax.ppermute(array, 'ctx', [(i, i ^ 1) for i in range(n)])  3.93 us
    pallas_call x2, Pallas kernels, project_next(): call(functools.partial(project_next_kernel, by), [IN_VMEM] * 4, struct((3...  3.18 us
  transfers between devices with their start and end apart: 43, of which 20 were waited for; matrix products, arithmetic and copies ran while one was open for 0% of the time, Pallas kernels for 20%

profile of v2, /device:TPU:1, one launch (start us, length us, event | category | flops | bytes accessed | tf_op | source)
XLA Modules:
  0.0 120.6 jit_solution(2238623699817631707)
XLA Ops:
  0.7 1.1 copy-done.1
  1.8 1.1 copy-done.7
  3.2 2.2 %collective-permute-start = (bf16[128,1024]{1,0:T(8,128)(2,1)S(1)}, bf16[128,1024]{1,0:T(8,128)(2,1)S(1)}, u32[]{:S(2)}, u32[]{:S(2)}) collective-permute-start(bf16[128,1024]{1,0:T(8,128)(2,1)S(1)} %get-tuple-element.50.own_ref), channel_id=1, source_target_pairs={{0,1},{1,2},{2,3},{3,0},{4,5},{5,6},{6,7},{7,4},{8,9},{9,10},{10,1... | collective-permute-start | bytes 786440 | tf_op jit(solution)/shard_map/ppermute | solution.py:623
  5.4 1.5 %collective-permute-start.2 = (bf16[128,1024]{1,0:T(8,128)(2,1)S(1)}, bf16[128,1024]{1,0:T(8,128)(2,1)S(1)}, u32[]{:S(2)}, u32[]{:S(2)}) collective-permute-start(bf16[128,1024]{1,0:T(8,128)(2,1)S(1)} %get-tuple-element.51), channel_id=1, source_target_pairs={{0,3},{1,0},{2,1},{3,2},{4,7},{5,4},{6,5},{7,6},{8,11},{9,8},{10,9... | collective-permute-start | bytes 786440 | tf_op jit(solution)/shard_map/ppermute | solution.py:623
  7.0 2.7 %collective-permute-start.4 = (bf16[128,1024]{1,0:T(8,128)(2,1)S(1)}, bf16[128,1024]{1,0:T(8,128)(2,1)S(1)}, u32[]{:S(2)}, u32[]{:S(2)}) collective-permute-start(bf16[128,1024]{1,0:T(8,128)(2,1)S(1)} %get-tuple-element.50.own_ref), channel_id=1, source_target_pairs={{0,3},{1,0},{2,1},{3,2},{4,7},{5,4},{6,5},{7,6},{8,11},{9,8},{10,9... | collective-permute-start | bytes 786440 | tf_op jit(solution)/shard_map/ppermute | solution.py:623
  9.7 1.4 %shard_map.128.sum_ref = f32[3,256,1024]{2,1,0:T(8,128)S(1)} custom-call(bf16[256,768]{1,0:T(8,128)(2,1)S(1)} %copy-done.1, bf16[3,3072,1024]{2,1,0:T(8,128)(2,1)S(1)} %bitcast.7), custom_call_target="tpu_custom_call" | custom-call | flops 1207959552 | bytes 4718592 | tf_op jit(solution)/shard_map/pallas_call | solution.py:99
  11.1 1.7 %collective-permute-done.top_ref.one_ref = bf16[128,1024]{1,0:T(8,128)(2,1)S(1)} collective-permute-done((bf16[128,1024]{1,0:T(8,128)(2,1)S(1)}, bf16[128,1024]{1,0:T(8,128)(2,1)S(1)}, u32[]{:S(2)}, u32[]{:S(2)}) %collective-permute-start) | collective-permute-done | bytes 262176 | tf_op jit(solution)/shard_map/ppermute | solution.py:623
  12.8 2.7 %collective-permute-start.3 = (bf16[128,1024]{1,0:T(8,128)(2,1)S(1)}, bf16[128,1024]{1,0:T(8,128)(2,1)S(1)}, u32[]{:S(2)}, u32[]{:S(2)}) collective-permute-start(bf16[128,1024]{1,0:T(8,128)(2,1)S(1)} %collective-permute-done.2.bottom_ref), channel_id=1, source_target_pairs={{0,3},{1,0},{2,1},{3,2},{4,7},{5,4},{6,5},{7,6},{8,11},{9,8},{10,9... | collective-permute-start | bytes 786440 | tf_op jit(solution)/shard_map/ppermute | solution.py:623
  15.4 2.9 %collective-permute-done.5.bottom_ref = bf16[128,1024]{1,0:T(8,128)(2,1)S(1)} collective-permute-done((bf16[128,1024]{1,0:T(8,128)(2,1)S(1)}, bf16[128,1024]{1,0:T(8,128)(2,1)S(1)}, u32[]{:S(2)}, u32[]{:S(2)}) %collective-permute-start.5) | collective-permute-done | bytes 262176 | tf_op jit(solution)/shard_map/ppermute | solution.py:623
  18.4 1.6 %shard_map.129.sum_ref = f32[3,256,1024]{2,1,0:T(8,128)S(1)} custom-call(bf16[128,1024]{1,0:T(8,128)(2,1)S(1)} %collective-permute-done.top_ref.one_ref, bf16[128,1024]{1,0:T(8,128)(2,1)S(1)} %collective-permute-done.5.bottom_ref, f32[3,256,1024]{2,1,0:T(8,128)S(1)} %shard_map.128.sum_ref, ...), custom_call_target="tpu_custom_call", output_to_operand_aliasing={{}: (2, {})} | custom-call | flops 1207959552 | bytes 4718592 | tf_op jit(solution)/shard_map/pallas_call | solution.py:123
  20.0 1.6 %shard_map.130.sum_ref.unread = f32[3,256,1024]{2,1,0:T(8,128)S(1)} custom-call(bf16[128,1024]{1,0:T(8,128)(2,1)S(1)} %collective-permute-done.4.top_ref.three_ref, bf16[128,1024]{1,0:T(8,128)(2,1)S(1)} %collective-permute-done.2.bottom_ref, f32[3,256,1024]{2,1,0:T(8,128)S(1)} %shard_map.129.sum_ref, ...), custom_call_target="tpu_custom_call", output_to_operand_aliasing={{}: (2, {})} | custom-call | flops 1207959552 | bytes 4718592 | tf_op jit(solution)/shard_map/pallas_call | solution.py:123
  22.0 2.7 %collective-permute-start.11 = (bf16[256,896]{1,0:T(8,128)(2,1)S(1)}, bf16[256,896]{1,0:T(8,128)(2,1)S(1)}, u32[]{:S(2)}, u32[]{:S(2)}) collective-permute-start(bf16[256,896]{1,0:T(8,128)(2,1)S(1)} %shard_map.134.cot0), channel_id=1, source_target_pairs={{0,3},{1,0},{2,1},{3,2},{4,7},{5,4},{6,5},{7,6},{8,11},{9,8},{10,9... | collective-permute-start | bytes 1376264 | tf_op jit(solution)/shard_map/ppermute | solution.py:623
  24.7 2.1 %shard_map.131 = (bf16[3,256,1024]{2,1,0:T(8,128)(2,1)S(1)}, f32[4,128,128]{2,1,0:T(8,128)S(1)}, bf16[4,128,128]{2,1,0:T(8,128)(2,1)S(1)}, bf16[256,48]{1,0:T(8,128)(2,1)S(1)}) custom-call(bf16[128,1024]{1,0:T(8,128)(2,1)S(1)} %collective-permute-done.1.top_ref, bf16[128,1024]{1,0:T(8,128)(2,1)S(1)} %collective-permute-done.3.bottom_ref, ...), custom_call_target="tpu_custom_call" | custom-call | flops 1207959552 | bytes 4718592 | tf_op jit(solution)/shard_map/pallas_call | solution.py:189
  26.8 3.0 %collective-permute-start.6 = (bf16[4,128,128]{2,1,0:T(8,128)(2,1)S(1)}, bf16[4,128,128]{2,1,0:T(8,128)(2,1)S(1)}, u32[]{:S(2)}, u32[]{:S(2)}) collective-permute-start(bf16[4,128,128]{2,1,0:T(8,128)(2,1)S(1)} %get-tuple-element.54), channel_id=1, source_target_pairs={{0,4},{4,0},{8,12},{12,8},{16,20},{20,16},{24,28},{28,24},{32,36},... | collective-permute-start | bytes 393224 | tf_op jit(solution)/shard_map/ppermute | solution.py:632
  30.8 1.4 %collective-permute-start.7 = (bf16[4,128,128]{2,1,0:T(8,128)(2,1)S(1)}, bf16[4,128,128]{2,1,0:T(8,128)(2,1)S(1)}, u32[]{:S(2)}, u32[]{:S(2)}) collective-permute-start(bf16[4,128,128]{2,1,0:T(8,128)(2,1)S(1)} %shard_map.132.unread), channel_id=1, source_target_pairs={{0,8},{4,12},{8,16},{12,20},{16,24},{20,28},{24,0},{28,4},{32,40},... | collective-permute-start | bytes 393224 | tf_op jit(solution)/shard_map/ppermute | solution.py:653
  32.2 1.4 %collective-permute-start.8 = (bf16[4,128,128]{2,1,0:T(8,128)(2,1)S(1)}, bf16[4,128,128]{2,1,0:T(8,128)(2,1)S(1)}, u32[]{:S(2)}, u32[]{:S(2)}) collective-permute-start(bf16[4,128,128]{2,1,0:T(8,128)(2,1)S(1)} %shard_map.132.unread), channel_id=1, source_target_pairs={{0,24},{4,28},{8,0},{12,4},{16,8},{20,12},{24,16},{28,20},{32,56},... | collective-permute-start | bytes 393224 | tf_op jit(solution)/shard_map/ppermute | solution.py:653
  33.6 1.6 %collective-permute-start.9 = (bf16[4,128,128]{2,1,0:T(8,128)(2,1)S(1)}, bf16[4,128,128]{2,1,0:T(8,128)(2,1)S(1)}, u32[]{:S(2)}, u32[]{:S(2)}) collective-permute-start(bf16[4,128,128]{2,1,0:T(8,128)(2,1)S(1)} %shard_map.132.unread), channel_id=1, source_target_pairs={{0,16},{4,20},{8,24},{12,28},{16,0},{20,4},{24,8},{28,12},{32,48},... | collective-permute-start | bytes 393224 | tf_op jit(solution)/shard_map/ppermute | solution.py:653
  35.2 1.6 %collective-permute-done.7.unread.one_ref = bf16[4,128,128]{2,1,0:T(8,128)(2,1)S(1)} collective-permute-done((bf16[4,128,128]{2,1,0:T(8,128)(2,1)S(1)}, bf16[4,128,128]{2,1,0:T(8,128)(2,1)S(1)}, u32[]{:S(2)}, u32[]{:S(2)}) %collective-permute-start.7) | collective-permute-done | bytes 131104 | tf_op jit(solution)/shard_map/ppermute | solution.py:653
  36.9 2.7 %collective-permute-start.17 = (bf16[128,896]{1,0:T(8,128)(2,1)S(1)}, bf16[128,896]{1,0:T(8,128)(2,1)S(1)}, u32[]{:S(2)}, u32[]{:S(2)}) collective-permute-start(bf16[128,896]{1,0:T(8,128)(2,1)S(1)} %get-tuple-element.62), channel_id=1, source_target_pairs={{0,3},{1,0},{2,1},{3,2},{4,7},{5,4},{6,5},{7,6},{8,11},{9,8},{10,9... | collective-permute-start | bytes 688136 | tf_op jit(solution)/shard_map/ppermute | solution.py:623
  40.9 1.9 %collective-permute-start.12 = (bf16[4,128,128]{2,1,0:T(8,128)(2,1)S(1)}, bf16[4,128,128]{2,1,0:T(8,128)(2,1)S(1)}, u32[]{:S(2)}, u32[]{:S(2)}) collective-permute-start(bf16[4,128,128]{2,1,0:T(8,128)(2,1)S(1)} %get-tuple-element.58.unread), channel_id=1, source_target_pairs={{0,32},{4,36},{8,40},{12,44},{16,48},{20,52},{24,56},{28,60},{32,6... | collective-permute-start | bytes 393224 | tf_op jit(solution)/shard_map/ppermute | solution.py:653
  42.8 2.2 %collective-permute-start.13 = (bf16[4,128,128]{2,1,0:T(8,128)(2,1)S(1)}, bf16[4,128,128]{2,1,0:T(8,128)(2,1)S(1)}, u32[]{:S(2)}, u32[]{:S(2)}) collective-permute-start(bf16[4,128,128]{2,1,0:T(8,128)(2,1)S(1)} %get-tuple-element.58.unread), channel_id=1, source_target_pairs={{0,96},{4,100},{8,104},{12,108},{16,112},{20,116},{24,120},{28,124... | collective-permute-start | bytes 393224 | tf_op jit(solution)/shard_map/ppermute | solution.py:653
  45.0 1.2 %collective-permute-start.14 = (bf16[4,128,128]{2,1,0:T(8,128)(2,1)S(1)}, bf16[4,128,128]{2,1,0:T(8,128)(2,1)S(1)}, u32[]{:S(2)}, u32[]{:S(2)}) collective-permute-start(bf16[4,128,128]{2,1,0:T(8,128)(2,1)S(1)} %get-tuple-element.58.unread), channel_id=1, source_target_pairs={{0,64},{4,68},{8,72},{12,76},{16,80},{20,84},{24,88},{28,92},{32,9... | collective-permute-start | bytes 393224 | tf_op jit(solution)/shard_map/ppermute | solution.py:653
  46.2 1.4 %shard_map.137 = (f32[256,1024]{1,0:T(8,128)S(1)}, f32[256,16]{1,0:T(8,128)S(1)}) custom-call(bf16[256,896]{1,0:T(8,128)(2,1)S(1)} %shard_map.134.cot0, bf16[256,896]{1,0:T(8,128)(2,1)S(1)} %collective-permute-done.10.one_ref.cot1, bf16[256,896]{1,0:T(8,128)(2,1)S(1)} %collective-permute-done.11.three_ref.cot3, ...), custom_call_target="tpu_custom_call" | custom-call | flops 1207959552 | bytes 6291456 | tf_op jit(solution)/shard_map/pallas_call | solution.py:218
  47.6 3.8 %collective-permute-done.14.two_ref = bf16[4,128,128]{2,1,0:T(8,128)(2,1)S(1)} collective-permute-done((bf16[4,128,128]{2,1,0:T(8,128)(2,1)S(1)}, bf16[4,128,128]{2,1,0:T(8,128)(2,1)S(1)}, u32[]{:S(2)}, u32[]{:S(2)}) %collective-permute-start.14) | collective-permute-done | bytes 131104 | tf_op jit(solution)/shard_map/ppermute | solution.py:653
  51.6 2.5 %collective-permute-start.15 = (bf16[4,128,128]{2,1,0:T(8,128)(2,1)S(1)}, bf16[4,128,128]{2,1,0:T(8,128)(2,1)S(1)}, u32[]{:S(2)}, u32[]{:S(2)}) collective-permute-start(bf16[4,128,128]{2,1,0:T(8,128)(2,1)S(1)} %get-tuple-element.61), channel_id=1, source_target_pairs={{0,4},{4,0},{8,12},{12,8},{16,20},{20,16},{24,28},{28,24},{32,36},... | collective-permute-start | bytes 393224 | tf_op jit(solution)/shard_map/ppermute | solution.py:632
  55.0 1.3 %shard_map.140 = (bf16[256,1024]{1,0:T(8,128)(2,1)S(1)}, bf16[256,1024]{1,0:T(8,128)(2,1)S(1)}, f32[4,128,128]{2,1,0:T(8,128)S(1)}, bf16[4,128,128]{2,1,0:T(8,128)(2,1)S(1)}) custom-call(bf16[3,256,1024]{2,1,0:T(8,128)(2,1)S(1)} %get-tuple-element.52.qkv_ref, f32[256,1024]{1,0:T(8,128)S(1)} %get-tuple-element.55.refs_0_.raw_ref, ...), custom_call_target="tpu_custom_call" | custom-call | flops 268435456 | bytes 3670016 | tf_op jit(solution)/shard_map/pallas_call | solution.py:330
  60.0 1.9 %collective-permute-start.23 = (bf16[4,128,128]{2,1,0:T(8,128)(2,1)S(1)}, bf16[4,128,128]{2,1,0:T(8,128)(2,1)S(1)}, u32[]{:S(2)}, u32[]{:S(2)}) collective-permute-start(bf16[4,128,128]{2,1,0:T(8,128)(2,1)S(1)} %shard_map.141.refs_0_), channel_id=1, source_target_pairs={{0,24},{4,28},{8,0},{12,4},{16,8},{20,12},{24,16},{28,20},{32,56},... | collective-permute-start | bytes 393224 | tf_op jit(solution)/shard_map/ppermute | solution.py:653
  61.9 1.4 %shard_map.142 = (f32[256,768]{1,0:T(8,128)S(1)}, bf16[256,768]{1,0:T(8,128)(2,1)S(1)}, bf16[256,768]{1,0:T(8,128)(2,1)S(1)}) custom-call(bf16[256,1024]{1,0:T(8,128)(2,1)S(1)} %get-tuple-element.65.att_ref, bf16[1024,3072]{1,0:T(8,128)(2,1)S(1)} %bitcast.9, bf16[4,128,128]{2,1,0:T(8,128)(2,1)S(1)} %shard_map.141.refs_0_), custom_call_target="tpu_custom_call" | custom-call | flops 1207959552 | bytes 4718592 | tf_op jit(solution)/shard_map/pallas_call | solution.py:430
  64.1 1.1 collective-permute-done.22.one_ref
  65.2 1.1 collective-permute-start.21
  66.2 1.3 %collective-permute-done.24.two_ref = bf16[4,128,128]{2,1,0:T(8,128)(2,1)S(1)} collective-permute-done((bf16[4,128,128]{2,1,0:T(8,128)(2,1)S(1)}, bf16[4,128,128]{2,1,0:T(8,128)(2,1)S(1)}, u32[]{:S(2)}, u32[]{:S(2)}) %collective-permute-start.24) | collective-permute-done | bytes 131104 | tf_op jit(solution)/shard_map/ppermute | solution.py:653
  67.5 1.4 %collective-permute-done.19.refs_1_.two_ref = bf16[256,768]{1,0:T(8,128)(2,1)S(1)} collective-permute-done((bf16[256,768]{1,0:T(8,128)(2,1)S(1)}, bf16[256,768]{1,0:T(8,128)(2,1)S(1)}, u32[]{:S(2)}, u32[]{:S(2)}) %collective-permute-start.19) | collective-permute-done | bytes 393248 | tf_op jit(solution)/shard_map/ppermute | solution.py:623
  69.6 2.2 %collective-permute-start.26 = (bf16[4,128,128]{2,1,0:T(8,128)(2,1)S(1)}, bf16[4,128,128]{2,1,0:T(8,128)(2,1)S(1)}, u32[]{:S(2)}, u32[]{:S(2)}) collective-permute-start(bf16[4,128,128]{2,1,0:T(8,128)(2,1)S(1)} %get-tuple-element.75.unread), channel_id=1, source_target_pairs={{0,96},{4,100},{8,104},{12,108},{16,112},{20,116},{24,120},{28,124... | collective-permute-start | bytes 393224 | tf_op jit(solution)/shard_map/ppermute | solution.py:653
  71.9 3.0 %shard_map.145 = (bf16[256,1024]{1,0:T(8,128)(2,1)S(1)}, f32[256,1024]{1,0:T(8,128)S(1)}, f32[256,1024]{1,0:T(8,128)S(1)}, f32[256,16]{1,0:T(8,128)S(1)}, f32[25...) custom-call(bf16[3,256,1024]{2,1,0:T(8,128)(2,1)S(1)} %get-tuple-element.52.qkv_ref, ...), custom_call_target="tpu_custom_call" | custom-call | flops 1073741824 | bytes 4718592 | tf_op jit(solution)/shard_map/pallas_call | solution.py:375
  74.9 1.8 %shard_map.147.refs_0_.dq_ref = f32[4,256,768]{2,1,0:T(8,128)S(1)} custom-call(bf16[256,1024]{1,0:T(8,128)(2,1)S(1)} %get-tuple-element.78.dq_ref, bf16[3,3072,1024]{2,1,0:T(8,128)(2,1)S(1)} %bitcast.7, bf16[4,128,128]{2,1,0:T(8,128)(2,1)S(1)} %get-tuple-element.75.unread), custom_call_target="tpu_custom_call" | custom-call | flops 1610612736 | bytes 6291456 | tf_op jit(solution)/shard_map/pallas_call | solution.py:481
  76.7 1.4 %collective-permute-done.27.two_ref = bf16[4,128,128]{2,1,0:T(8,128)(2,1)S(1)} collective-permute-done((bf16[4,128,128]{2,1,0:T(8,128)(2,1)S(1)}, bf16[4,128,128]{2,1,0:T(8,128)(2,1)S(1)}, u32[]{:S(2)}, u32[]{:S(2)}) %collective-permute-start.27) | collective-permute-done | bytes 131104 | tf_op jit(solution)/shard_map/ppermute | solution.py:653
  78.3 2.8 %collective-permute-start.28 = (bf16[4,128,128]{2,1,0:T(8,128)(2,1)S(1)}, bf16[4,128,128]{2,1,0:T(8,128)(2,1)S(1)}, u32[]{:S(2)}, u32[]{:S(2)}) collective-permute-start(bf16[4,128,128]{2,1,0:T(8,128)(2,1)S(1)} %get-tuple-element.80), channel_id=1, source_target_pairs={{0,4},{4,0},{8,12},{12,8},{16,20},{20,16},{24,28},{28,24},{32,36},... | collective-permute-start | bytes 393224 | tf_op jit(solution)/shard_map/ppermute | solution.py:632
  84.0 2.7 %collective-permute-start.31 = (bf16[256,64]{1,0:T(8,128)(2,1)S(1)}, bf16[256,64]{1,0:T(8,128)(2,1)S(1)}, u32[]{:S(2)}, u32[]{:S(2)}) collective-permute-start(bf16[256,64]{1,0:T(8,128)(2,1)S(1)} %get-tuple-element.85.back0), channel_id=1, source_target_pairs={{0,3},{1,0},{2,1},{3,2},{4,7},{5,4},{6,5},{7,6},{8,11},{9,8},{10,9... | collective-permute-start | bytes 98312 | tf_op jit(solution)/shard_map/ppermute | solution.py:623
  89.6 1.1 collective-permute-start.36
  92.3 2.4 %collective-permute-start.32 = (bf16[28,16,128]{2,1,0:T(8,128)(2,1)S(1)}, bf16[28,16,128]{2,1,0:T(8,128)(2,1)S(1)}, u32[]{:S(2)}, u32[]{:S(2)}) collective-permute-start(bf16[28,16,128]{2,1,0:T(8,128)(2,1)S(1)} %get-tuple-element.89), channel_id=1, source_target_pairs={{0,4},{4,0},{8,12},{12,8},{16,20},{20,16},{24,28},{28,24},{32,36},... | collective-permute-start | bytes 344072 | tf_op jit(solution)/shard_map/ppermute | solution.py:632
  96.6 2.7 %collective-permute-start.38 = (bf16[256,768]{1,0:T(8,128)(2,1)S(1)}, bf16[256,768]{1,0:T(8,128)(2,1)S(1)}, u32[]{:S(2)}, u32[]{:S(2)}) collective-permute-start(bf16[256,768]{1,0:T(8,128)(2,1)S(1)} %shard_map.152.refs_0_), channel_id=1, source_target_pairs={{0,3},{1,0},{2,1},{3,2},{4,7},{5,4},{6,5},{7,6},{8,11},{9,8},{10,9... | collective-permute-start | bytes 1179656 | tf_op jit(solution)/shard_map/ppermute | solution.py:623
  99.3 1.8 %collective-permute-start.34 = (bf16[28,16,128]{2,1,0:T(8,128)(2,1)S(1)}, bf16[28,16,128]{2,1,0:T(8,128)(2,1)S(1)}, u32[]{:S(2)}, u32[]{:S(2)}) collective-permute-start(bf16[28,16,128]{2,1,0:T(8,128)(2,1)S(1)} %shard_map.154), channel_id=1, source_target_pairs={{0,24},{4,28},{8,0},{12,4},{16,8},{20,12},{24,16},{28,20},{32,56},... | collective-permute-start | bytes 344072 | tf_op jit(solution)/shard_map/ppermute | solution.py:653
  102.1 1.1 collective-permute-done.34.refs_2_
  103.2 3.3 %collective-permute-done.35.refs_3_ = bf16[28,16,128]{2,1,0:T(8,128)(2,1)S(1)} collective-permute-done((bf16[28,16,128]{2,1,0:T(8,128)(2,1)S(1)}, bf16[28,16,128]{2,1,0:T(8,128)(2,1)S(1)}, u32[]{:S(2)}, u32[]{:S(2)}) %collective-permute-start.35) | collective-permute-done | bytes 114720 | tf_op jit(solution)/shard_map/ppermute | solution.py:653
  106.6 2.7 %collective-permute-start.40 = (bf16[28,16,128]{2,1,0:T(8,128)(2,1)S(1)}, bf16[28,16,128]{2,1,0:T(8,128)(2,1)S(1)}, u32[]{:S(2)}, u32[]{:S(2)}) collective-permute-start(bf16[28,16,128]{2,1,0:T(8,128)(2,1)S(1)} %shard_map.155.unread.mine_ref), channel_id=1, source_target_pairs={{0,96},{4,100},{8,104},{12,108},{16,112},{20,116},{24,120},{28,124... | collective-permute-start | bytes 344072 | tf_op jit(solution)/shard_map/ppermute | solution.py:653
  112.3 3.0 %collective-permute-done.41.refs_2_ = bf16[28,16,128]{2,1,0:T(8,128)(2,1)S(1)} collective-permute-done((bf16[28,16,128]{2,1,0:T(8,128)(2,1)S(1)}, bf16[28,16,128]{2,1,0:T(8,128)(2,1)S(1)}, u32[]{:S(2)}, u32[]{:S(2)}) %collective-permute-start.41) | collective-permute-done | bytes 114720 | tf_op jit(solution)/shard_map/ppermute | solution.py:653
  115.3 3.4 %collective-permute-start.42 = (bf16[28,16,128]{2,1,0:T(8,128)(2,1)S(1)}, bf16[28,16,128]{2,1,0:T(8,128)(2,1)S(1)}, u32[]{:S(2)}, u32[]{:S(2)}) collective-permute-start(bf16[28,16,128]{2,1,0:T(8,128)(2,1)S(1)} %shard_map.159.own_ref), channel_id=1, source_target_pairs={{0,4},{4,0},{8,12},{12,8},{16,20},{20,16},{24,28},{28,24},{32,36},... | collective-permute-start | bytes 344072 | tf_op jit(solution)/shard_map/ppermute | solution.py:632
  118.7 1.1 shard_map.158
  (106 shorter events, 23.8 us)
Async XLA Ops:
  0.6 9.0 %slice-start = ((s8[18874368]{0:T(1024)(128)(4,1)}), s8[4194304]{0:T(1024)(128)(4,1)S(1)}, s32[]{:S(2)}) async-start(s8[18874368]{0:T(1024)(128)(4,1)} %bitcast.6), calls=%async_computation | async-start | bytes 8388608
  3.2 9.5 %collective-permute-start = (bf16[128,1024]{1,0:T(8,128)(2,1)S(1)}, bf16[128,1024]{1,0:T(8,128)(2,1)S(1)}, u32[]{:S(2)}, u32[]{:S(2)}) collective-permute-start(bf16[128,1024]{1,0:T(8,128)(2,1)S(1)} %get-tuple-element.50.own_ref), channel_id=1, source_target_pairs={{0,1},{1,2},{2,3},{3,0},{4,5},{5,6},{6,7},{7,4},{8,9},{9,10},{10,1... | collective-permute-start | bytes 786440 | tf_op jit(solution)/shard_map/ppermute | solution.py:623
  5.4 7.3 %collective-permute-start.2 = (bf16[128,1024]{1,0:T(8,128)(2,1)S(1)}, bf16[128,1024]{1,0:T(8,128)(2,1)S(1)}, u32[]{:S(2)}, u32[]{:S(2)}) collective-permute-start(bf16[128,1024]{1,0:T(8,128)(2,1)S(1)} %get-tuple-element.51), channel_id=1, source_target_pairs={{0,3},{1,0},{2,1},{3,2},{4,7},{5,4},{6,5},{7,6},{8,11},{9,8},{10,9... | collective-permute-start | bytes 786440 | tf_op jit(solution)/shard_map/ppermute | solution.py:623
  7.0 11.4 %collective-permute-start.5 = (bf16[128,1024]{1,0:T(8,128)(2,1)S(1)}, bf16[128,1024]{1,0:T(8,128)(2,1)S(1)}, u32[]{:S(2)}, u32[]{:S(2)}) collective-permute-start(bf16[128,1024]{1,0:T(8,128)(2,1)S(1)} %get-tuple-element.51), channel_id=1, source_target_pairs={{0,1},{1,2},{2,3},{3,0},{4,5},{5,6},{6,7},{7,4},{8,9},{9,10},{10,1... | collective-permute-start | bytes 786440 | tf_op jit(solution)/shard_map/ppermute | solution.py:623
  7.0 13.0 %collective-permute-start.4 = (bf16[128,1024]{1,0:T(8,128)(2,1)S(1)}, bf16[128,1024]{1,0:T(8,128)(2,1)S(1)}, u32[]{:S(2)}, u32[]{:S(2)}) collective-permute-start(bf16[128,1024]{1,0:T(8,128)(2,1)S(1)} %get-tuple-element.50.own_ref), channel_id=1, source_target_pairs={{0,3},{1,0},{2,1},{3,2},{4,7},{5,4},{6,5},{7,6},{8,11},{9,8},{10,9... | collective-permute-start | bytes 786440 | tf_op jit(solution)/shard_map/ppermute | solution.py:623
  12.7 11.9 %collective-permute-start.1 = (bf16[128,1024]{1,0:T(8,128)(2,1)S(1)}, bf16[128,1024]{1,0:T(8,128)(2,1)S(1)}, u32[]{:S(2)}, u32[]{:S(2)}) collective-permute-start(bf16[128,1024]{1,0:T(8,128)(2,1)S(1)} %collective-permute-done.top_ref.one_ref), channel_id=1, source_target_pairs={{0,1},{1,2},{2,3},{3,0},{4,5},{5,6},{6,7},{7,4},{8,9},{9,10},{10,1... | collective-permute-start | bytes 786440 | tf_op jit(solution)/shard_map/ppermute | solution.py:623
  12.8 11.9 %collective-permute-start.3 = (bf16[128,1024]{1,0:T(8,128)(2,1)S(1)}, bf16[128,1024]{1,0:T(8,128)(2,1)S(1)}, u32[]{:S(2)}, u32[]{:S(2)}) collective-permute-start(bf16[128,1024]{1,0:T(8,128)(2,1)S(1)} %collective-permute-done.2.bottom_ref), channel_id=1, source_target_pairs={{0,3},{1,0},{2,1},{3,2},{4,7},{5,4},{6,5},{7,6},{8,11},{9,8},{10,9... | collective-permute-start | bytes 786440 | tf_op jit(solution)/shard_map/ppermute | solution.py:623
  21.6 24.6 %slice-start.5 = ((s8[6291456]{0:T(1024)(128)(4,1)}), s8[4194304]{0:T(1024)(128)(4,1)S(1)}, s32[]{:S(2)}) async-start(s8[6291456]{0:T(1024)(128)(4,1)} %bitcast.8), calls=%async_computation.5 | async-start | bytes 8388608
  21.9 24.3 %slice-start.6 = ((s8[6291456]{0:T(1024)(128)(4,1)}), s8[2097152]{0:T(1024)(128)(4,1)S(1)}, s32[]{:S(2)}) async-start(s8[6291456]{0:T(1024)(128)(4,1)} %bitcast.8), calls=%async_computation.6 | async-start | bytes 4194304
  21.9 13.3 %collective-permute-start.10 = (bf16[256,896]{1,0:T(8,128)(2,1)S(1)}, bf16[256,896]{1,0:T(8,128)(2,1)S(1)}, u32[]{:S(2)}, u32[]{:S(2)}) collective-permute-start(bf16[256,896]{1,0:T(8,128)(2,1)S(1)} %shard_map.134.cot0), channel_id=1, source_target_pairs={{0,1},{1,2},{2,3},{3,0},{4,5},{5,6},{6,7},{7,4},{8,9},{9,10},{10,1... | collective-permute-start | bytes 1376264 | tf_op jit(solution)/shard_map/ppermute | solution.py:623
  22.0 13.2 %collective-permute-start.11 = (bf16[256,896]{1,0:T(8,128)(2,1)S(1)}, bf16[256,896]{1,0:T(8,128)(2,1)S(1)}, u32[]{:S(2)}, u32[]{:S(2)}) collective-permute-start(bf16[256,896]{1,0:T(8,128)(2,1)S(1)} %shard_map.134.cot0), channel_id=1, source_target_pairs={{0,3},{1,0},{2,1},{3,2},{4,7},{5,4},{6,5},{7,6},{8,11},{9,8},{10,9... | collective-permute-start | bytes 1376264 | tf_op jit(solution)/shard_map/ppermute | solution.py:623
  26.8 4.0 %collective-permute-start.6 = (bf16[4,128,128]{2,1,0:T(8,128)(2,1)S(1)}, bf16[4,128,128]{2,1,0:T(8,128)(2,1)S(1)}, u32[]{:S(2)}, u32[]{:S(2)}) collective-permute-start(bf16[4,128,128]{2,1,0:T(8,128)(2,1)S(1)} %get-tuple-element.54), channel_id=1, source_target_pairs={{0,4},{4,0},{8,12},{12,8},{16,20},{20,16},{24,28},{28,24},{32,36},... | collective-permute-start | bytes 393224 | tf_op jit(solution)/shard_map/ppermute | solution.py:632
  30.8 6.0 %collective-permute-start.7 = (bf16[4,128,128]{2,1,0:T(8,128)(2,1)S(1)}, bf16[4,128,128]{2,1,0:T(8,128)(2,1)S(1)}, u32[]{:S(2)}, u32[]{:S(2)}) collective-permute-start(bf16[4,128,128]{2,1,0:T(8,128)(2,1)S(1)} %shard_map.132.unread), channel_id=1, source_target_pairs={{0,8},{4,12},{8,16},{12,20},{16,24},{20,28},{24,0},{28,4},{32,40},... | collective-permute-start | bytes 393224 | tf_op jit(solution)/shard_map/ppermute | solution.py:653
  32.2 8.3 %collective-permute-start.8 = (bf16[4,128,128]{2,1,0:T(8,128)(2,1)S(1)}, bf16[4,128,128]{2,1,0:T(8,128)(2,1)S(1)}, u32[]{:S(2)}, u32[]{:S(2)}) collective-permute-start(bf16[4,128,128]{2,1,0:T(8,128)(2,1)S(1)} %shard_map.132.unread), channel_id=1, source_target_pairs={{0,24},{4,28},{8,0},{12,4},{16,8},{20,12},{24,16},{28,20},{32,56},... | collective-permute-start | bytes 393224 | tf_op jit(solution)/shard_map/ppermute | solution.py:653
  33.6 7.1 %collective-permute-start.9 = (bf16[4,128,128]{2,1,0:T(8,128)(2,1)S(1)}, bf16[4,128,128]{2,1,0:T(8,128)(2,1)S(1)}, u32[]{:S(2)}, u32[]{:S(2)}) collective-permute-start(bf16[4,128,128]{2,1,0:T(8,128)(2,1)S(1)} %shard_map.132.unread), channel_id=1, source_target_pairs={{0,16},{4,20},{8,24},{12,28},{16,0},{20,4},{24,8},{28,12},{32,48},... | collective-permute-start | bytes 393224 | tf_op jit(solution)/shard_map/ppermute | solution.py:653
  36.9 17.2 %collective-permute-start.16 = (bf16[128,896]{1,0:T(8,128)(2,1)S(1)}, bf16[128,896]{1,0:T(8,128)(2,1)S(1)}, u32[]{:S(2)}, u32[]{:S(2)}) collective-permute-start(bf16[128,896]{1,0:T(8,128)(2,1)S(1)} %get-tuple-element.56.refs_1_), channel_id=1, source_target_pairs={{0,1},{1,2},{2,3},{3,0},{4,5},{5,6},{6,7},{7,4},{8,9},{9,10},{10,1... | collective-permute-start | bytes 688136 | tf_op jit(solution)/shard_map/ppermute | solution.py:623
  36.9 17.1 %collective-permute-start.17 = (bf16[128,896]{1,0:T(8,128)(2,1)S(1)}, bf16[128,896]{1,0:T(8,128)(2,1)S(1)}, u32[]{:S(2)}, u32[]{:S(2)}) collective-permute-start(bf16[128,896]{1,0:T(8,128)(2,1)S(1)} %get-tuple-element.62), channel_id=1, source_target_pairs={{0,3},{1,0},{2,1},{3,2},{4,7},{5,4},{6,5},{7,6},{8,11},{9,8},{10,9... | collective-permute-start | bytes 688136 | tf_op jit(solution)/shard_map/ppermute | solution.py:623
  40.9 13.2 %copy-start.5 = (bf16[1024,16]{0,1:T(8,128)(2,1)S(1)}, bf16[1024,16]{0,1:T(8,128)(2,1)}, u32[]{:S(2)}) copy-start(bf16[1024,16]{0,1:T(8,128)(2,1)} %param.13) | copy-start | bytes 98308
  40.9 6.8 %collective-permute-start.12 = (bf16[4,128,128]{2,1,0:T(8,128)(2,1)S(1)}, bf16[4,128,128]{2,1,0:T(8,128)(2,1)S(1)}, u32[]{:S(2)}, u32[]{:S(2)}) collective-permute-start(bf16[4,128,128]{2,1,0:T(8,128)(2,1)S(1)} %get-tuple-element.58.unread), channel_id=1, source_target_pairs={{0,32},{4,36},{8,40},{12,44},{16,48},{20,52},{24,56},{28,60},{32,6... | collective-permute-start | bytes 393224 | tf_op jit(solution)/shard_map/ppermute | solution.py:653
  42.8 4.9 %collective-permute-start.13 = (bf16[4,128,128]{2,1,0:T(8,128)(2,1)S(1)}, bf16[4,128,128]{2,1,0:T(8,128)(2,1)S(1)}, u32[]{:S(2)}, u32[]{:S(2)}) collective-permute-start(bf16[4,128,128]{2,1,0:T(8,128)(2,1)S(1)} %get-tuple-element.58.unread), channel_id=1, source_target_pairs={{0,96},{4,100},{8,104},{12,108},{16,112},{20,116},{24,120},{28,124... | collective-permute-start | bytes 393224 | tf_op jit(solution)/shard_map/ppermute | solution.py:653
  45.0 6.4 %collective-permute-start.14 = (bf16[4,128,128]{2,1,0:T(8,128)(2,1)S(1)}, bf16[4,128,128]{2,1,0:T(8,128)(2,1)S(1)}, u32[]{:S(2)}, u32[]{:S(2)}) collective-permute-start(bf16[4,128,128]{2,1,0:T(8,128)(2,1)S(1)} %get-tuple-element.58.unread), channel_id=1, source_target_pairs={{0,64},{4,68},{8,72},{12,76},{16,80},{20,84},{24,88},{28,92},{32,9... | collective-permute-start | bytes 393224 | tf_op jit(solution)/shard_map/ppermute | solution.py:653
  51.6 3.4 %collective-permute-start.15 = (bf16[4,128,128]{2,1,0:T(8,128)(2,1)S(1)}, bf16[4,128,128]{2,1,0:T(8,128)(2,1)S(1)}, u32[]{:S(2)}, u32[]{:S(2)}) collective-permute-start(bf16[4,128,128]{2,1,0:T(8,128)(2,1)S(1)} %get-tuple-element.61), channel_id=1, source_target_pairs={{0,4},{4,0},{8,12},{12,8},{16,20},{20,16},{24,28},{28,24},{32,36},... | collective-permute-start | bytes 393224 | tf_op jit(solution)/shard_map/ppermute | solution.py:632
  57.0 11.9 %collective-permute-start.19 = (bf16[256,768]{1,0:T(8,128)(2,1)S(1)}, bf16[256,768]{1,0:T(8,128)(2,1)S(1)}, u32[]{:S(2)}, u32[]{:S(2)}) collective-permute-start(bf16[256,768]{1,0:T(8,128)(2,1)S(1)} %shard_map.143), channel_id=1, source_target_pairs={{0,2},{1,3},{2,0},{3,1},{4,6},{5,7},{6,4},{7,5},{8,10},{9,11},{10,... | collective-permute-start | bytes 1179656 | tf_op jit(solution)/shard_map/ppermute | solution.py:623
  57.5 1.6 %collective-permute-start.18 = (bf16[4,128,128]{2,1,0:T(8,128)(2,1)S(1)}, bf16[4,128,128]{2,1,0:T(8,128)(2,1)S(1)}, u32[]{:S(2)}, u32[]{:S(2)}) collective-permute-start(bf16[4,128,128]{2,1,0:T(8,128)(2,1)S(1)} %get-tuple-element.67), channel_id=1, source_target_pairs={{0,4},{4,0},{8,12},{12,8},{16,20},{20,16},{24,28},{28,24},{32,36},... | collective-permute-start | bytes 393224 | tf_op jit(solution)/shard_map/ppermute | solution.py:632
  59.2 6.0 %collective-permute-start.22 = (bf16[4,128,128]{2,1,0:T(8,128)(2,1)S(1)}, bf16[4,128,128]{2,1,0:T(8,128)(2,1)S(1)}, u32[]{:S(2)}, u32[]{:S(2)}) collective-permute-start(bf16[4,128,128]{2,1,0:T(8,128)(2,1)S(1)} %shard_map.141.refs_0_), channel_id=1, source_target_pairs={{0,8},{4,12},{8,16},{12,20},{16,24},{20,28},{24,0},{28,4},{32,40},... | collective-permute-start | bytes 393224 | tf_op jit(solution)/shard_map/ppermute | solution.py:653
  60.0 6.2 %collective-permute-start.23 = (bf16[4,128,128]{2,1,0:T(8,128)(2,1)S(1)}, bf16[4,128,128]{2,1,0:T(8,128)(2,1)S(1)}, u32[]{:S(2)}, u32[]{:S(2)}) collective-permute-start(bf16[4,128,128]{2,1,0:T(8,128)(2,1)S(1)} %shard_map.141.refs_0_), channel_id=1, source_target_pairs={{0,24},{4,28},{8,0},{12,4},{16,8},{20,12},{24,16},{28,20},{32,56},... | collective-permute-start | bytes 393224 | tf_op jit(solution)/shard_map/ppermute | solution.py:653
  61.9 5.6 %collective-permute-start.24 = (bf16[4,128,128]{2,1,0:T(8,128)(2,1)S(1)}, bf16[4,128,128]{2,1,0:T(8,128)(2,1)S(1)}, u32[]{:S(2)}, u32[]{:S(2)}) collective-permute-start(bf16[4,128,128]{2,1,0:T(8,128)(2,1)S(1)} %shard_map.141.refs_0_), channel_id=1, source_target_pairs={{0,16},{4,20},{8,24},{12,28},{16,0},{20,4},{24,8},{28,12},{32,48},... | collective-permute-start | bytes 393224 | tf_op jit(solution)/shard_map/ppermute | solution.py:653
  63.4 17.7 %collective-permute-start.20 = (bf16[256,768]{1,0:T(8,128)(2,1)S(1)}, bf16[256,768]{1,0:T(8,128)(2,1)S(1)}, u32[]{:S(2)}, u32[]{:S(2)}) collective-permute-start(bf16[256,768]{1,0:T(8,128)(2,1)S(1)} %get-tuple-element.69), channel_id=1, source_target_pairs={{0,1},{1,2},{2,3},{3,0},{4,5},{5,6},{6,7},{7,4},{8,9},{9,10},{10,1... | collective-permute-start | bytes 1179656 | tf_op jit(solution)/shard_map/ppermute | solution.py:623
  65.2 15.9 %collective-permute-start.21 = (bf16[256,768]{1,0:T(8,128)(2,1)S(1)}, bf16[256,768]{1,0:T(8,128)(2,1)S(1)}, u32[]{:S(2)}, u32[]{:S(2)}) collective-permute-start(bf16[256,768]{1,0:T(8,128)(2,1)S(1)} %get-tuple-element.70), channel_id=1, source_target_pairs={{0,3},{1,0},{2,1},{3,2},{4,7},{5,4},{6,5},{7,6},{8,11},{9,8},{10,9... | collective-permute-start | bytes 1179656 | tf_op jit(solution)/shard_map/ppermute | solution.py:623
  69.0 7.7 %collective-permute-start.25 = (bf16[4,128,128]{2,1,0:T(8,128)(2,1)S(1)}, bf16[4,128,128]{2,1,0:T(8,128)(2,1)S(1)}, u32[]{:S(2)}, u32[]{:S(2)}) collective-permute-start(bf16[4,128,128]{2,1,0:T(8,128)(2,1)S(1)} %get-tuple-element.75.unread), channel_id=1, source_target_pairs={{0,32},{4,36},{8,40},{12,44},{16,48},{20,52},{24,56},{28,60},{32,6... | collective-permute-start | bytes 393224 | tf_op jit(solution)/shard_map/ppermute | solution.py:653
  69.6 7.2 %collective-permute-start.26 = (bf16[4,128,128]{2,1,0:T(8,128)(2,1)S(1)}, bf16[4,128,128]{2,1,0:T(8,128)(2,1)S(1)}, u32[]{:S(2)}, u32[]{:S(2)}) collective-permute-start(bf16[4,128,128]{2,1,0:T(8,128)(2,1)S(1)} %get-tuple-element.75.unread), channel_id=1, source_target_pairs={{0,96},{4,100},{8,104},{12,108},{16,112},{20,116},{24,120},{28,124... | collective-permute-start | bytes 393224 | tf_op jit(solution)/shard_map/ppermute | solution.py:653
  71.8 6.3 %collective-permute-start.27 = (bf16[4,128,128]{2,1,0:T(8,128)(2,1)S(1)}, bf16[4,128,128]{2,1,0:T(8,128)(2,1)S(1)}, u32[]{:S(2)}, u32[]{:S(2)}) collective-permute-start(bf16[4,128,128]{2,1,0:T(8,128)(2,1)S(1)} %get-tuple-element.75.unread), channel_id=1, source_target_pairs={{0,64},{4,68},{8,72},{12,76},{16,80},{20,84},{24,88},{28,92},{32,9... | collective-permute-start | bytes 393224 | tf_op jit(solution)/shard_map/ppermute | solution.py:653
  78.3 3.8 %collective-permute-start.28 = (bf16[4,128,128]{2,1,0:T(8,128)(2,1)S(1)}, bf16[4,128,128]{2,1,0:T(8,128)(2,1)S(1)}, u32[]{:S(2)}, u32[]{:S(2)}) collective-permute-start(bf16[4,128,128]{2,1,0:T(8,128)(2,1)S(1)} %get-tuple-element.80), channel_id=1, source_target_pairs={{0,4},{4,0},{8,12},{12,8},{16,20},{20,16},{24,28},{28,24},{32,36},... | collective-permute-start | bytes 393224 | tf_op jit(solution)/shard_map/ppermute | solution.py:632
  82.9 4.7 %collective-permute-start.29 = (bf16[256,64]{1,0:T(8,128)(2,1)S(1)}, bf16[256,64]{1,0:T(8,128)(2,1)S(1)}, u32[]{:S(2)}, u32[]{:S(2)}) collective-permute-start(bf16[256,64]{1,0:T(8,128)(2,1)S(1)} %get-tuple-element.85.back0), channel_id=1, source_target_pairs={{0,2},{1,3},{2,0},{3,1},{4,6},{5,7},{6,4},{7,5},{8,10},{9,11},{10,... | collective-permute-start | bytes 98312 | tf_op jit(solution)/shard_map/ppermute | solution.py:623
  84.0 7.8 %collective-permute-start.30 = (bf16[256,64]{1,0:T(8,128)(2,1)S(1)}, bf16[256,64]{1,0:T(8,128)(2,1)S(1)}, u32[]{:S(2)}, u32[]{:S(2)}) collective-permute-start(bf16[256,64]{1,0:T(8,128)(2,1)S(1)} %get-tuple-element.85.back0), channel_id=1, source_target_pairs={{0,1},{1,2},{2,3},{3,0},{4,5},{5,6},{6,7},{7,4},{8,9},{9,10},{10,1... | collective-permute-start | bytes 98312 | tf_op jit(solution)/shard_map/ppermute | solution.py:623
  84.0 7.8 %collective-permute-start.31 = (bf16[256,64]{1,0:T(8,128)(2,1)S(1)}, bf16[256,64]{1,0:T(8,128)(2,1)S(1)}, u32[]{:S(2)}, u32[]{:S(2)}) collective-permute-start(bf16[256,64]{1,0:T(8,128)(2,1)S(1)} %get-tuple-element.85.back0), channel_id=1, source_target_pairs={{0,3},{1,0},{2,1},{3,2},{4,7},{5,4},{6,5},{7,6},{8,11},{9,8},{10,9... | collective-permute-start | bytes 98312 | tf_op jit(solution)/shard_map/ppermute | solution.py:623
  89.6 16.8 %collective-permute-start.36 = (bf16[256,768]{1,0:T(8,128)(2,1)S(1)}, bf16[256,768]{1,0:T(8,128)(2,1)S(1)}, u32[]{:S(2)}, u32[]{:S(2)}) collective-permute-start(bf16[256,768]{1,0:T(8,128)(2,1)S(1)} %shard_map.150.unread), channel_id=1, source_target_pairs={{0,2},{1,3},{2,0},{3,1},{4,6},{5,7},{6,4},{7,5},{8,10},{9,11},{10,... | collective-permute-start | bytes 1179656 | tf_op jit(solution)/shard_map/ppermute | solution.py:623
  92.3 3.4 %collective-permute-start.32 = (bf16[28,16,128]{2,1,0:T(8,128)(2,1)S(1)}, bf16[28,16,128]{2,1,0:T(8,128)(2,1)S(1)}, u32[]{:S(2)}, u32[]{:S(2)}) collective-permute-start(bf16[28,16,128]{2,1,0:T(8,128)(2,1)S(1)} %get-tuple-element.89), channel_id=1, source_target_pairs={{0,4},{4,0},{8,12},{12,8},{16,20},{20,16},{24,28},{28,24},{32,36},... | collective-permute-start | bytes 344072 | tf_op jit(solution)/shard_map/ppermute | solution.py:632
  95.7 5.7 %collective-permute-start.33 = (bf16[28,16,128]{2,1,0:T(8,128)(2,1)S(1)}, bf16[28,16,128]{2,1,0:T(8,128)(2,1)S(1)}, u32[]{:S(2)}, u32[]{:S(2)}) collective-permute-start(bf16[28,16,128]{2,1,0:T(8,128)(2,1)S(1)} %shard_map.154), channel_id=1, source_target_pairs={{0,8},{4,12},{8,16},{12,20},{16,24},{20,28},{24,0},{28,4},{32,40},... | collective-permute-start | bytes 344072 | tf_op jit(solution)/shard_map/ppermute | solution.py:653
  96.6 22.1 %collective-permute-start.37 = (bf16[256,768]{1,0:T(8,128)(2,1)S(1)}, bf16[256,768]{1,0:T(8,128)(2,1)S(1)}, u32[]{:S(2)}, u32[]{:S(2)}) collective-permute-start(bf16[256,768]{1,0:T(8,128)(2,1)S(1)} %shard_map.151.unread), channel_id=1, source_target_pairs={{0,1},{1,2},{2,3},{3,0},{4,5},{5,6},{6,7},{7,4},{8,9},{9,10},{10,1... | collective-permute-start | bytes 1179656 | tf_op jit(solution)/shard_map/ppermute | solution.py:623
  96.6 22.1 %collective-permute-start.38 = (bf16[256,768]{1,0:T(8,128)(2,1)S(1)}, bf16[256,768]{1,0:T(8,128)(2,1)S(1)}, u32[]{:S(2)}, u32[]{:S(2)}) collective-permute-start(bf16[256,768]{1,0:T(8,128)(2,1)S(1)} %shard_map.152.refs_0_), channel_id=1, source_target_pairs={{0,3},{1,0},{2,1},{3,2},{4,7},{5,4},{6,5},{7,6},{8,11},{9,8},{10,9... | collective-permute-start | bytes 1179656 | tf_op jit(solution)/shard_map/ppermute | solution.py:623
  99.3 3.9 %collective-permute-start.34 = (bf16[28,16,128]{2,1,0:T(8,128)(2,1)S(1)}, bf16[28,16,128]{2,1,0:T(8,128)(2,1)S(1)}, u32[]{:S(2)}, u32[]{:S(2)}) collective-permute-start(bf16[28,16,128]{2,1,0:T(8,128)(2,1)S(1)} %shard_map.154), channel_id=1, source_target_pairs={{0,24},{4,28},{8,0},{12,4},{16,8},{20,12},{24,16},{28,20},{32,56},... | collective-permute-start | bytes 344072 | tf_op jit(solution)/shard_map/ppermute | solution.py:653
  101.3 5.1 %collective-permute-start.35 = (bf16[28,16,128]{2,1,0:T(8,128)(2,1)S(1)}, bf16[28,16,128]{2,1,0:T(8,128)(2,1)S(1)}, u32[]{:S(2)}, u32[]{:S(2)}) collective-permute-start(bf16[28,16,128]{2,1,0:T(8,128)(2,1)S(1)} %shard_map.154), channel_id=1, source_target_pairs={{0,16},{4,20},{8,24},{12,28},{16,0},{20,4},{24,8},{28,12},{32,48},... | collective-permute-start | bytes 344072 | tf_op jit(solution)/shard_map/ppermute | solution.py:653
  106.6 5.2 %collective-permute-start.39 = (bf16[28,16,128]{2,1,0:T(8,128)(2,1)S(1)}, bf16[28,16,128]{2,1,0:T(8,128)(2,1)S(1)}, u32[]{:S(2)}, u32[]{:S(2)}) collective-permute-start(bf16[28,16,128]{2,1,0:T(8,128)(2,1)S(1)} %shard_map.155.unread.mine_ref), channel_id=1, source_target_pairs={{0,32},{4,36},{8,40},{12,44},{16,48},{20,52},{24,56},{28,60},{32,6... | collective-permute-start | bytes 344072 | tf_op jit(solution)/shard_map/ppermute | solution.py:653
  106.6 5.6 %collective-permute-start.40 = (bf16[28,16,128]{2,1,0:T(8,128)(2,1)S(1)}, bf16[28,16,128]{2,1,0:T(8,128)(2,1)S(1)}, u32[]{:S(2)}, u32[]{:S(2)}) collective-permute-start(bf16[28,16,128]{2,1,0:T(8,128)(2,1)S(1)} %shard_map.155.unread.mine_ref), channel_id=1, source_target_pairs={{0,96},{4,100},{8,104},{12,108},{16,112},{20,116},{24,120},{28,124... | collective-permute-start | bytes 344072 | tf_op jit(solution)/shard_map/ppermute | solution.py:653
  109.3 5.9 %collective-permute-start.41 = (bf16[28,16,128]{2,1,0:T(8,128)(2,1)S(1)}, bf16[28,16,128]{2,1,0:T(8,128)(2,1)S(1)}, u32[]{:S(2)}, u32[]{:S(2)}) collective-permute-start(bf16[28,16,128]{2,1,0:T(8,128)(2,1)S(1)} %shard_map.155.unread.mine_ref), channel_id=1, source_target_pairs={{0,64},{4,68},{8,72},{12,76},{16,80},{20,84},{24,88},{28,92},{32,9... | collective-permute-start | bytes 344072 | tf_op jit(solution)/shard_map/ppermute | solution.py:653
  110.8 8.0 %copy-start.8 = (bf16[3,768,16]{1,2,0:T(8,128)(2,1)S(1)}, bf16[3,768,16]{1,2,0:T(8,128)(2,1)}, u32[]{:S(2)}) copy-start(bf16[3,768,16]{1,2,0:T(8,128)(2,1)} %param.11) | copy-start | bytes 221188
  115.3 4.5 %collective-permute-start.42 = (bf16[28,16,128]{2,1,0:T(8,128)(2,1)S(1)}, bf16[28,16,128]{2,1,0:T(8,128)(2,1)S(1)}, u32[]{:S(2)}, u32[]{:S(2)}) collective-permute-start(bf16[28,16,128]{2,1,0:T(8,128)(2,1)S(1)} %shard_map.159.own_ref), channel_id=1, source_target_pairs={{0,4},{4,0},{8,12},{12,8},{16,20},{20,16},{24,28},{28,24},{32,36},... | collective-permute-start | bytes 344072 | tf_op jit(solution)/shard_map/ppermute | solution.py:632
  (11 other events, 43.8 us)

commit v3 on v2

--- a/solution.py
+++ b/solution.py
@@ -781,16 +781,16 @@
     )
 
     pair, got = scan_pair(mine, given)
-    scores, raw = inside_forward(qkv, pair)
     arrived = from_axis(pair, "x")
     cot_top, cot_bottom = halves(cot_one, cot_three, arrived[0])
     cot_two = shift(cot_top, 1), shift(cot_bottom, 3)
-    middle = scan_row(mine, got, arrived, False, [raw, cot_top])
+    middle = scan_row(mine, got, arrived, False, [cot_top])
+    scores, raw = inside_forward(qkv, middle[2])
     near_grad, back_near = gradient_near(
         [cot_own, cot_one, cot_three], output_weight, middle[2]
     )
     grad, back_mid = gradient_far(cot_two, near_grad, back_near, down_out_t, output_weight)
-    held = scan_rest(middle, from_axis(middle[2], "z"), False, [near_grad])
+    held = scan_rest(middle, from_axis(middle[2], "z"), False, [near_grad, raw])
 
     attended, d_raw, mine, given = forward_heads(qkv, raw, held, grad)
     pair, got = scan_pair(mine, given)

time: 121 us -> 120 us (level)
  no operation moved by 1% of the time
where the time goes in v3:
time: 120 us
  starting transfers between devices  60.2 us (50%)
  waiting for transfers between devices  28.7 us (24%)
  Pallas kernels  27.9 us (23%)
  local copies, waits for them, and re-layouts  2.32 us (2%)
    ppermute x19, starting transfers between devices, shift(): return lax.ppermute(array, 'head', [(i, (i + by) % n) for i in range(n)])  24.2 us
    ppermute x18, starting transfers between devices, along(): return lax.ppermute(array, 'ctx', pairs)  21.8 us
    ppermute x18, waiting for transfers between devices, along(): return lax.ppermute(array, 'ctx', pairs)  18 us
    ppermute x6, starting transfers between devices, swap_cores(): return lax.ppermute(array, 'ctx', [(i, i ^ 1) for i in range(n)])  14.2 us
    ppermute x19, waiting for transfers between devices, shift(): return lax.ppermute(array, 'head', [(i, (i + by) % n) for i in range(n)])  6.79 us
    pallas_call x4, Pallas kernels, input_call(): call(kernel, [IN_VMEM] * 3 + [UNREAD] * len(more), out, 4 * rows * cols *...  4.05 us
    ppermute x6, waiting for transfers between devices, swap_cores(): return lax.ppermute(array, 'ctx', [(i, i ^ 1) for i in range(n)])  3.93 us
    pallas_call x2, Pallas kernels, project_next(): call(functools.partial(project_next_kernel, by), [IN_VMEM] * 4, struct((3...  3.18 us
  transfers between devices with their start and end apart: 43, of which 20 were waited for; matrix products, arithmetic and copies ran while one was open for 0% of the time, Pallas kernels for 20%

profile of v3, /device:TPU:1, one launch (start us, length us, event | category | flops | bytes accessed | tf_op | source)
XLA Modules:
  0.0 120.2 jit_solution(14236351752417855562)
XLA Ops:
  0.7 1.1 copy-done.1
  1.8 1.1 copy-done.7
  3.2 2.2 %collective-permute-start = (bf16[128,1024]{1,0:T(8,128)(2,1)S(1)}, bf16[128,1024]{1,0:T(8,128)(2,1)S(1)}, u32[]{:S(2)}, u32[]{:S(2)}) collective-permute-start(bf16[128,1024]{1,0:T(8,128)(2,1)S(1)} %get-tuple-element.50.own_ref), channel_id=1, source_target_pairs={{0,1},{1,2},{2,3},{3,0},{4,5},{5,6},{6,7},{7,4},{8,9},{9,10},{10,1... | collective-permute-start | bytes 786440 | tf_op jit(solution)/shard_map/ppermute | solution.py:623
  5.4 1.5 %collective-permute-start.2 = (bf16[128,1024]{1,0:T(8,128)(2,1)S(1)}, bf16[128,1024]{1,0:T(8,128)(2,1)S(1)}, u32[]{:S(2)}, u32[]{:S(2)}) collective-permute-start(bf16[128,1024]{1,0:T(8,128)(2,1)S(1)} %get-tuple-element.51), channel_id=1, source_target_pairs={{0,3},{1,0},{2,1},{3,2},{4,7},{5,4},{6,5},{7,6},{8,11},{9,8},{10,9... | collective-permute-start | bytes 786440 | tf_op jit(solution)/shard_map/ppermute | solution.py:623
  7.0 2.7 %collective-permute-start.4 = (bf16[128,1024]{1,0:T(8,128)(2,1)S(1)}, bf16[128,1024]{1,0:T(8,128)(2,1)S(1)}, u32[]{:S(2)}, u32[]{:S(2)}) collective-permute-start(bf16[128,1024]{1,0:T(8,128)(2,1)S(1)} %get-tuple-element.50.own_ref), channel_id=1, source_target_pairs={{0,3},{1,0},{2,1},{3,2},{4,7},{5,4},{6,5},{7,6},{8,11},{9,8},{10,9... | collective-permute-start | bytes 786440 | tf_op jit(solution)/shard_map/ppermute | solution.py:623
  9.7 1.4 %shard_map.128.sum_ref = f32[3,256,1024]{2,1,0:T(8,128)S(1)} custom-call(bf16[256,768]{1,0:T(8,128)(2,1)S(1)} %copy-done.1, bf16[3,3072,1024]{2,1,0:T(8,128)(2,1)S(1)} %bitcast.7), custom_call_target="tpu_custom_call" | custom-call | flops 1207959552 | bytes 4718592 | tf_op jit(solution)/shard_map/pallas_call | solution.py:99
  11.1 1.7 %collective-permute-done.top_ref.one_ref = bf16[128,1024]{1,0:T(8,128)(2,1)S(1)} collective-permute-done((bf16[128,1024]{1,0:T(8,128)(2,1)S(1)}, bf16[128,1024]{1,0:T(8,128)(2,1)S(1)}, u32[]{:S(2)}, u32[]{:S(2)}) %collective-permute-start) | collective-permute-done | bytes 262176 | tf_op jit(solution)/shard_map/ppermute | solution.py:623
  12.8 2.7 %collective-permute-start.3 = (bf16[128,1024]{1,0:T(8,128)(2,1)S(1)}, bf16[128,1024]{1,0:T(8,128)(2,1)S(1)}, u32[]{:S(2)}, u32[]{:S(2)}) collective-permute-start(bf16[128,1024]{1,0:T(8,128)(2,1)S(1)} %collective-permute-done.2.bottom_ref), channel_id=1, source_target_pairs={{0,3},{1,0},{2,1},{3,2},{4,7},{5,4},{6,5},{7,6},{8,11},{9,8},{10,9... | collective-permute-start | bytes 786440 | tf_op jit(solution)/shard_map/ppermute | solution.py:623
  15.4 2.9 %collective-permute-done.5.bottom_ref = bf16[128,1024]{1,0:T(8,128)(2,1)S(1)} collective-permute-done((bf16[128,1024]{1,0:T(8,128)(2,1)S(1)}, bf16[128,1024]{1,0:T(8,128)(2,1)S(1)}, u32[]{:S(2)}, u32[]{:S(2)}) %collective-permute-start.5) | collective-permute-done | bytes 262176 | tf_op jit(solution)/shard_map/ppermute | solution.py:623
  18.4 1.6 %shard_map.129.sum_ref = f32[3,256,1024]{2,1,0:T(8,128)S(1)} custom-call(bf16[128,1024]{1,0:T(8,128)(2,1)S(1)} %collective-permute-done.top_ref.one_ref, bf16[128,1024]{1,0:T(8,128)(2,1)S(1)} %collective-permute-done.5.bottom_ref, f32[3,256,1024]{2,1,0:T(8,128)S(1)} %shard_map.128.sum_ref, ...), custom_call_target="tpu_custom_call", output_to_operand_aliasing={{}: (2, {})} | custom-call | flops 1207959552 | bytes 4718592 | tf_op jit(solution)/shard_map/pallas_call | solution.py:123
  20.0 1.6 %shard_map.130.sum_ref.unread = f32[3,256,1024]{2,1,0:T(8,128)S(1)} custom-call(bf16[128,1024]{1,0:T(8,128)(2,1)S(1)} %collective-permute-done.4.top_ref.three_ref, bf16[128,1024]{1,0:T(8,128)(2,1)S(1)} %collective-permute-done.2.bottom_ref, f32[3,256,1024]{2,1,0:T(8,128)S(1)} %shard_map.129.sum_ref, ...), custom_call_target="tpu_custom_call", output_to_operand_aliasing={{}: (2, {})} | custom-call | flops 1207959552 | bytes 4718592 | tf_op jit(solution)/shard_map/pallas_call | solution.py:123
  22.0 2.7 %collective-permute-start.11 = (bf16[256,896]{1,0:T(8,128)(2,1)S(1)}, bf16[256,896]{1,0:T(8,128)(2,1)S(1)}, u32[]{:S(2)}, u32[]{:S(2)}) collective-permute-start(bf16[256,896]{1,0:T(8,128)(2,1)S(1)} %shard_map.133.cot0), channel_id=1, source_target_pairs={{0,3},{1,0},{2,1},{3,2},{4,7},{5,4},{6,5},{7,6},{8,11},{9,8},{10,9... | collective-permute-start | bytes 1376264 | tf_op jit(solution)/shard_map/ppermute | solution.py:623
  24.7 2.1 %shard_map.131 = (bf16[3,256,1024]{2,1,0:T(8,128)(2,1)S(1)}, f32[4,128,128]{2,1,0:T(8,128)S(1)}, bf16[4,128,128]{2,1,0:T(8,128)(2,1)S(1)}, bf16[256,48]{1,0:T(8,128)(2,1)S(1)}) custom-call(bf16[128,1024]{1,0:T(8,128)(2,1)S(1)} %collective-permute-done.1.top_ref, bf16[128,1024]{1,0:T(8,128)(2,1)S(1)} %collective-permute-done.3.bottom_ref, ...), custom_call_target="tpu_custom_call" | custom-call | flops 1207959552 | bytes 4718592 | tf_op jit(solution)/shard_map/pallas_call | solution.py:189
  26.8 3.0 %collective-permute-start.6 = (bf16[4,128,128]{2,1,0:T(8,128)(2,1)S(1)}, bf16[4,128,128]{2,1,0:T(8,128)(2,1)S(1)}, u32[]{:S(2)}, u32[]{:S(2)}) collective-permute-start(bf16[4,128,128]{2,1,0:T(8,128)(2,1)S(1)} %get-tuple-element.54), channel_id=1, source_target_pairs={{0,4},{4,0},{8,12},{12,8},{16,20},{20,16},{24,28},{28,24},{32,36},... | collective-permute-start | bytes 393224 | tf_op jit(solution)/shard_map/ppermute | solution.py:632
  30.8 1.4 %collective-permute-start.7 = (bf16[4,128,128]{2,1,0:T(8,128)(2,1)S(1)}, bf16[4,128,128]{2,1,0:T(8,128)(2,1)S(1)}, u32[]{:S(2)}, u32[]{:S(2)}) collective-permute-start(bf16[4,128,128]{2,1,0:T(8,128)(2,1)S(1)} %shard_map.132), channel_id=1, source_target_pairs={{0,8},{4,12},{8,16},{12,20},{16,24},{20,28},{24,0},{28,4},{32,40},... | collective-permute-start | bytes 393224 | tf_op jit(solution)/shard_map/ppermute | solution.py:653
  32.2 1.4 %collective-permute-start.8 = (bf16[4,128,128]{2,1,0:T(8,128)(2,1)S(1)}, bf16[4,128,128]{2,1,0:T(8,128)(2,1)S(1)}, u32[]{:S(2)}, u32[]{:S(2)}) collective-permute-start(bf16[4,128,128]{2,1,0:T(8,128)(2,1)S(1)} %shard_map.132), channel_id=1, source_target_pairs={{0,24},{4,28},{8,0},{12,4},{16,8},{20,12},{24,16},{28,20},{32,56},... | collective-permute-start | bytes 393224 | tf_op jit(solution)/shard_map/ppermute | solution.py:653
  33.6 1.6 %collective-permute-start.9 = (bf16[4,128,128]{2,1,0:T(8,128)(2,1)S(1)}, bf16[4,128,128]{2,1,0:T(8,128)(2,1)S(1)}, u32[]{:S(2)}, u32[]{:S(2)}) collective-permute-start(bf16[4,128,128]{2,1,0:T(8,128)(2,1)S(1)} %shard_map.132), channel_id=1, source_target_pairs={{0,16},{4,20},{8,24},{12,28},{16,0},{20,4},{24,8},{28,12},{32,48},... | collective-permute-start | bytes 393224 | tf_op jit(solution)/shard_map/ppermute | solution.py:653
  35.2 1.6 %collective-permute-done.7.unread.one_ref = bf16[4,128,128]{2,1,0:T(8,128)(2,1)S(1)} collective-permute-done((bf16[4,128,128]{2,1,0:T(8,128)(2,1)S(1)}, bf16[4,128,128]{2,1,0:T(8,128)(2,1)S(1)}, u32[]{:S(2)}, u32[]{:S(2)}) %collective-permute-start.7) | collective-permute-done | bytes 131104 | tf_op jit(solution)/shard_map/ppermute | solution.py:653
  36.9 2.7 %collective-permute-start.17 = (bf16[128,896]{1,0:T(8,128)(2,1)S(1)}, bf16[128,896]{1,0:T(8,128)(2,1)S(1)}, u32[]{:S(2)}, u32[]{:S(2)}) collective-permute-start(bf16[128,896]{1,0:T(8,128)(2,1)S(1)} %get-tuple-element.62), channel_id=1, source_target_pairs={{0,3},{1,0},{2,1},{3,2},{4,7},{5,4},{6,5},{7,6},{8,11},{9,8},{10,9... | collective-permute-start | bytes 688136 | tf_op jit(solution)/shard_map/ppermute | solution.py:623
  39.6 1.1 collective-permute-done.9.two_ref
  40.9 1.7 %collective-permute-start.12 = (bf16[4,128,128]{2,1,0:T(8,128)(2,1)S(1)}, bf16[4,128,128]{2,1,0:T(8,128)(2,1)S(1)}, u32[]{:S(2)}, u32[]{:S(2)}) collective-permute-start(bf16[4,128,128]{2,1,0:T(8,128)(2,1)S(1)} %get-tuple-element.56.unread), channel_id=1, source_target_pairs={{0,32},{4,36},{8,40},{12,44},{16,48},{20,52},{24,56},{28,60},{32,6... | collective-permute-start | bytes 393224 | tf_op jit(solution)/shard_map/ppermute | solution.py:653
  42.6 2.2 %collective-permute-start.13 = (bf16[4,128,128]{2,1,0:T(8,128)(2,1)S(1)}, bf16[4,128,128]{2,1,0:T(8,128)(2,1)S(1)}, u32[]{:S(2)}, u32[]{:S(2)}) collective-permute-start(bf16[4,128,128]{2,1,0:T(8,128)(2,1)S(1)} %get-tuple-element.56.unread), channel_id=1, source_target_pairs={{0,96},{4,100},{8,104},{12,108},{16,112},{20,116},{24,120},{28,124... | collective-permute-start | bytes 393224 | tf_op jit(solution)/shard_map/ppermute | solution.py:653
  44.8 1.2 %collective-permute-start.14 = (bf16[4,128,128]{2,1,0:T(8,128)(2,1)S(1)}, bf16[4,128,128]{2,1,0:T(8,128)(2,1)S(1)}, u32[]{:S(2)}, u32[]{:S(2)}) collective-permute-start(bf16[4,128,128]{2,1,0:T(8,128)(2,1)S(1)} %get-tuple-element.56.unread), channel_id=1, source_target_pairs={{0,64},{4,68},{8,72},{12,76},{16,80},{20,84},{24,88},{28,92},{32,9... | collective-permute-start | bytes 393224 | tf_op jit(solution)/shard_map/ppermute | solution.py:653
  47.0 1.4 %shard_map.137 = (f32[256,1024]{1,0:T(8,128)S(1)}, f32[256,16]{1,0:T(8,128)S(1)}) custom-call(bf16[256,896]{1,0:T(8,128)(2,1)S(1)} %shard_map.133.cot0, bf16[256,896]{1,0:T(8,128)(2,1)S(1)} %collective-permute-done.10.one_ref.cot1, bf16[256,896]{1,0:T(8,128)(2,1)S(1)} %collective-permute-done.11.three_ref.cot3, ...), custom_call_target="tpu_custom_call" | custom-call | flops 1207959552 | bytes 6291456 | tf_op jit(solution)/shard_map/pallas_call | solution.py:218
  48.4 3.4 %collective-permute-done.14.two_ref = bf16[4,128,128]{2,1,0:T(8,128)(2,1)S(1)} collective-permute-done((bf16[4,128,128]{2,1,0:T(8,128)(2,1)S(1)}, bf16[4,128,128]{2,1,0:T(8,128)(2,1)S(1)}, u32[]{:S(2)}, u32[]{:S(2)}) %collective-permute-start.14) | collective-permute-done | bytes 131104 | tf_op jit(solution)/shard_map/ppermute | solution.py:653
  52.0 1.7 %collective-permute-start.15 = (bf16[4,128,128]{2,1,0:T(8,128)(2,1)S(1)}, bf16[4,128,128]{2,1,0:T(8,128)(2,1)S(1)}, u32[]{:S(2)}, u32[]{:S(2)}) collective-permute-start(bf16[4,128,128]{2,1,0:T(8,128)(2,1)S(1)} %get-tuple-element.61), channel_id=1, source_target_pairs={{0,4},{4,0},{8,12},{12,8},{16,20},{20,16},{24,28},{28,24},{32,36},... | collective-permute-start | bytes 393224 | tf_op jit(solution)/shard_map/ppermute | solution.py:632
  54.6 1.3 %shard_map.140 = (bf16[256,1024]{1,0:T(8,128)(2,1)S(1)}, bf16[256,1024]{1,0:T(8,128)(2,1)S(1)}, f32[4,128,128]{2,1,0:T(8,128)S(1)}, bf16[4,128,128]{2,1,0:T(8,128)(2,1)S(1)}) custom-call(bf16[3,256,1024]{2,1,0:T(8,128)(2,1)S(1)} %get-tuple-element.52.qkv_ref, f32[256,1024]{1,0:T(8,128)S(1)} %get-tuple-element.57.refs_1_.raw_ref, ...), custom_call_target="tpu_custom_call" | custom-call | flops 268435456 | bytes 3670016 | tf_op jit(solution)/shard_map/pallas_call | solution.py:330
  59.8 1.9 %collective-permute-start.23 = (bf16[4,128,128]{2,1,0:T(8,128)(2,1)S(1)}, bf16[4,128,128]{2,1,0:T(8,128)(2,1)S(1)}, u32[]{:S(2)}, u32[]{:S(2)}) collective-permute-start(bf16[4,128,128]{2,1,0:T(8,128)(2,1)S(1)} %shard_map.141.refs_0_), channel_id=1, source_target_pairs={{0,24},{4,28},{8,0},{12,4},{16,8},{20,12},{24,16},{28,20},{32,56},... | collective-permute-start | bytes 393224 | tf_op jit(solution)/shard_map/ppermute | solution.py:653
  61.7 1.4 %shard_map.142 = (f32[256,768]{1,0:T(8,128)S(1)}, bf16[256,768]{1,0:T(8,128)(2,1)S(1)}, bf16[256,768]{1,0:T(8,128)(2,1)S(1)}) custom-call(bf16[256,1024]{1,0:T(8,128)(2,1)S(1)} %get-tuple-element.65.att_ref, bf16[1024,3072]{1,0:T(8,128)(2,1)S(1)} %bitcast.9, bf16[4,128,128]{2,1,0:T(8,128)(2,1)S(1)} %shard_map.141.refs_0_), custom_call_target="tpu_custom_call" | custom-call | flops 1207959552 | bytes 4718592 | tf_op jit(solution)/shard_map/pallas_call | solution.py:430
  63.5 1.4 %collective-permute-done.22.one_ref = bf16[4,128,128]{2,1,0:T(8,128)(2,1)S(1)} collective-permute-done((bf16[4,128,128]{2,1,0:T(8,128)(2,1)S(1)}, bf16[4,128,128]{2,1,0:T(8,128)(2,1)S(1)}, u32[]{:S(2)}, u32[]{:S(2)}) %collective-permute-start.22) | collective-permute-done | bytes 131104 | tf_op jit(solution)/shard_map/ppermute | solution.py:653
  65.0 1.1 collective-permute-start.21
  66.0 1.3 %collective-permute-done.24.two_ref = bf16[4,128,128]{2,1,0:T(8,128)(2,1)S(1)} collective-permute-done((bf16[4,128,128]{2,1,0:T(8,128)(2,1)S(1)}, bf16[4,128,128]{2,1,0:T(8,128)(2,1)S(1)}, u32[]{:S(2)}, u32[]{:S(2)}) %collective-permute-start.24) | collective-permute-done | bytes 131104 | tf_op jit(solution)/shard_map/ppermute | solution.py:653
  67.3 1.2 collective-permute-done.19.refs_1_.two_ref
  69.3 2.1 %collective-permute-start.26 = (bf16[4,128,128]{2,1,0:T(8,128)(2,1)S(1)}, bf16[4,128,128]{2,1,0:T(8,128)(2,1)S(1)}, u32[]{:S(2)}, u32[]{:S(2)}) collective-permute-start(bf16[4,128,128]{2,1,0:T(8,128)(2,1)S(1)} %get-tuple-element.75.unread), channel_id=1, source_target_pairs={{0,96},{4,100},{8,104},{12,108},{16,112},{20,116},{24,120},{28,124... | collective-permute-start | bytes 393224 | tf_op jit(solution)/shard_map/ppermute | solution.py:653
  71.5 3.0 %shard_map.145 = (bf16[256,1024]{1,0:T(8,128)(2,1)S(1)}, f32[256,1024]{1,0:T(8,128)S(1)}, f32[256,1024]{1,0:T(8,128)S(1)}, f32[256,16]{1,0:T(8,128)S(1)}, f32[25...) custom-call(bf16[3,256,1024]{2,1,0:T(8,128)(2,1)S(1)} %get-tuple-element.52.qkv_ref, ...), custom_call_target="tpu_custom_call" | custom-call | flops 1073741824 | bytes 4718592 | tf_op jit(solution)/shard_map/pallas_call | solution.py:375
  74.4 1.8 %shard_map.147.refs_0_.dq_ref = f32[4,256,768]{2,1,0:T(8,128)S(1)} custom-call(bf16[256,1024]{1,0:T(8,128)(2,1)S(1)} %get-tuple-element.78.dq_ref, bf16[3,3072,1024]{2,1,0:T(8,128)(2,1)S(1)} %bitcast.7, bf16[4,128,128]{2,1,0:T(8,128)(2,1)S(1)} %get-tuple-element.75.unread), custom_call_target="tpu_custom_call" | custom-call | flops 1610612736 | bytes 6291456 | tf_op jit(solution)/shard_map/pallas_call | solution.py:481
  76.3 1.4 %collective-permute-done.27.two_ref = bf16[4,128,128]{2,1,0:T(8,128)(2,1)S(1)} collective-permute-done((bf16[4,128,128]{2,1,0:T(8,128)(2,1)S(1)}, bf16[4,128,128]{2,1,0:T(8,128)(2,1)S(1)}, u32[]{:S(2)}, u32[]{:S(2)}) %collective-permute-start.27) | collective-permute-done | bytes 131104 | tf_op jit(solution)/shard_map/ppermute | solution.py:653
  77.8 2.8 %collective-permute-start.28 = (bf16[4,128,128]{2,1,0:T(8,128)(2,1)S(1)}, bf16[4,128,128]{2,1,0:T(8,128)(2,1)S(1)}, u32[]{:S(2)}, u32[]{:S(2)}) collective-permute-start(bf16[4,128,128]{2,1,0:T(8,128)(2,1)S(1)} %get-tuple-element.80), channel_id=1, source_target_pairs={{0,4},{4,0},{8,12},{12,8},{16,20},{20,16},{24,28},{28,24},{32,36},... | collective-permute-start | bytes 393224 | tf_op jit(solution)/shard_map/ppermute | solution.py:632
  83.5 2.7 %collective-permute-start.31 = (bf16[256,64]{1,0:T(8,128)(2,1)S(1)}, bf16[256,64]{1,0:T(8,128)(2,1)S(1)}, u32[]{:S(2)}, u32[]{:S(2)}) collective-permute-start(bf16[256,64]{1,0:T(8,128)(2,1)S(1)} %get-tuple-element.85.back0), channel_id=1, source_target_pairs={{0,3},{1,0},{2,1},{3,2},{4,7},{5,4},{6,5},{7,6},{8,11},{9,8},{10,9... | collective-permute-start | bytes 98312 | tf_op jit(solution)/shard_map/ppermute | solution.py:623
  89.2 1.1 collective-permute-start.36
  91.8 2.4 %collective-permute-start.32 = (bf16[28,16,128]{2,1,0:T(8,128)(2,1)S(1)}, bf16[28,16,128]{2,1,0:T(8,128)(2,1)S(1)}, u32[]{:S(2)}, u32[]{:S(2)}) collective-permute-start(bf16[28,16,128]{2,1,0:T(8,128)(2,1)S(1)} %get-tuple-element.89), channel_id=1, source_target_pairs={{0,4},{4,0},{8,12},{12,8},{16,20},{20,16},{24,28},{28,24},{32,36},... | collective-permute-start | bytes 344072 | tf_op jit(solution)/shard_map/ppermute | solution.py:632
  95.9 2.7 %collective-permute-start.38 = (bf16[256,768]{1,0:T(8,128)(2,1)S(1)}, bf16[256,768]{1,0:T(8,128)(2,1)S(1)}, u32[]{:S(2)}, u32[]{:S(2)}) collective-permute-start(bf16[256,768]{1,0:T(8,128)(2,1)S(1)} %shard_map.152.refs_0_), channel_id=1, source_target_pairs={{0,3},{1,0},{2,1},{3,2},{4,7},{5,4},{6,5},{7,6},{8,11},{9,8},{10,9... | collective-permute-start | bytes 1179656 | tf_op jit(solution)/shard_map/ppermute | solution.py:623
  98.6 2.0 %collective-permute-start.34 = (bf16[28,16,128]{2,1,0:T(8,128)(2,1)S(1)}, bf16[28,16,128]{2,1,0:T(8,128)(2,1)S(1)}, u32[]{:S(2)}, u32[]{:S(2)}) collective-permute-start(bf16[28,16,128]{2,1,0:T(8,128)(2,1)S(1)} %shard_map.154), channel_id=1, source_target_pairs={{0,24},{4,28},{8,0},{12,4},{16,8},{20,12},{24,16},{28,20},{32,56},... | collective-permute-start | bytes 344072 | tf_op jit(solution)/shard_map/ppermute | solution.py:653
  102.5 3.5 %collective-permute-done.35.refs_3_ = bf16[28,16,128]{2,1,0:T(8,128)(2,1)S(1)} collective-permute-done((bf16[28,16,128]{2,1,0:T(8,128)(2,1)S(1)}, bf16[28,16,128]{2,1,0:T(8,128)(2,1)S(1)}, u32[]{:S(2)}, u32[]{:S(2)}) %collective-permute-start.35) | collective-permute-done | bytes 114720 | tf_op jit(solution)/shard_map/ppermute | solution.py:653
  106.2 2.7 %collective-permute-start.40 = (bf16[28,16,128]{2,1,0:T(8,128)(2,1)S(1)}, bf16[28,16,128]{2,1,0:T(8,128)(2,1)S(1)}, u32[]{:S(2)}, u32[]{:S(2)}) collective-permute-start(bf16[28,16,128]{2,1,0:T(8,128)(2,1)S(1)} %shard_map.155.unread.mine_ref), channel_id=1, source_target_pairs={{0,96},{4,100},{8,104},{12,108},{16,112},{20,116},{24,120},{28,124... | collective-permute-start | bytes 344072 | tf_op jit(solution)/shard_map/ppermute | solution.py:653
  111.8 2.7 %collective-permute-done.41.refs_2_ = bf16[28,16,128]{2,1,0:T(8,128)(2,1)S(1)} collective-permute-done((bf16[28,16,128]{2,1,0:T(8,128)(2,1)S(1)}, bf16[28,16,128]{2,1,0:T(8,128)(2,1)S(1)}, u32[]{:S(2)}, u32[]{:S(2)}) %collective-permute-start.41) | collective-permute-done | bytes 114720 | tf_op jit(solution)/shard_map/ppermute | solution.py:653
  114.6 3.7 %collective-permute-start.42 = (bf16[28,16,128]{2,1,0:T(8,128)(2,1)S(1)}, bf16[28,16,128]{2,1,0:T(8,128)(2,1)S(1)}, u32[]{:S(2)}, u32[]{:S(2)}) collective-permute-start(bf16[28,16,128]{2,1,0:T(8,128)(2,1)S(1)} %shard_map.159.own_ref), channel_id=1, source_target_pairs={{0,4},{4,0},{8,12},{12,8},{16,20},{20,16},{24,28},{28,24},{32,36},... | collective-permute-start | bytes 344072 | tf_op jit(solution)/shard_map/ppermute | solution.py:632
  118.3 1.1 shard_map.158
  (106 shorter events, 24.3 us)
Async XLA Ops:
  0.6 9.0 %slice-start = ((s8[18874368]{0:T(1024)(128)(4,1)}), s8[4194304]{0:T(1024)(128)(4,1)S(1)}, s32[]{:S(2)}) async-start(s8[18874368]{0:T(1024)(128)(4,1)} %bitcast.6), calls=%async_computation | async-start | bytes 8388608
  2.9 6.7 %slice-start.4 = ((s8[18874368]{0:T(1024)(128)(4,1)}), s8[2097152]{0:T(1024)(128)(4,1)S(1)}, s32[]{:S(2)}) async-start(s8[18874368]{0:T(1024)(128)(4,1)} %bitcast.6), calls=%async_computation.4 | async-start | bytes 4194304
  3.2 9.5 %collective-permute-start = (bf16[128,1024]{1,0:T(8,128)(2,1)S(1)}, bf16[128,1024]{1,0:T(8,128)(2,1)S(1)}, u32[]{:S(2)}, u32[]{:S(2)}) collective-permute-start(bf16[128,1024]{1,0:T(8,128)(2,1)S(1)} %get-tuple-element.50.own_ref), channel_id=1, source_target_pairs={{0,1},{1,2},{2,3},{3,0},{4,5},{5,6},{6,7},{7,4},{8,9},{9,10},{10,1... | collective-permute-start | bytes 786440 | tf_op jit(solution)/shard_map/ppermute | solution.py:623
  5.4 7.3 %collective-permute-start.2 = (bf16[128,1024]{1,0:T(8,128)(2,1)S(1)}, bf16[128,1024]{1,0:T(8,128)(2,1)S(1)}, u32[]{:S(2)}, u32[]{:S(2)}) collective-permute-start(bf16[128,1024]{1,0:T(8,128)(2,1)S(1)} %get-tuple-element.51), channel_id=1, source_target_pairs={{0,3},{1,0},{2,1},{3,2},{4,7},{5,4},{6,5},{7,6},{8,11},{9,8},{10,9... | collective-permute-start | bytes 786440 | tf_op jit(solution)/shard_map/ppermute | solution.py:623
  7.0 11.4 %collective-permute-start.5 = (bf16[128,1024]{1,0:T(8,128)(2,1)S(1)}, bf16[128,1024]{1,0:T(8,128)(2,1)S(1)}, u32[]{:S(2)}, u32[]{:S(2)}) collective-permute-start(bf16[128,1024]{1,0:T(8,128)(2,1)S(1)} %get-tuple-element.51), channel_id=1, source_target_pairs={{0,1},{1,2},{2,3},{3,0},{4,5},{5,6},{6,7},{7,4},{8,9},{9,10},{10,1... | collective-permute-start | bytes 786440 | tf_op jit(solution)/shard_map/ppermute | solution.py:623
  7.0 13.0 %collective-permute-start.4 = (bf16[128,1024]{1,0:T(8,128)(2,1)S(1)}, bf16[128,1024]{1,0:T(8,128)(2,1)S(1)}, u32[]{:S(2)}, u32[]{:S(2)}) collective-permute-start(bf16[128,1024]{1,0:T(8,128)(2,1)S(1)} %get-tuple-element.50.own_ref), channel_id=1, source_target_pairs={{0,3},{1,0},{2,1},{3,2},{4,7},{5,4},{6,5},{7,6},{8,11},{9,8},{10,9... | collective-permute-start | bytes 786440 | tf_op jit(solution)/shard_map/ppermute | solution.py:623
  12.7 11.9 %collective-permute-start.1 = (bf16[128,1024]{1,0:T(8,128)(2,1)S(1)}, bf16[128,1024]{1,0:T(8,128)(2,1)S(1)}, u32[]{:S(2)}, u32[]{:S(2)}) collective-permute-start(bf16[128,1024]{1,0:T(8,128)(2,1)S(1)} %collective-permute-done.top_ref.one_ref), channel_id=1, source_target_pairs={{0,1},{1,2},{2,3},{3,0},{4,5},{5,6},{6,7},{7,4},{8,9},{9,10},{10,1... | collective-permute-start | bytes 786440 | tf_op jit(solution)/shard_map/ppermute | solution.py:623
  12.8 11.9 %collective-permute-start.3 = (bf16[128,1024]{1,0:T(8,128)(2,1)S(1)}, bf16[128,1024]{1,0:T(8,128)(2,1)S(1)}, u32[]{:S(2)}, u32[]{:S(2)}) collective-permute-start(bf16[128,1024]{1,0:T(8,128)(2,1)S(1)} %collective-permute-done.2.bottom_ref), channel_id=1, source_target_pairs={{0,3},{1,0},{2,1},{3,2},{4,7},{5,4},{6,5},{7,6},{8,11},{9,8},{10,9... | collective-permute-start | bytes 786440 | tf_op jit(solution)/shard_map/ppermute | solution.py:623
  21.6 25.3 %slice-start.5 = ((s8[6291456]{0:T(1024)(128)(4,1)}), s8[4194304]{0:T(1024)(128)(4,1)S(1)}, s32[]{:S(2)}) async-start(s8[6291456]{0:T(1024)(128)(4,1)} %bitcast.8), calls=%async_computation.5 | async-start | bytes 8388608
  21.9 25.0 %slice-start.6 = ((s8[6291456]{0:T(1024)(128)(4,1)}), s8[2097152]{0:T(1024)(128)(4,1)S(1)}, s32[]{:S(2)}) async-start(s8[6291456]{0:T(1024)(128)(4,1)} %bitcast.8), calls=%async_computation.6 | async-start | bytes 4194304
  21.9 13.3 %collective-permute-start.10 = (bf16[256,896]{1,0:T(8,128)(2,1)S(1)}, bf16[256,896]{1,0:T(8,128)(2,1)S(1)}, u32[]{:S(2)}, u32[]{:S(2)}) collective-permute-start(bf16[256,896]{1,0:T(8,128)(2,1)S(1)} %shard_map.133.cot0), channel_id=1, source_target_pairs={{0,1},{1,2},{2,3},{3,0},{4,5},{5,6},{6,7},{7,4},{8,9},{9,10},{10,1... | collective-permute-start | bytes 1376264 | tf_op jit(solution)/shard_map/ppermute | solution.py:623
  22.0 13.2 %collective-permute-start.11 = (bf16[256,896]{1,0:T(8,128)(2,1)S(1)}, bf16[256,896]{1,0:T(8,128)(2,1)S(1)}, u32[]{:S(2)}, u32[]{:S(2)}) collective-permute-start(bf16[256,896]{1,0:T(8,128)(2,1)S(1)} %shard_map.133.cot0), channel_id=1, source_target_pairs={{0,3},{1,0},{2,1},{3,2},{4,7},{5,4},{6,5},{7,6},{8,11},{9,8},{10,9... | collective-permute-start | bytes 1376264 | tf_op jit(solution)/shard_map/ppermute | solution.py:623
  26.8 4.0 %collective-permute-start.6 = (bf16[4,128,128]{2,1,0:T(8,128)(2,1)S(1)}, bf16[4,128,128]{2,1,0:T(8,128)(2,1)S(1)}, u32[]{:S(2)}, u32[]{:S(2)}) collective-permute-start(bf16[4,128,128]{2,1,0:T(8,128)(2,1)S(1)} %get-tuple-element.54), channel_id=1, source_target_pairs={{0,4},{4,0},{8,12},{12,8},{16,20},{20,16},{24,28},{28,24},{32,36},... | collective-permute-start | bytes 393224 | tf_op jit(solution)/shard_map/ppermute | solution.py:632
  30.8 6.0 %collective-permute-start.7 = (bf16[4,128,128]{2,1,0:T(8,128)(2,1)S(1)}, bf16[4,128,128]{2,1,0:T(8,128)(2,1)S(1)}, u32[]{:S(2)}, u32[]{:S(2)}) collective-permute-start(bf16[4,128,128]{2,1,0:T(8,128)(2,1)S(1)} %shard_map.132), channel_id=1, source_target_pairs={{0,8},{4,12},{8,16},{12,20},{16,24},{20,28},{24,0},{28,4},{32,40},... | collective-permute-start | bytes 393224 | tf_op jit(solution)/shard_map/ppermute | solution.py:653
  32.2 7.4 %collective-permute-start.8 = (bf16[4,128,128]{2,1,0:T(8,128)(2,1)S(1)}, bf16[4,128,128]{2,1,0:T(8,128)(2,1)S(1)}, u32[]{:S(2)}, u32[]{:S(2)}) collective-permute-start(bf16[4,128,128]{2,1,0:T(8,128)(2,1)S(1)} %shard_map.132), channel_id=1, source_target_pairs={{0,24},{4,28},{8,0},{12,4},{16,8},{20,12},{24,16},{28,20},{32,56},... | collective-permute-start | bytes 393224 | tf_op jit(solution)/shard_map/ppermute | solution.py:653
  33.6 7.1 %collective-permute-start.9 = (bf16[4,128,128]{2,1,0:T(8,128)(2,1)S(1)}, bf16[4,128,128]{2,1,0:T(8,128)(2,1)S(1)}, u32[]{:S(2)}, u32[]{:S(2)}) collective-permute-start(bf16[4,128,128]{2,1,0:T(8,128)(2,1)S(1)} %shard_map.132), channel_id=1, source_target_pairs={{0,16},{4,20},{8,24},{12,28},{16,0},{20,4},{24,8},{28,12},{32,48},... | collective-permute-start | bytes 393224 | tf_op jit(solution)/shard_map/ppermute | solution.py:653
  36.9 16.8 %collective-permute-start.16 = (bf16[128,896]{1,0:T(8,128)(2,1)S(1)}, bf16[128,896]{1,0:T(8,128)(2,1)S(1)}, u32[]{:S(2)}, u32[]{:S(2)}) collective-permute-start(bf16[128,896]{1,0:T(8,128)(2,1)S(1)} %get-tuple-element.55.refs_0_), channel_id=1, source_target_pairs={{0,1},{1,2},{2,3},{3,0},{4,5},{5,6},{6,7},{7,4},{8,9},{9,10},{10,1... | collective-permute-start | bytes 688136 | tf_op jit(solution)/shard_map/ppermute | solution.py:623
  36.9 16.7 %collective-permute-start.17 = (bf16[128,896]{1,0:T(8,128)(2,1)S(1)}, bf16[128,896]{1,0:T(8,128)(2,1)S(1)}, u32[]{:S(2)}, u32[]{:S(2)}) collective-permute-start(bf16[128,896]{1,0:T(8,128)(2,1)S(1)} %get-tuple-element.62), channel_id=1, source_target_pairs={{0,3},{1,0},{2,1},{3,2},{4,7},{5,4},{6,5},{7,6},{8,11},{9,8},{10,9... | collective-permute-start | bytes 688136 | tf_op jit(solution)/shard_map/ppermute | solution.py:623
  40.9 7.5 %collective-permute-start.12 = (bf16[4,128,128]{2,1,0:T(8,128)(2,1)S(1)}, bf16[4,128,128]{2,1,0:T(8,128)(2,1)S(1)}, u32[]{:S(2)}, u32[]{:S(2)}) collective-permute-start(bf16[4,128,128]{2,1,0:T(8,128)(2,1)S(1)} %get-tuple-element.56.unread), channel_id=1, source_target_pairs={{0,32},{4,36},{8,40},{12,44},{16,48},{20,52},{24,56},{28,60},{32,6... | collective-permute-start | bytes 393224 | tf_op jit(solution)/shard_map/ppermute | solution.py:653
  42.6 5.9 %collective-permute-start.13 = (bf16[4,128,128]{2,1,0:T(8,128)(2,1)S(1)}, bf16[4,128,128]{2,1,0:T(8,128)(2,1)S(1)}, u32[]{:S(2)}, u32[]{:S(2)}) collective-permute-start(bf16[4,128,128]{2,1,0:T(8,128)(2,1)S(1)} %get-tuple-element.56.unread), channel_id=1, source_target_pairs={{0,96},{4,100},{8,104},{12,108},{16,112},{20,116},{24,120},{28,124... | collective-permute-start | bytes 393224 | tf_op jit(solution)/shard_map/ppermute | solution.py:653
  44.8 7.0 %collective-permute-start.14 = (bf16[4,128,128]{2,1,0:T(8,128)(2,1)S(1)}, bf16[4,128,128]{2,1,0:T(8,128)(2,1)S(1)}, u32[]{:S(2)}, u32[]{:S(2)}) collective-permute-start(bf16[4,128,128]{2,1,0:T(8,128)(2,1)S(1)} %get-tuple-element.56.unread), channel_id=1, source_target_pairs={{0,64},{4,68},{8,72},{12,76},{16,80},{20,84},{24,88},{28,92},{32,9... | collective-permute-start | bytes 393224 | tf_op jit(solution)/shard_map/ppermute | solution.py:653
  52.0 2.6 %collective-permute-start.15 = (bf16[4,128,128]{2,1,0:T(8,128)(2,1)S(1)}, bf16[4,128,128]{2,1,0:T(8,128)(2,1)S(1)}, u32[]{:S(2)}, u32[]{:S(2)}) collective-permute-start(bf16[4,128,128]{2,1,0:T(8,128)(2,1)S(1)} %get-tuple-element.61), channel_id=1, source_target_pairs={{0,4},{4,0},{8,12},{12,8},{16,20},{20,16},{24,28},{28,24},{32,36},... | collective-permute-start | bytes 393224 | tf_op jit(solution)/shard_map/ppermute | solution.py:632
  56.6 11.9 %collective-permute-start.19 = (bf16[256,768]{1,0:T(8,128)(2,1)S(1)}, bf16[256,768]{1,0:T(8,128)(2,1)S(1)}, u32[]{:S(2)}, u32[]{:S(2)}) collective-permute-start(bf16[256,768]{1,0:T(8,128)(2,1)S(1)} %shard_map.143), channel_id=1, source_target_pairs={{0,2},{1,3},{2,0},{3,1},{4,6},{5,7},{6,4},{7,5},{8,10},{9,11},{10,... | collective-permute-start | bytes 1179656 | tf_op jit(solution)/shard_map/ppermute | solution.py:623
  57.3 1.6 %collective-permute-start.18 = (bf16[4,128,128]{2,1,0:T(8,128)(2,1)S(1)}, bf16[4,128,128]{2,1,0:T(8,128)(2,1)S(1)}, u32[]{:S(2)}, u32[]{:S(2)}) collective-permute-start(bf16[4,128,128]{2,1,0:T(8,128)(2,1)S(1)} %get-tuple-element.67), channel_id=1, source_target_pairs={{0,4},{4,0},{8,12},{12,8},{16,20},{20,16},{24,28},{28,24},{32,36},... | collective-permute-start | bytes 393224 | tf_op jit(solution)/shard_map/ppermute | solution.py:632
  59.0 6.0 %collective-permute-start.22 = (bf16[4,128,128]{2,1,0:T(8,128)(2,1)S(1)}, bf16[4,128,128]{2,1,0:T(8,128)(2,1)S(1)}, u32[]{:S(2)}, u32[]{:S(2)}) collective-permute-start(bf16[4,128,128]{2,1,0:T(8,128)(2,1)S(1)} %shard_map.141.refs_0_), channel_id=1, source_target_pairs={{0,8},{4,12},{8,16},{12,20},{16,24},{20,28},{24,0},{28,4},{32,40},... | collective-permute-start | bytes 393224 | tf_op jit(solution)/shard_map/ppermute | solution.py:653
  59.8 6.2 %collective-permute-start.23 = (bf16[4,128,128]{2,1,0:T(8,128)(2,1)S(1)}, bf16[4,128,128]{2,1,0:T(8,128)(2,1)S(1)}, u32[]{:S(2)}, u32[]{:S(2)}) collective-permute-start(bf16[4,128,128]{2,1,0:T(8,128)(2,1)S(1)} %shard_map.141.refs_0_), channel_id=1, source_target_pairs={{0,24},{4,28},{8,0},{12,4},{16,8},{20,12},{24,16},{28,20},{32,56},... | collective-permute-start | bytes 393224 | tf_op jit(solution)/shard_map/ppermute | solution.py:653
  61.7 5.6 %collective-permute-start.24 = (bf16[4,128,128]{2,1,0:T(8,128)(2,1)S(1)}, bf16[4,128,128]{2,1,0:T(8,128)(2,1)S(1)}, u32[]{:S(2)}, u32[]{:S(2)}) collective-permute-start(bf16[4,128,128]{2,1,0:T(8,128)(2,1)S(1)} %shard_map.141.refs_0_), channel_id=1, source_target_pairs={{0,16},{4,20},{8,24},{12,28},{16,0},{20,4},{24,8},{28,12},{32,48},... | collective-permute-start | bytes 393224 | tf_op jit(solution)/shard_map/ppermute | solution.py:653
  63.2 17.5 %collective-permute-start.20 = (bf16[256,768]{1,0:T(8,128)(2,1)S(1)}, bf16[256,768]{1,0:T(8,128)(2,1)S(1)}, u32[]{:S(2)}, u32[]{:S(2)}) collective-permute-start(bf16[256,768]{1,0:T(8,128)(2,1)S(1)} %get-tuple-element.69), channel_id=1, source_target_pairs={{0,1},{1,2},{2,3},{3,0},{4,5},{5,6},{6,7},{7,4},{8,9},{9,10},{10,1... | collective-permute-start | bytes 1179656 | tf_op jit(solution)/shard_map/ppermute | solution.py:623
  65.0 15.7 %collective-permute-start.21 = (bf16[256,768]{1,0:T(8,128)(2,1)S(1)}, bf16[256,768]{1,0:T(8,128)(2,1)S(1)}, u32[]{:S(2)}, u32[]{:S(2)}) collective-permute-start(bf16[256,768]{1,0:T(8,128)(2,1)S(1)} %get-tuple-element.70), channel_id=1, source_target_pairs={{0,3},{1,0},{2,1},{3,2},{4,7},{5,4},{6,5},{7,6},{8,11},{9,8},{10,9... | collective-permute-start | bytes 1179656 | tf_op jit(solution)/shard_map/ppermute | solution.py:623
  68.6 7.6 %collective-permute-start.25 = (bf16[4,128,128]{2,1,0:T(8,128)(2,1)S(1)}, bf16[4,128,128]{2,1,0:T(8,128)(2,1)S(1)}, u32[]{:S(2)}, u32[]{:S(2)}) collective-permute-start(bf16[4,128,128]{2,1,0:T(8,128)(2,1)S(1)} %get-tuple-element.75.unread), channel_id=1, source_target_pairs={{0,32},{4,36},{8,40},{12,44},{16,48},{20,52},{24,56},{28,60},{32,6... | collective-permute-start | bytes 393224 | tf_op jit(solution)/shard_map/ppermute | solution.py:653
  69.3 7.0 %collective-permute-start.26 = (bf16[4,128,128]{2,1,0:T(8,128)(2,1)S(1)}, bf16[4,128,128]{2,1,0:T(8,128)(2,1)S(1)}, u32[]{:S(2)}, u32[]{:S(2)}) collective-permute-start(bf16[4,128,128]{2,1,0:T(8,128)(2,1)S(1)} %get-tuple-element.75.unread), channel_id=1, source_target_pairs={{0,96},{4,100},{8,104},{12,108},{16,112},{20,116},{24,120},{28,124... | collective-permute-start | bytes 393224 | tf_op jit(solution)/shard_map/ppermute | solution.py:653
  71.4 6.3 %collective-permute-start.27 = (bf16[4,128,128]{2,1,0:T(8,128)(2,1)S(1)}, bf16[4,128,128]{2,1,0:T(8,128)(2,1)S(1)}, u32[]{:S(2)}, u32[]{:S(2)}) collective-permute-start(bf16[4,128,128]{2,1,0:T(8,128)(2,1)S(1)} %get-tuple-element.75.unread), channel_id=1, source_target_pairs={{0,64},{4,68},{8,72},{12,76},{16,80},{20,84},{24,88},{28,92},{32,9... | collective-permute-start | bytes 393224 | tf_op jit(solution)/shard_map/ppermute | solution.py:653
  77.8 3.8 %collective-permute-start.28 = (bf16[4,128,128]{2,1,0:T(8,128)(2,1)S(1)}, bf16[4,128,128]{2,1,0:T(8,128)(2,1)S(1)}, u32[]{:S(2)}, u32[]{:S(2)}) collective-permute-start(bf16[4,128,128]{2,1,0:T(8,128)(2,1)S(1)} %get-tuple-element.80), channel_id=1, source_target_pairs={{0,4},{4,0},{8,12},{12,8},{16,20},{20,16},{24,28},{28,24},{32,36},... | collective-permute-start | bytes 393224 | tf_op jit(solution)/shard_map/ppermute | solution.py:632
  82.5 4.7 %collective-permute-start.29 = (bf16[256,64]{1,0:T(8,128)(2,1)S(1)}, bf16[256,64]{1,0:T(8,128)(2,1)S(1)}, u32[]{:S(2)}, u32[]{:S(2)}) collective-permute-start(bf16[256,64]{1,0:T(8,128)(2,1)S(1)} %get-tuple-element.85.back0), channel_id=1, source_target_pairs={{0,2},{1,3},{2,0},{3,1},{4,6},{5,7},{6,4},{7,5},{8,10},{9,11},{10,... | collective-permute-start | bytes 98312 | tf_op jit(solution)/shard_map/ppermute | solution.py:623
  83.5 7.8 %collective-permute-start.30 = (bf16[256,64]{1,0:T(8,128)(2,1)S(1)}, bf16[256,64]{1,0:T(8,128)(2,1)S(1)}, u32[]{:S(2)}, u32[]{:S(2)}) collective-permute-start(bf16[256,64]{1,0:T(8,128)(2,1)S(1)} %get-tuple-element.85.back0), channel_id=1, source_target_pairs={{0,1},{1,2},{2,3},{3,0},{4,5},{5,6},{6,7},{7,4},{8,9},{9,10},{10,1... | collective-permute-start | bytes 98312 | tf_op jit(solution)/shard_map/ppermute | solution.py:623
  83.5 7.8 %collective-permute-start.31 = (bf16[256,64]{1,0:T(8,128)(2,1)S(1)}, bf16[256,64]{1,0:T(8,128)(2,1)S(1)}, u32[]{:S(2)}, u32[]{:S(2)}) collective-permute-start(bf16[256,64]{1,0:T(8,128)(2,1)S(1)} %get-tuple-element.85.back0), channel_id=1, source_target_pairs={{0,3},{1,0},{2,1},{3,2},{4,7},{5,4},{6,5},{7,6},{8,11},{9,8},{10,9... | collective-permute-start | bytes 98312 | tf_op jit(solution)/shard_map/ppermute | solution.py:623
  89.2 16.8 %collective-permute-start.36 = (bf16[256,768]{1,0:T(8,128)(2,1)S(1)}, bf16[256,768]{1,0:T(8,128)(2,1)S(1)}, u32[]{:S(2)}, u32[]{:S(2)}) collective-permute-start(bf16[256,768]{1,0:T(8,128)(2,1)S(1)} %shard_map.150.unread), channel_id=1, source_target_pairs={{0,2},{1,3},{2,0},{3,1},{4,6},{5,7},{6,4},{7,5},{8,10},{9,11},{10,... | collective-permute-start | bytes 1179656 | tf_op jit(solution)/shard_map/ppermute | solution.py:623
  91.8 3.4 %collective-permute-start.32 = (bf16[28,16,128]{2,1,0:T(8,128)(2,1)S(1)}, bf16[28,16,128]{2,1,0:T(8,128)(2,1)S(1)}, u32[]{:S(2)}, u32[]{:S(2)}) collective-permute-start(bf16[28,16,128]{2,1,0:T(8,128)(2,1)S(1)} %get-tuple-element.89), channel_id=1, source_target_pairs={{0,4},{4,0},{8,12},{12,8},{16,20},{20,16},{24,28},{28,24},{32,36},... | collective-permute-start | bytes 344072 | tf_op jit(solution)/shard_map/ppermute | solution.py:632
  95.2 5.7 %collective-permute-start.33 = (bf16[28,16,128]{2,1,0:T(8,128)(2,1)S(1)}, bf16[28,16,128]{2,1,0:T(8,128)(2,1)S(1)}, u32[]{:S(2)}, u32[]{:S(2)}) collective-permute-start(bf16[28,16,128]{2,1,0:T(8,128)(2,1)S(1)} %shard_map.154), channel_id=1, source_target_pairs={{0,8},{4,12},{8,16},{12,20},{16,24},{20,28},{24,0},{28,4},{32,40},... | collective-permute-start | bytes 344072 | tf_op jit(solution)/shard_map/ppermute | solution.py:653
  95.9 22.3 %collective-permute-start.37 = (bf16[256,768]{1,0:T(8,128)(2,1)S(1)}, bf16[256,768]{1,0:T(8,128)(2,1)S(1)}, u32[]{:S(2)}, u32[]{:S(2)}) collective-permute-start(bf16[256,768]{1,0:T(8,128)(2,1)S(1)} %shard_map.151.unread), channel_id=1, source_target_pairs={{0,1},{1,2},{2,3},{3,0},{4,5},{5,6},{6,7},{7,4},{8,9},{9,10},{10,1... | collective-permute-start | bytes 1179656 | tf_op jit(solution)/shard_map/ppermute | solution.py:623
  95.9 22.3 %collective-permute-start.38 = (bf16[256,768]{1,0:T(8,128)(2,1)S(1)}, bf16[256,768]{1,0:T(8,128)(2,1)S(1)}, u32[]{:S(2)}, u32[]{:S(2)}) collective-permute-start(bf16[256,768]{1,0:T(8,128)(2,1)S(1)} %shard_map.152.refs_0_), channel_id=1, source_target_pairs={{0,3},{1,0},{2,1},{3,2},{4,7},{5,4},{6,5},{7,6},{8,11},{9,8},{10,9... | collective-permute-start | bytes 1179656 | tf_op jit(solution)/shard_map/ppermute | solution.py:623
  98.6 3.9 %collective-permute-start.34 = (bf16[28,16,128]{2,1,0:T(8,128)(2,1)S(1)}, bf16[28,16,128]{2,1,0:T(8,128)(2,1)S(1)}, u32[]{:S(2)}, u32[]{:S(2)}) collective-permute-start(bf16[28,16,128]{2,1,0:T(8,128)(2,1)S(1)} %shard_map.154), channel_id=1, source_target_pairs={{0,24},{4,28},{8,0},{12,4},{16,8},{20,12},{24,16},{28,20},{32,56},... | collective-permute-start | bytes 344072 | tf_op jit(solution)/shard_map/ppermute | solution.py:653
  100.9 5.1 %collective-permute-start.35 = (bf16[28,16,128]{2,1,0:T(8,128)(2,1)S(1)}, bf16[28,16,128]{2,1,0:T(8,128)(2,1)S(1)}, u32[]{:S(2)}, u32[]{:S(2)}) collective-permute-start(bf16[28,16,128]{2,1,0:T(8,128)(2,1)S(1)} %shard_map.154), channel_id=1, source_target_pairs={{0,16},{4,20},{8,24},{12,28},{16,0},{20,4},{24,8},{28,12},{32,48},... | collective-permute-start | bytes 344072 | tf_op jit(solution)/shard_map/ppermute | solution.py:653
  106.1 5.2 %collective-permute-start.39 = (bf16[28,16,128]{2,1,0:T(8,128)(2,1)S(1)}, bf16[28,16,128]{2,1,0:T(8,128)(2,1)S(1)}, u32[]{:S(2)}, u32[]{:S(2)}) collective-permute-start(bf16[28,16,128]{2,1,0:T(8,128)(2,1)S(1)} %shard_map.155.unread.mine_ref), channel_id=1, source_target_pairs={{0,32},{4,36},{8,40},{12,44},{16,48},{20,52},{24,56},{28,60},{32,6... | collective-permute-start | bytes 344072 | tf_op jit(solution)/shard_map/ppermute | solution.py:653
  106.2 5.6 %collective-permute-start.40 = (bf16[28,16,128]{2,1,0:T(8,128)(2,1)S(1)}, bf16[28,16,128]{2,1,0:T(8,128)(2,1)S(1)}, u32[]{:S(2)}, u32[]{:S(2)}) collective-permute-start(bf16[28,16,128]{2,1,0:T(8,128)(2,1)S(1)} %shard_map.155.unread.mine_ref), channel_id=1, source_target_pairs={{0,96},{4,100},{8,104},{12,108},{16,112},{20,116},{24,120},{28,124... | collective-permute-start | bytes 344072 | tf_op jit(solution)/shard_map/ppermute | solution.py:653
  108.9 5.7 %collective-permute-start.41 = (bf16[28,16,128]{2,1,0:T(8,128)(2,1)S(1)}, bf16[28,16,128]{2,1,0:T(8,128)(2,1)S(1)}, u32[]{:S(2)}, u32[]{:S(2)}) collective-permute-start(bf16[28,16,128]{2,1,0:T(8,128)(2,1)S(1)} %shard_map.155.unread.mine_ref), channel_id=1, source_target_pairs={{0,64},{4,68},{8,72},{12,76},{16,80},{20,84},{24,88},{28,92},{32,9... | collective-permute-start | bytes 344072 | tf_op jit(solution)/shard_map/ppermute | solution.py:653
  110.3 8.0 %copy-start.8 = (bf16[3,768,16]{1,2,0:T(8,128)(2,1)S(1)}, bf16[3,768,16]{1,2,0:T(8,128)(2,1)}, u32[]{:S(2)}) copy-start(bf16[3,768,16]{1,2,0:T(8,128)(2,1)} %param.11) | copy-start | bytes 221188
  114.6 4.8 %collective-permute-start.42 = (bf16[28,16,128]{2,1,0:T(8,128)(2,1)S(1)}, bf16[28,16,128]{2,1,0:T(8,128)(2,1)S(1)}, u32[]{:S(2)}, u32[]{:S(2)}) collective-permute-start(bf16[28,16,128]{2,1,0:T(8,128)(2,1)S(1)} %shard_map.159.own_ref), channel_id=1, source_target_pairs={{0,4},{4,0},{8,12},{12,8},{16,20},{20,16},{24,28},{28,24},{32,36},... | collective-permute-start | bytes 344072 | tf_op jit(solution)/shard_map/ppermute | solution.py:632
  (11 other events, 42.0 us)
